TPU v7x, 768 devices: a whole 4x8x12 slice. The times are simulated.
768 devices in a mesh: dp: 768 (over y, z, x, core).
Axes of the slice: x: 4, y: 8, z: 12, core: 2. Of those that a mesh axis runs over, the one named last changes fastest.
Arguments:
- query_hidden: bfloat16 [98304, 3584], P('dp'), may hold values from -6 to 6, as said below
- doc_hidden: bfloat16 [98304, 3584], P('dp'), may hold values from -6 to 6, as said below
- gain: float32 [3584], replicated, may hold values from 0.5 to 1.5
- positives: int32 [98304], P('dp'), may hold values from 0 to 127
- neg_blocks: int32 [768, 4], P('dp'), may hold values from 0 to 767, as said below
Outputs:
- mean_loss: float32 [], replicated
- grad_gain: float32 [3584], replicated
- grad_query: bfloat16 [98304, 3584], P('dp')
- grad_doc: bfloat16 [98304, 3584], P('dp')
Inputs may be any that keep to these rules, and one draw needn't show every extreme that they name: `neg_blocks`: row b lists 4 block ids; each entry is either b itself (an unused entry) or (b + o) mod 768 with 1 <= |o| <= 2; the entries other than b are distinct, at least one per row, and some row lists all 4 of them. `query_hidden`: rows are pooled hidden states of order one. `doc_hidden`: rows are pooled hidden states of order one.
All inputs are finite; a program needn't handle non-finite values.
Results may differ from a plain program's by a relative error of at most 0.0079.
Values may be sent and summed in bfloat16 or wider, within the bound.
No kernel may reach another device: no remote copies, remote signals or barrier semaphores. Data moves between devices by JAX's collectives and lax.ppermute only.
A program may use at most 64 MiB of HBM per device.

v0:
```python
import math

import jax
import jax.numpy as jnp
from jax import lax
from jax.sharding import PartitionSpec as P

logit_scale = 4.0


def from_behind(block, axis, distance):
    devices = range(lax.axis_size(axis))
    route = [((i - distance) % len(devices), i) for i in devices]
    return lax.ppermute(block, axis, route)


def head(hidden, gain):
    values = hidden.astype(jnp.float32)
    factor = lax.rsqrt(jnp.mean(values * values, axis=-1, keepdims=True) + 1e-06)
    return values * factor * gain


def rounded(term):
    held = lax.optimization_barrier(term.astype(jnp.bfloat16))
    return held.astype(jnp.float32)


def body(query_hidden, doc_hidden, gain, positives, neg_blocks):
    count = lax.axis_size("dp")
    me_index = lax.axis_index("dp")
    rows, width = query_hidden.shape
    factor = logit_scale / math.sqrt(width)
    q_norm = head(query_hidden, gain).astype(jnp.bfloat16)
    d_norm = head(doc_hidden, gain).astype(jnp.bfloat16)
    reach = neg_blocks.shape[1] // 2
    offsets = [o for o in range(-reach, reach + 1) if o != 0]
    flags = [jnp.any(neg_blocks[0] == (me_index + o) % count) for o in offsets]
    onehot = (jnp.arange(rows, dtype=jnp.int32)[None, :] == positives[:, None]).astype(jnp.float32)
    own = factor * jnp.dot(q_norm, d_norm.T, preferred_element_type=jnp.float32)
    blank = jnp.zeros((rows, rows), jnp.float32)
    empty = jnp.zeros((rows, width), jnp.bfloat16)

    def tile_scores(left, right):
        return factor * jnp.dot(left, right.T, preferred_element_type=jnp.float32)

    def no_scores(left, right):
        return blank

    top = jnp.max(own, axis=1)
    tiles = []
    for o, flag in zip(offsets, flags):
        marker = flag.astype(jnp.bfloat16).reshape(1)
        arrived, arrived_flag = from_behind((q_norm, marker), "dp", o)
        visiting = arrived_flag[0] > 0
        scores = lax.cond(visiting, tile_scores, no_scores, arrived, d_norm)
        row_top = jnp.max(scores, axis=1)
        row_total = jnp.sum(jnp.exp(scores - row_top[:, None]), axis=1)
        back_top, back_total = from_behind((row_top, row_total), "dp", -o)
        tiles.append((o, flag, arrived, visiting, scores, back_top, back_total))
        top = jnp.maximum(top, jnp.where(flag, back_top, -jnp.inf))
    total = jnp.sum(jnp.exp(own - top[:, None]), axis=1)
    for o, flag, arrived, visiting, scores, back_top, back_total in tiles:
        total = total + jnp.where(flag, back_total * jnp.exp(back_top - top), 0.0)
    lse = top + jnp.log(total)
    weight = (jnp.exp(own - lse[:, None]) - onehot).astype(jnp.bfloat16)
    q_grad = rounded(jnp.dot(weight, d_norm, preferred_element_type=jnp.float32))
    d_grad = rounded(jnp.dot(weight.T, q_norm, preferred_element_type=jnp.float32))

    def owner_terms(scores, arrived, lse_in):
        probs = jnp.exp(scores - lse_in[:, None]).astype(jnp.bfloat16)
        doc_term = jnp.dot(probs.T, arrived, preferred_element_type=jnp.float32).astype(
            jnp.bfloat16
        )
        query_term = jnp.dot(probs, d_norm, preferred_element_type=jnp.float32).astype(jnp.bfloat16)
        return (doc_term, query_term)

    def no_owner_terms(scores, arrived, lse_in):
        return (empty, empty)

    for o, flag, arrived, visiting, scores, back_top, back_total in tiles:
        lse_in = from_behind(lse, "dp", o)
        doc_term, query_term = lax.cond(
            visiting, owner_terms, no_owner_terms, scores, arrived, lse_in
        )
        d_grad = d_grad + doc_term.astype(jnp.float32)
        returned = from_behind(query_term, "dp", -o)
        q_grad = q_grad + returned.astype(jnp.float32)
    q_grad = factor * q_grad
    d_grad = factor * d_grad
    _, pull_query = jax.vjp(head, query_hidden, gain)
    grad_query, gain_query = pull_query(q_grad)
    _, pull_doc = jax.vjp(head, doc_hidden, gain)
    grad_doc, gain_doc = pull_doc(d_grad)
    losses = lse - jnp.sum(own * onehot, axis=1)
    gain_sum, loss_sum = lax.psum((gain_query + gain_doc, jnp.sum(losses)), "dp")
    denom = rows * count
    return (loss_sum / denom, gain_sum / denom, grad_query, grad_doc)


def solution(mesh):
    placed = (P("dp", None), P("dp", None), P(), P("dp"), P("dp", None))
    return jax.shard_map(
        body,
        mesh=mesh,
        in_specs=placed,
        out_specs=(P(), P(), P("dp", None), P("dp", None)),
        check_vma=False,
    )
```

profile of v0, /device:TPU:1, one launch (start us, length us, event | category | flops | bytes accessed | tf_op | source)
XLA Modules:
  0.0 309.4 jit_solution(1185129584333861689)
XLA Ops:
  0.6 0.0 copy-start
  0.7 1.6 fusion.14
  2.2 1.4 fusion.16
  3.7 2.2 fusion.8
  5.9 3.9 %collective-permute-start.10 = (bf16[128,3584]{1,0:T(8,128)(2,1)}, bf16[128,3584]{1,0:T(8,128)(2,1)}, u32[]{:S(2)}, u32[]{:S(2)}) collective-permute-start(bf16[128,3584]{1,0:T(8,128)(2,1)} %get-tuple-element.165), channel_id=1, source_target_pairs={{766,0},{767,1},{0,2},{1,3},{2,4},{3,5},{4,6},{5,7},{6,8},{7,9},{8... | collective-permute-start | bytes 2752520 | tf_op jit(solution)/shard_map/ppermute | solution.py:14
  9.8 4.0 %collective-permute-start.7 = (bf16[128,3584]{1,0:T(8,128)(2,1)}, bf16[128,3584]{1,0:T(8,128)(2,1)}, u32[]{:S(2)}, u32[]{:S(2)}) collective-permute-start(bf16[128,3584]{1,0:T(8,128)(2,1)} %get-tuple-element.165), channel_id=1, source_target_pairs={{767,0},{0,1},{1,2},{2,3},{3,4},{4,5},{5,6},{6,7},{7,8},{8,9},{9,1... | collective-permute-start | bytes 2752520 | tf_op jit(solution)/shard_map/ppermute | solution.py:14
  13.8 8.4 %collective-permute-start.4 = (bf16[128,3584]{1,0:T(8,128)(2,1)}, bf16[128,3584]{1,0:T(8,128)(2,1)}, u32[]{:S(2)}, u32[]{:S(2)}) collective-permute-start(bf16[128,3584]{1,0:T(8,128)(2,1)} %get-tuple-element.165), channel_id=1, source_target_pairs={{1,0},{2,1},{3,2},{4,3},{5,4},{6,5},{7,6},{8,7},{9,8},{10,9},{11,1... | collective-permute-start | bytes 2752520 | tf_op jit(solution)/shard_map/ppermute | solution.py:14
  22.1 10.4 %collective-permute-start.1 = (bf16[128,3584]{1,0:T(8,128)(2,1)}, bf16[128,3584]{1,0:T(8,128)(2,1)}, u32[]{:S(2)}, u32[]{:S(2)}) collective-permute-start(bf16[128,3584]{1,0:T(8,128)(2,1)} %get-tuple-element.165), channel_id=1, source_target_pairs={{2,0},{3,1},{4,2},{5,3},{6,4},{7,5},{8,6},{9,7},{10,8},{11,9},{12,... | collective-permute-start | bytes 2752520 | tf_op jit(solution)/shard_map/ppermute | solution.py:14
  32.6 0.7 compare_reduce_fusion.3
  34.0 6.1 %collective-permute-start.9 = (bf16[1]{0:T(256)(128)(2,1)}, bf16[1]{0:T(256)(128)(2,1)}, u32[]{:S(2)}, u32[]{:S(2)}) collective-permute-start(bf16[1]{0:T(256)(128)(2,1)} %bitcast.6), channel_id=1, source_target_pairs={{766,0},{767,1},{0,2},{1,3},{2,4},{3,5},{4,6},{5,7},{6,8},{7,9},{8... | collective-permute-start | bytes 14 | tf_op jit(solution)/shard_map/ppermute | solution.py:14
  42.0 1.6 fusion.35
  43.6 13.5 %collective-permute-done.9 = bf16[1]{0:T(256)(128)(2,1)} collective-permute-done((bf16[1]{0:T(256)(128)(2,1)}, bf16[1]{0:T(256)(128)(2,1)}, u32[]{:S(2)}, u32[]{:S(2)}) %collective-permute-start.9) | collective-permute-done | bytes 34 | tf_op jit(solution)/shard_map/ppermute | solution.py:14
  57.1 2.6 collective-permute-start.6
  60.4 5.8 %collective-permute-start.3 = (bf16[1]{0:T(256)(128)(2,1)}, bf16[1]{0:T(256)(128)(2,1)}, u32[]{:S(2)}, u32[]{:S(2)}) collective-permute-start(bf16[1]{0:T(256)(128)(2,1)} %bitcast.2), channel_id=1, source_target_pairs={{1,0},{2,1},{3,2},{4,3},{5,4},{6,5},{7,6},{8,7},{9,8},{10,9},{11,1... | collective-permute-start | bytes 14 | tf_op jit(solution)/shard_map/ppermute | solution.py:14
  66.9 9.3 %collective-permute-start = (bf16[1]{0:T(256)(128)(2,1)}, bf16[1]{0:T(256)(128)(2,1)}, u32[]{:S(2)}, u32[]{:S(2)}) collective-permute-start(bf16[1]{0:T(256)(128)(2,1)} %bitcast), channel_id=1, source_target_pairs={{2,0},{3,1},{4,2},{5,3},{6,4},{7,5},{8,6},{9,7},{10,8},{11,9},{12,... | collective-permute-start | bytes 14 | tf_op jit(solution)/shard_map/ppermute | solution.py:14
  77.6 1.6 conditional.11
  77.6 1.6 fusion.34
  79.2 6.8 %collective-permute-start.11 = (f32[128]{0:T(128)S(1)}, f32[128]{0:T(128)S(1)}, u32[]{:S(2)}, u32[]{:S(2)}) collective-permute-start(f32[128]{0:T(128)S(1)} %get-tuple-element.107), channel_id=1, source_target_pairs={{2,0},{3,1},{4,2},{5,3},{6,4},{7,5},{8,6},{9,7},{10,8},{11,9},{12,... | collective-permute-start | bytes 1544 | tf_op jit(solution)/shard_map/ppermute | solution.py:14
  86.0 1.6 conditional.10
  86.0 1.6 fusion.33
  87.6 1.9 collective-permute-start.8
  89.5 1.6 conditional.9
  89.5 1.6 fusion.32
  91.1 2.1 collective-permute-start.5
  93.3 1.9 collective-permute-start.2
  95.2 8.8 %collective-permute-start.15 = (f32[128]{0:T(128)S(1)}, f32[128]{0:T(128)S(1)}, u32[]{:S(2)}, u32[]{:S(2)}) collective-permute-start(f32[128]{0:T(128)S(1)} %exponential_reduce_fusion), channel_id=1, source_target_pairs={{2,0},{3,1},{4,2},{5,3},{6,4},{7,5},{8,6},{9,7},{10,8},{11,9},{12,... | collective-permute-start | bytes 1544 | tf_op jit(solution)/shard_map/ppermute | solution.py:14
  104.2 4.4 %collective-permute-start.14 = (f32[128]{0:T(128)S(1)}, f32[128]{0:T(128)S(1)}, u32[]{:S(2)}, u32[]{:S(2)}) collective-permute-start(f32[128]{0:T(128)S(1)} %exponential_reduce_fusion.1), channel_id=1, source_target_pairs={{1,0},{2,1},{3,2},{4,3},{5,4},{6,5},{7,6},{8,7},{9,8},{10,9},{11,1... | collective-permute-start | bytes 1544 | tf_op jit(solution)/shard_map/ppermute | solution.py:14
  108.6 1.9 collective-permute-start.13
  110.5 1.9 collective-permute-start.12
  112.4 2.6 fusion.24
  115.1 5.1 %collective-permute-done.12 = f32[128]{0:T(128)S(1)} collective-permute-done((f32[128]{0:T(128)S(1)}, f32[128]{0:T(128)S(1)}, u32[]{:S(2)}, u32[]{:S(2)}) %collective-permute-start.12) | collective-permute-done | bytes 544 | tf_op jit(solution)/shard_map/ppermute | solution.py:14
  120.2 3.2 %subtract_reduce_fusion = (f32[]{:T(128)}, f32[128]{0:T(128)S(1)}) fusion(f32[128]{0:T(128)S(1)} %get-tuple-element.140, f32[128]{0:T(128)S(1)} %collective-permute-done.15, f32[128]{0:T(128)S(1)} %collective-permute-done.11, f32[128]{0:T(128)S(1)} %collective-permute-done.14, f32[128]{0:T(128)S(1)} %collective-permute-done.8, ...), kind=kLoop, calls=%fused_computation.83 | loop fusion | flops 3455 | bytes 6152 | tf_op jit(solution)/shard_map/reduce_sum | solution.py:95
  123.5 1.9 collective-permute-start.22
  125.4 1.9 collective-permute-start.20
  127.3 3.6 %collective-permute-start.18 = (f32[128]{0:T(128)S(1)}, f32[128]{0:T(128)S(1)}, u32[]{:S(2)}, u32[]{:S(2)}) collective-permute-start(f32[128]{0:T(128)S(1)} %get-tuple-element.153), channel_id=1, source_target_pairs={{1,0},{2,1},{3,2},{4,3},{5,4},{6,5},{7,6},{8,7},{9,8},{10,9},{11,1... | collective-permute-start | bytes 1544 | tf_op jit(solution)/shard_map/ppermute | solution.py:14
  130.9 9.1 %collective-permute-start.16 = (f32[128]{0:T(128)S(1)}, f32[128]{0:T(128)S(1)}, u32[]{:S(2)}, u32[]{:S(2)}) collective-permute-start(f32[128]{0:T(128)S(1)} %get-tuple-element.153), channel_id=1, source_target_pairs={{2,0},{3,1},{4,2},{5,3},{6,4},{7,5},{8,6},{9,7},{10,8},{11,9},{12,... | collective-permute-start | bytes 1544 | tf_op jit(solution)/shard_map/ppermute | solution.py:14
  139.9 3.2 %conditional.15 = (bf16[128,3584]{1,0:T(8,128)(2,1)}, f32[128,3584]{1,0:T(8,128)S(1)}) conditional(s32[]{:T(128)} %bitcast.7, () %tuple.102, (f32[128]{0:T(128)S(1)}, f32[128,128]{0,1:T(8,128)S(1)}, bf16[128,3584]{1,0:T(8,128)(2,1)S(1)}, bf16[128,3584]{1,0:T(8,128)(2,1)}) %tuple.103), branch_computations={%region_33.34_spmd, %region_34.35_spmd} | conditional | flops 236322816 | bytes 4850704 | solution.py:82
  140.0 0.1 copy.12
  140.1 1.4 convolution_convert_fusion.7
  141.4 1.7 fusion.3
  143.1 1.9 collective-permute-start.23
  145.1 3.2 %conditional.14 = (bf16[128,3584]{1,0:T(8,128)(2,1)}, f32[128,3584]{1,0:T(8,128)S(1)}) conditional(s32[]{:T(128)} %bitcast.5, () %tuple.100, (f32[128]{0:T(128)S(1)}, f32[128,128]{0,1:T(8,128)S(1)}, bf16[128,3584]{1,0:T(8,128)(2,1)S(1)}, bf16[128,3584]{1,0:T(8,128)(2,1)}) %tuple.101), branch_computations={%region_31.32_spmd, %region_32.33_spmd} | conditional | flops 236322816 | bytes 4850704 | solution.py:82
  145.1 0.1 copy.11
  145.2 1.4 convolution_convert_fusion.5
  146.6 1.7 fusion.2
  148.3 3.9 %collective-permute-start.21 = (bf16[128,3584]{1,0:T(8,128)(2,1)}, bf16[128,3584]{1,0:T(8,128)(2,1)}, u32[]{:S(2)}, u32[]{:S(2)}) collective-permute-start(bf16[128,3584]{1,0:T(8,128)(2,1)} %get-tuple-element.114), channel_id=1, source_target_pairs={{1,0},{2,1},{3,2},{4,3},{5,4},{6,5},{7,6},{8,7},{9,8},{10,9},{11,1... | collective-permute-start | bytes 2752520 | tf_op jit(solution)/shard_map/ppermute | solution.py:14
  152.2 3.2 %conditional.13 = (bf16[128,3584]{1,0:T(8,128)(2,1)}, f32[128,3584]{1,0:T(8,128)S(1)}) conditional(s32[]{:T(128)} %bitcast.3, () %tuple.98, (f32[128]{0:T(128)S(1)}, f32[128,128]{0,1:T(8,128)S(1)}, bf16[128,3584]{1,0:T(8,128)(2,1)S(1)}, bf16[128,3584]{1,0:T(8,128)(2,1)}) %tuple.99), branch_computations={%region_29.30_spmd, %region_30.31_spmd} | conditional | flops 236322816 | bytes 4850704 | solution.py:82
  152.3 0.1 copy.10
  152.3 1.4 convolution_convert_fusion.3
  153.8 1.7 fusion.1
  155.5 1.9 collective-permute-start.19
  157.4 0.3 conditional.12
  157.4 0.1 broadcast_in_dim.41
  157.5 0.2 broadcast_in_dim.42
  157.7 1.9 collective-permute-start.17
  159.7 0.4 convolution_convert_fusion.9
  160.1 1.8 convolution_convert_fusion.8
  161.9 3.3 %collective-permute-done.23 = bf16[128,3584]{1,0:T(8,128)(2,1)} collective-permute-done((bf16[128,3584]{1,0:T(8,128)(2,1)}, bf16[128,3584]{1,0:T(8,128)(2,1)}, u32[]{:S(2)}, u32[]{:S(2)}) %collective-permute-start.23) | collective-permute-done | bytes 917536 | tf_op jit(solution)/shard_map/ppermute | solution.py:14
  165.2 12.3 %collective-permute-done.21 = bf16[128,3584]{1,0:T(8,128)(2,1)} collective-permute-done((bf16[128,3584]{1,0:T(8,128)(2,1)}, bf16[128,3584]{1,0:T(8,128)(2,1)}, u32[]{:S(2)}, u32[]{:S(2)}) %collective-permute-start.21) | collective-permute-done | bytes 917536 | tf_op jit(solution)/shard_map/ppermute | solution.py:14
  177.4 15.4 %collective-permute-done.17 = bf16[128,3584]{1,0:T(8,128)(2,1)S(1)} collective-permute-done((bf16[128,3584]{1,0:T(8,128)(2,1)S(1)}, bf16[128,3584]{1,0:T(8,128)(2,1)S(1)}, u32[]{:S(2)}, u32[]{:S(2)}) %collective-permute-start.17) | collective-permute-done | bytes 917536 | tf_op jit(solution)/shard_map/ppermute | solution.py:14
  192.8 6.4 %fusion.17 = (f32[128]{0:T(128)S(1)}, f32[3584]{0:T(1024)S(1)}, f32[3584]{0:T(1024)S(1)}, f32[128]{0:T(128)S(1)}, f32[128,3584]{1,0:T(8,128)}, /*index=5*/f32[128,3584]{1,0:T(8,128)}) fusion(bf16[128,3584]{1,0:T(8,128)(2,1)S(1)} %copy-done, f32[3584]{0:T(1024)S(1)} %broadcast_multiply_fusion, f32[128]{0:T(128)S(1)} %get-tuple-element.169, ...), kind=kLoop, calls=%fused_computation.45 | loop fusion | flops 13755136 | bytes 18395136 | tf_op jit(solution)/shard_map/transpose(jvp())/reduce_sum | solution.py:20
  199.2 103.5 %all-reduce = (f32[]{:T(128)}, f32[3584]{0:T(1024)S(1)}) all-reduce(f32[]{:T(128)} %get-tuple-element.152, f32[3584]{0:T(1024)S(1)} %add.116), channel_id=1, replica_groups=mesh['dp'=768] {'dp'}, use_global_device_ids=true, to_apply=%region_26.27 | all-reduce | flops 3585 | bytes 28680 | tf_op jit(solution)/shard_map/psum | solution.py:95
  302.8 0.6 broadcast_multiply_fusion.1
  304.0 4.2 %fusion.13 = (bf16[128,3584]{1,0:T(8,128)(2,1)}, bf16[128,3584]{1,0:T(8,128)(2,1)}) fusion(bf16[128,3584]{1,0:T(8,128)(2,1)S(1)} %copy-done, f32[128,3584]{1,0:T(8,128)} %get-tuple-element.151, f32[128]{0:T(128)S(1)} %multiply_multiply_fusion, f32[3584]{0:T(1024)S(1)} %broadcast_multiply_fusion, f32[128]{0:T(128)S(1)} %get-tuple-element.169, ...), kind=kLoop, calls=%fused_computation.41 | loop fusion | flops 6422528 | bytes 7356416 | tf_op jit(solution)/shard_map/transpose(jvp())/convert_element_type | solution.py:18
  (53 shorter events, 0.4 us)
Async XLA Ops:
  0.6 3.1 copy-start.1
  0.6 3.1 copy-start
  3.7 28.9 %copy-start.10 = (s32[1,4]{1,0:T(1,128)S(1)}, s32[1,4]{1,0:T(1,128)}, u32[]{:S(2)}) copy-start(s32[1,4]{1,0:T(1,128)} %param.25) | copy-start | bytes 52
  5.9 71.7 %collective-permute-start.10 = (bf16[128,3584]{1,0:T(8,128)(2,1)}, bf16[128,3584]{1,0:T(8,128)(2,1)}, u32[]{:S(2)}, u32[]{:S(2)}) collective-permute-start(bf16[128,3584]{1,0:T(8,128)(2,1)} %get-tuple-element.165), channel_id=1, source_target_pairs={{766,0},{767,1},{0,2},{1,3},{2,4},{3,5},{4,6},{5,7},{6,8},{7,9},{8... | collective-permute-start | bytes 2752520 | tf_op jit(solution)/shard_map/ppermute | solution.py:14
  9.8 76.1 %collective-permute-start.7 = (bf16[128,3584]{1,0:T(8,128)(2,1)}, bf16[128,3584]{1,0:T(8,128)(2,1)}, u32[]{:S(2)}, u32[]{:S(2)}) collective-permute-start(bf16[128,3584]{1,0:T(8,128)(2,1)} %get-tuple-element.165), channel_id=1, source_target_pairs={{767,0},{0,1},{1,2},{2,3},{3,4},{4,5},{5,6},{6,7},{7,8},{8,9},{9,1... | collective-permute-start | bytes 2752520 | tf_op jit(solution)/shard_map/ppermute | solution.py:14
  13.8 75.7 %collective-permute-start.4 = (bf16[128,3584]{1,0:T(8,128)(2,1)}, bf16[128,3584]{1,0:T(8,128)(2,1)}, u32[]{:S(2)}, u32[]{:S(2)}) collective-permute-start(bf16[128,3584]{1,0:T(8,128)(2,1)} %get-tuple-element.165), channel_id=1, source_target_pairs={{1,0},{2,1},{3,2},{4,3},{5,4},{6,5},{7,6},{8,7},{9,8},{10,9},{11,1... | collective-permute-start | bytes 2752520 | tf_op jit(solution)/shard_map/ppermute | solution.py:14
  22.1 71.1 %collective-permute-start.1 = (bf16[128,3584]{1,0:T(8,128)(2,1)}, bf16[128,3584]{1,0:T(8,128)(2,1)}, u32[]{:S(2)}, u32[]{:S(2)}) collective-permute-start(bf16[128,3584]{1,0:T(8,128)(2,1)} %get-tuple-element.165), channel_id=1, source_target_pairs={{2,0},{3,1},{4,2},{5,3},{6,4},{7,5},{8,6},{9,7},{10,8},{11,9},{12,... | collective-permute-start | bytes 2752520 | tf_op jit(solution)/shard_map/ppermute | solution.py:14
  34.0 23.1 %collective-permute-start.9 = (bf16[1]{0:T(256)(128)(2,1)}, bf16[1]{0:T(256)(128)(2,1)}, u32[]{:S(2)}, u32[]{:S(2)}) collective-permute-start(bf16[1]{0:T(256)(128)(2,1)} %bitcast.6), channel_id=1, source_target_pairs={{766,0},{767,1},{0,2},{1,3},{2,4},{3,5},{4,6},{5,7},{6,8},{7,9},{8... | collective-permute-start | bytes 14 | tf_op jit(solution)/shard_map/ppermute | solution.py:14
  57.1 3.3 %collective-permute-start.6 = (bf16[1]{0:T(256)(128)(2,1)}, bf16[1]{0:T(256)(128)(2,1)}, u32[]{:S(2)}, u32[]{:S(2)}) collective-permute-start(bf16[1]{0:T(256)(128)(2,1)} %bitcast.4), channel_id=1, source_target_pairs={{767,0},{0,1},{1,2},{2,3},{3,4},{4,5},{5,6},{6,7},{7,8},{8,9},{9,1... | collective-permute-start | bytes 14 | tf_op jit(solution)/shard_map/ppermute | solution.py:14
  60.4 6.5 %collective-permute-start.3 = (bf16[1]{0:T(256)(128)(2,1)}, bf16[1]{0:T(256)(128)(2,1)}, u32[]{:S(2)}, u32[]{:S(2)}) collective-permute-start(bf16[1]{0:T(256)(128)(2,1)} %bitcast.2), channel_id=1, source_target_pairs={{1,0},{2,1},{3,2},{4,3},{5,4},{6,5},{7,6},{8,7},{9,8},{10,9},{11,1... | collective-permute-start | bytes 14 | tf_op jit(solution)/shard_map/ppermute | solution.py:14
  66.9 10.0 %collective-permute-start = (bf16[1]{0:T(256)(128)(2,1)}, bf16[1]{0:T(256)(128)(2,1)}, u32[]{:S(2)}, u32[]{:S(2)}) collective-permute-start(bf16[1]{0:T(256)(128)(2,1)} %bitcast), channel_id=1, source_target_pairs={{2,0},{3,1},{4,2},{5,3},{6,4},{7,5},{8,6},{9,7},{10,8},{11,9},{12,... | collective-permute-start | bytes 14 | tf_op jit(solution)/shard_map/ppermute | solution.py:14
  79.2 25.0 %collective-permute-start.11 = (f32[128]{0:T(128)S(1)}, f32[128]{0:T(128)S(1)}, u32[]{:S(2)}, u32[]{:S(2)}) collective-permute-start(f32[128]{0:T(128)S(1)} %get-tuple-element.107), channel_id=1, source_target_pairs={{2,0},{3,1},{4,2},{5,3},{6,4},{7,5},{8,6},{9,7},{10,8},{11,9},{12,... | collective-permute-start | bytes 1544 | tf_op jit(solution)/shard_map/ppermute | solution.py:14
  87.6 21.0 %collective-permute-start.8 = (f32[128]{0:T(128)S(1)}, f32[128]{0:T(128)S(1)}, u32[]{:S(2)}, u32[]{:S(2)}) collective-permute-start(f32[128]{0:T(128)S(1)} %get-tuple-element.106), channel_id=1, source_target_pairs={{1,0},{2,1},{3,2},{4,3},{5,4},{6,5},{7,6},{8,7},{9,8},{10,9},{11,1... | collective-permute-start | bytes 1544 | tf_op jit(solution)/shard_map/ppermute | solution.py:14
  89.5 25.5 %copy-start.9 = (s32[128]{0:T(128)S(1)}, s32[128]{0:T(128)}, u32[]{:S(2)}) copy-start(s32[128]{0:T(128)} %param.24) | copy-start | bytes 1540
  91.1 19.4 %collective-permute-start.5 = (f32[128]{0:T(128)S(1)}, f32[128]{0:T(128)S(1)}, u32[]{:S(2)}, u32[]{:S(2)}) collective-permute-start(f32[128]{0:T(128)S(1)} %get-tuple-element.105), channel_id=1, source_target_pairs={{767,0},{0,1},{1,2},{2,3},{3,4},{4,5},{5,6},{6,7},{7,8},{8,9},{9,1... | collective-permute-start | bytes 1544 | tf_op jit(solution)/shard_map/ppermute | solution.py:14
  93.3 19.2 %collective-permute-start.2 = (f32[128]{0:T(128)S(1)}, f32[128]{0:T(128)S(1)}, u32[]{:S(2)}, u32[]{:S(2)}) collective-permute-start(f32[128]{0:T(128)S(1)} %get-tuple-element.104), channel_id=1, source_target_pairs={{766,0},{767,1},{0,2},{1,3},{2,4},{3,5},{4,6},{5,7},{6,8},{7,9},{8... | collective-permute-start | bytes 1544 | tf_op jit(solution)/shard_map/ppermute | solution.py:14
  95.2 19.8 %collective-permute-start.15 = (f32[128]{0:T(128)S(1)}, f32[128]{0:T(128)S(1)}, u32[]{:S(2)}, u32[]{:S(2)}) collective-permute-start(f32[128]{0:T(128)S(1)} %exponential_reduce_fusion), channel_id=1, source_target_pairs={{2,0},{3,1},{4,2},{5,3},{6,4},{7,5},{8,6},{9,7},{10,8},{11,9},{12,... | collective-permute-start | bytes 1544 | tf_op jit(solution)/shard_map/ppermute | solution.py:14
  104.2 10.9 %collective-permute-start.14 = (f32[128]{0:T(128)S(1)}, f32[128]{0:T(128)S(1)}, u32[]{:S(2)}, u32[]{:S(2)}) collective-permute-start(f32[128]{0:T(128)S(1)} %exponential_reduce_fusion.1), channel_id=1, source_target_pairs={{1,0},{2,1},{3,2},{4,3},{5,4},{6,5},{7,6},{8,7},{9,8},{10,9},{11,1... | collective-permute-start | bytes 1544 | tf_op jit(solution)/shard_map/ppermute | solution.py:14
  108.6 6.5 %collective-permute-start.13 = (f32[128]{0:T(128)S(1)}, f32[128]{0:T(128)S(1)}, u32[]{:S(2)}, u32[]{:S(2)}) collective-permute-start(f32[128]{0:T(128)S(1)} %exponential_reduce_fusion.2), channel_id=1, source_target_pairs={{767,0},{0,1},{1,2},{2,3},{3,4},{4,5},{5,6},{6,7},{7,8},{8,9},{9,1... | collective-permute-start | bytes 1544 | tf_op jit(solution)/shard_map/ppermute | solution.py:14
  110.5 9.7 %collective-permute-start.12 = (f32[128]{0:T(128)S(1)}, f32[128]{0:T(128)S(1)}, u32[]{:S(2)}, u32[]{:S(2)}) collective-permute-start(f32[128]{0:T(128)S(1)} %exponential_reduce_fusion.3), channel_id=1, source_target_pairs={{766,0},{767,1},{0,2},{1,3},{2,4},{3,5},{4,6},{5,7},{6,8},{7,9},{8... | collective-permute-start | bytes 1544 | tf_op jit(solution)/shard_map/ppermute | solution.py:14
  123.5 16.5 %collective-permute-start.22 = (f32[128]{0:T(128)S(1)}, f32[128]{0:T(128)S(1)}, u32[]{:S(2)}, u32[]{:S(2)}) collective-permute-start(f32[128]{0:T(128)S(1)} %get-tuple-element.153), channel_id=1, source_target_pairs={{766,0},{767,1},{0,2},{1,3},{2,4},{3,5},{4,6},{5,7},{6,8},{7,9},{8... | collective-permute-start | bytes 1544 | tf_op jit(solution)/shard_map/ppermute | solution.py:14
  125.4 19.7 %collective-permute-start.20 = (f32[128]{0:T(128)S(1)}, f32[128]{0:T(128)S(1)}, u32[]{:S(2)}, u32[]{:S(2)}) collective-permute-start(f32[128]{0:T(128)S(1)} %get-tuple-element.153), channel_id=1, source_target_pairs={{767,0},{0,1},{1,2},{2,3},{3,4},{4,5},{5,6},{6,7},{7,8},{8,9},{9,1... | collective-permute-start | bytes 1544 | tf_op jit(solution)/shard_map/ppermute | solution.py:14
  127.3 24.9 %collective-permute-start.18 = (f32[128]{0:T(128)S(1)}, f32[128]{0:T(128)S(1)}, u32[]{:S(2)}, u32[]{:S(2)}) collective-permute-start(f32[128]{0:T(128)S(1)} %get-tuple-element.153), channel_id=1, source_target_pairs={{1,0},{2,1},{3,2},{4,3},{5,4},{6,5},{7,6},{8,7},{9,8},{10,9},{11,1... | collective-permute-start | bytes 1544 | tf_op jit(solution)/shard_map/ppermute | solution.py:14
  130.9 26.5 %collective-permute-start.16 = (f32[128]{0:T(128)S(1)}, f32[128]{0:T(128)S(1)}, u32[]{:S(2)}, u32[]{:S(2)}) collective-permute-start(f32[128]{0:T(128)S(1)} %get-tuple-element.153), channel_id=1, source_target_pairs={{2,0},{3,1},{4,2},{5,3},{6,4},{7,5},{8,6},{9,7},{10,8},{11,9},{12,... | collective-permute-start | bytes 1544 | tf_op jit(solution)/shard_map/ppermute | solution.py:14
  143.1 2.0 copy-start.2
  143.1 22.0 %collective-permute-start.23 = (bf16[128,3584]{1,0:T(8,128)(2,1)}, bf16[128,3584]{1,0:T(8,128)(2,1)}, u32[]{:S(2)}, u32[]{:S(2)}) collective-permute-start(bf16[128,3584]{1,0:T(8,128)(2,1)} %get-tuple-element.115), channel_id=1, source_target_pairs={{2,0},{3,1},{4,2},{5,3},{6,4},{7,5},{8,6},{9,7},{10,8},{11,9},{12,... | collective-permute-start | bytes 2752520 | tf_op jit(solution)/shard_map/ppermute | solution.py:14
  148.3 3.9 %copy-start.4 = (f32[128,3584]{1,0:T(8,128)}, f32[128,3584]{1,0:T(8,128)S(1)}, u32[]{:S(2)}) copy-start(f32[128,3584]{1,0:T(8,128)S(1)} %get-tuple-element.118) | copy-start | bytes 5505028
  148.3 29.2 %collective-permute-start.21 = (bf16[128,3584]{1,0:T(8,128)(2,1)}, bf16[128,3584]{1,0:T(8,128)(2,1)}, u32[]{:S(2)}, u32[]{:S(2)}) collective-permute-start(bf16[128,3584]{1,0:T(8,128)(2,1)} %get-tuple-element.114), channel_id=1, source_target_pairs={{1,0},{2,1},{3,2},{4,3},{5,4},{6,5},{7,6},{8,7},{9,8},{10,9},{11,1... | collective-permute-start | bytes 2752520 | tf_op jit(solution)/shard_map/ppermute | solution.py:14
  155.4 2.0 copy-start.6
  155.5 22.0 %collective-permute-start.19 = (bf16[128,3584]{1,0:T(8,128)(2,1)}, bf16[128,3584]{1,0:T(8,128)(2,1)}, u32[]{:S(2)}, u32[]{:S(2)}) collective-permute-start(bf16[128,3584]{1,0:T(8,128)(2,1)} %get-tuple-element.113), channel_id=1, source_target_pairs={{767,0},{0,1},{1,2},{2,3},{3,4},{4,5},{5,6},{6,7},{7,8},{8,9},{9,1... | collective-permute-start | bytes 2752520 | tf_op jit(solution)/shard_map/ppermute | solution.py:14
  157.4 2.2 copy-start.8
  157.7 2.4 copy-start.7
  157.7 35.1 %collective-permute-start.17 = (bf16[128,3584]{1,0:T(8,128)(2,1)S(1)}, bf16[128,3584]{1,0:T(8,128)(2,1)S(1)}, u32[]{:S(2)}, u32[]{:S(2)}) collective-permute-start(bf16[128,3584]{1,0:T(8,128)(2,1)S(1)} %get-tuple-element.112), channel_id=1, source_target_pairs={{766,0},{767,1},{0,2},{1,3},{2,4},{3,5},{4,6},{5,7},{6,8},{7,9},{8... | collective-permute-start | bytes 2752520 | tf_op jit(solution)/shard_map/ppermute | solution.py:14
  159.6 33.2 %copy-start.3 = (f32[128,3584]{1,0:T(8,128)S(1)}, f32[128,3584]{1,0:T(8,128)}, u32[]{:S(2)}) copy-start(f32[128,3584]{1,0:T(8,128)} %copy-done.2) | copy-start | bytes 5505028
  159.7 33.1 %copy-start.5 = (f32[128,3584]{1,0:T(8,128)S(1)}, f32[128,3584]{1,0:T(8,128)}, u32[]{:S(2)}) copy-start(f32[128,3584]{1,0:T(8,128)} %copy-done.4) | copy-start | bytes 5505028
where the time goes:
time: 311 us; the launch traced here: 309 us
  starting transfers between devices  106 us (34%)
  blocking collectives  104 us (33%)
  waiting for transfers between devices  49.5 us (16%)
  other arithmetic  23.1 us (7%)
  matrix products  17.8 us (6%)
  between operations  8.2 us (3%)
    ppermute x24, starting transfers between devices, from_behind(): return lax.ppermute(block, axis, route)  106 us
    psum x1, blocking collectives, body(): lax.psum((gain_query + gain_doc, jnp.sum(losses)), 'dp')  104 us
    ppermute x24, waiting for transfers between devices, from_behind(): return lax.ppermute(block, axis, route)  49.5 us
    reduce_sum x1, other arithmetic, head(): return values * factor * gain  6.4 us
  transfers between devices with their start and end apart: 24, of which 5 were waited for; matrix products, arithmetic and copies ran while one was open for 7% of the time, Pallas kernels for 0%

commit v1 on v0

v1 whole, which is shorter than its diff:
```python
import functools
import math

import jax
import jax.numpy as jnp
import numpy as np
from jax import lax
from jax.experimental import pallas as pl
from jax.experimental.pallas import tpu as pltpu
from jax.sharding import Mesh
from jax.sharding import PartitionSpec as P

logit_scale = 4.0
ROWS = 128
WIDTH = 3584
FACTOR = logit_scale / math.sqrt(WIDTH)
LANES = 128
GAIN_ROWS = WIDTH // LANES
SUM_ROWS = 32
CHUNK = 512
HIDDEN = -1e30
STEP = 16
f32, bf16 = jnp.float32, jnp.bfloat16
AXES = ("y", "z", "row")

in_vmem = pl.BlockSpec(memory_space=pltpu.VMEM)
anywhere = pl.BlockSpec(memory_space=pl.ANY)
in_smem = pl.BlockSpec(memory_space=pltpu.SMEM)


def held(shape, dtype):
    return pltpu.VMEM(shape, dtype)


def call(kernel, out_shape, args, scratch=(), aliases=None, scalars=(), after=()):
    arrays = [*scalars, *args, *after]
    specs = [in_smem] * len(scalars) + [in_vmem] * len(args) + [anywhere] * len(after)

    def run(*refs):
        given = len(scalars) + len(args)
        kernel(*refs[:given], *refs[given + len(after) :])

    return pl.pallas_call(
        run,
        in_specs=specs,
        out_specs=jax.tree.map(lambda _: in_vmem, out_shape),
        out_shape=out_shape,
        scratch_shapes=list(scratch),
        input_output_aliases=aliases or {},
        compiler_params=pltpu.CompilerParams(vmem_limit_bytes=14 * 2**20),
    )(*arrays)


def kept(x):
    return pltpu.with_memory_space_constraint(x, pltpu.VMEM)


def factor_of(values):
    return lax.rsqrt(jnp.mean(values * values, axis=-1, keepdims=True) + 1e-06)


def head_into(hidden_ref, gain, out_ref):
    for i in range(0, ROWS, STEP):
        values = hidden_ref[i : i + STEP, :].astype(f32)
        out_ref[i : i + STEP, :] = (values * factor_of(values) * gain).astype(bf16)


def scores_of(queries, docs):
    dims = (((1,), (1,)), ((), ()))
    return FACTOR * lax.dot_general(queries, docs, dims, preferred_element_type=f32)


def across(column):
    return jnp.broadcast_to(column, (ROWS, LANES))


def onehot_of(positives_ref):
    slots = lax.broadcasted_iota(jnp.int32, (ROWS, ROWS), 0)
    return (slots == positives_ref[...]).astype(f32).T


def gain_of(gain_ref):
    return jnp.concatenate([gain_ref[i : i + 1, :] for i in range(GAIN_ROWS)], axis=1)


def listed(neg_ref, distance):
    place, count = 0, 1
    for axis in AXES:
        place = place * lax.axis_size(axis) + lax.axis_index(axis)
        count = count * lax.axis_size(axis)
    sign = 1 - 2 * lax.rem(place, 2)
    block = lax.rem(place + sign * distance + count, count)
    found = neg_ref[0, 0] == block
    for i in range(1, neg_ref.shape[1]):
        found = jnp.logical_or(found, neg_ref[0, i] == block)
    return found


def own_kernel(q_ref, d_ref, gain_ref, pos_ref, qn_ref, dn_ref, s_ref, top_ref, total_ref, acc_ref, picked_ref):
    gain = gain_of(gain_ref)
    head_into(d_ref, gain, dn_ref)
    head_into(q_ref, gain, qn_ref)
    scores = scores_of(qn_ref[...], dn_ref[...])
    top = jnp.max(scores, axis=1, keepdims=True)
    probs = jnp.exp(scores - top)
    s_ref[...] = scores
    top_ref[...] = across(top)
    total_ref[...] = across(jnp.sum(probs, axis=1, keepdims=True))
    probs = probs.astype(bf16)
    onehot = onehot_of(pos_ref).astype(bf16)
    for c in range(0, WIDTH, CHUNK):
        docs = dn_ref[:, c : c + CHUNK]
        acc_ref[:, c : c + CHUNK] = jnp.dot(probs, docs, preferred_element_type=f32)
        picked_ref[:, c : c + CHUNK] = jnp.dot(onehot, docs, preferred_element_type=f32).astype(bf16)


def head_kernel(x_ref, gain_ref, out_ref):
    head_into(x_ref, gain_of(gain_ref), out_ref)


def fold(scores, dn_ref, top0_ref, total0_ref, acc0_ref):
    before = top0_ref[:, 0:1]
    top = jnp.maximum(before, jnp.max(scores, axis=1, keepdims=True))
    shrink = jnp.exp(before - top)
    probs = jnp.exp(scores - top)
    total = total0_ref[:, 0:1] * shrink + jnp.sum(probs, axis=1, keepdims=True)
    probs = probs.astype(bf16)

    def weighted(c):
        term = jnp.dot(probs, dn_ref[:, c : c + CHUNK], preferred_element_type=f32)
        return acc0_ref[:, c : c + CHUNK] * shrink + term

    return top, total, weighted


def step_kernel(distance, raw, neg_ref, x_ref, gain_ref, qn_ref, top0_ref, total0_ref, acc0_ref, s_ref, top_ref, total_ref, acc_ref, *scratch):
    dn_ref = x_ref
    if raw:
        dn_ref = scratch[0]
        head_into(x_ref, gain_of(gain_ref), dn_ref)
    scores = jnp.where(listed(neg_ref, distance), scores_of(qn_ref[...], dn_ref[...]), HIDDEN)
    top, total, weighted = fold(scores, dn_ref, top0_ref, total0_ref, acc0_ref)
    s_ref[...] = scores
    for c in range(0, WIDTH, CHUNK):
        acc_ref[:, c : c + CHUNK] = weighted(c)
    top_ref[...] = across(top)
    total_ref[...] = across(total)


def last_kernel(
    distance, neg_ref, dn_ref, q_ref, qn_ref, top0_ref, total0_ref, acc0_ref, picked_ref, pos_ref,
    s_own_ref, s_swap_ref, s_relay_ref, s_far_ref,
    gq_ref, part_ref, t_own_ref, t_near_ref, t_far_ref, t_back_ref, gain_sum,
):
    scores = jnp.where(listed(neg_ref, distance), scores_of(qn_ref[...], dn_ref[...]), HIDDEN)
    top, total, weighted = fold(scores, dn_ref, top0_ref, total0_ref, acc0_ref)
    lse = top + jnp.log(total)
    share = FACTOR / total
    onehot = onehot_of(pos_ref)
    loss = jnp.sum(lse - jnp.sum(s_own_ref[...] * onehot, axis=1, keepdims=True))

    for c in range(0, WIDTH, CHUNK):
        gq_ref[:, c : c + CHUNK] = weighted(c) * share - FACTOR * picked_ref[:, c : c + CHUNK].astype(f32)
    for i in range(0, ROWS, STEP):
        values = q_ref[i : i + STEP, :].astype(f32)
        added = gq_ref[i : i + STEP, :] * (values * factor_of(values))
        added = added[:8] + added[8:]
        gain_sum[...] = added if i == 0 else gain_sum[...] + added
    gain_part = 2.0 * jnp.sum(gain_sum[...], axis=0, keepdims=True)
    copies = part_ref.shape[0]
    for i in range(GAIN_ROWS):
        line = gain_part[:, i * LANES : (i + 1) * LANES]
        part_ref[:, i : i + 1, :] = jnp.broadcast_to(line[None], (copies, 1, LANES))
    part_ref[:, GAIN_ROWS:, :] = jnp.full((copies, SUM_ROWS - GAIN_ROWS, LANES), loss, f32)

    def turned(block_scores, less):
        weight = jnp.exp(block_scores - lse)
        weight = weight if less is None else weight - less
        return weight.T.astype(bf16)

    w_own = turned(s_own_ref[...], onehot)
    w_swap = turned(s_swap_ref[...], None)
    w_relay = turned(s_relay_ref[...], None)
    w_far = turned(s_far_ref[...], None)
    w_back = turned(scores, None)
    for c in range(0, WIDTH, CHUNK):
        cols = slice(c, c + CHUNK)
        queries = qn_ref[:, cols]

        def term(weight):
            return jnp.dot(weight, queries, preferred_element_type=f32)

        t_back_ref[:, cols] = term(w_back).astype(bf16)
        t_near_ref[0, :, cols] = term(w_relay).astype(bf16)
        t_near_ref[1, :, cols] = term(w_swap).astype(bf16)
        t_far_ref[:, cols] = term(w_far)
        t_own_ref[:, cols] = term(w_own)


def pull_into(values, gain, cotangent):
    factor = factor_of(values)
    scaled = gain * cotangent
    inner = jnp.sum(values * scaled, axis=-1, keepdims=True) / WIDTH
    return factor * scaled - values * (factor * factor * factor * inner)


def grad_query_kernel(q_ref, gain_ref, gq_ref, out_ref):
    gain = gain_of(gain_ref)
    for i in range(0, ROWS, STEP):
        rows = slice(i, i + STEP)
        out_ref[rows, :] = pull_into(q_ref[rows, :].astype(f32), gain, gq_ref[rows, :]).astype(bf16)


def grad_doc_kernel(d_ref, gain_ref, t_own_ref, near_ref, back_ref, far_ref, out_ref):
    gain = gain_of(gain_ref)
    for i in range(0, ROWS, STEP):
        rows = slice(i, i + STEP)
        total = t_own_ref[rows, :] + near_ref[1, rows, :].astype(f32)
        total = total + back_ref[rows, :].astype(f32) + far_ref[rows, :].astype(f32)
        out_ref[rows, :] = pull_into(d_ref[rows, :].astype(f32), gain, FACTOR * total).astype(bf16)


def add_kernel(t_far_ref, near_ref, out_ref):
    for i in range(0, ROWS, STEP):
        rows = slice(i, i + STEP)
        out_ref[rows, :] = (t_far_ref[rows, :] + near_ref[0, rows, :].astype(f32)).astype(bf16)


def sum_kernel(in_ref, out_ref):
    total = jnp.sum(in_ref[...], axis=0)
    out_ref[...] = jnp.broadcast_to(total[None], out_ref.shape)


def end_kernel(denom, in_ref, gain_ref, loss_ref):
    total = jnp.sum(in_ref[...], axis=0) / denom
    gain_ref[...] = total[:GAIN_ROWS]
    loss_ref[...] = total[GAIN_ROWS : GAIN_ROWS + 1, 0:1]


def body(query_hidden, doc_hidden, gain, positives, neg_blocks):
    count = lax.axis_size(AXES)
    gain = gain.reshape(GAIN_ROWS, LANES)
    positives = positives.reshape(1, ROWS)

    devices = range(count)
    far_source = [(i + 2 if i % 2 == 0 else i - 2) % count for i in devices]
    back_source = [(i - 2 if i % 2 == 0 else i + 2) % count for i in devices]

    def permute(x, route):
        return lax.ppermute(x, AXES, route)

    swap_route = [(i, i ^ 1) for i in devices]
    far = permute(doc_hidden, [(far_source[i], i) for i in devices])
    swap = permute(doc_hidden, swap_route)
    square, block = (ROWS, LANES), (ROWS, WIDTH)
    qn, dn, s_own, *state, picked = call(
        own_kernel,
        [held(block, bf16)] * 2 + [held(square, f32)] * 3 + [held(block, f32), held(block, bf16)],
        (query_hidden, doc_hidden, gain, positives),
    )
    qn, picked, s_own = kept(qn), kept(picked), kept(s_own)
    back = permute(dn, [(back_source[i], i) for i in devices])

    def step(distance, docs, state, raw=False):
        return call(
            functools.partial(step_kernel, distance, raw),
            [held(square, f32)] * 3 + [held(block, f32)],
            (docs, gain, qn, *map(kept, state)),
            scalars=(neg_blocks,),
            scratch=[pltpu.VMEM(block, bf16)] if raw else (),
            aliases={4: 1, 5: 2, 6: 3},
        )

    s_swap, *state = step(1, swap, state, raw=True)
    far = call(head_kernel, held(block, bf16), (far, gain), after=(s_swap,))
    relay = permute(far, swap_route)
    s_far, *state = step(2, far, state)
    s_relay, *state = step(-1, relay, state)
    sizes = [lax.axis_size(a) for a in AXES]
    gq, part, t_own, t_near, t_far, t_back = call(
        functools.partial(last_kernel, -2),
        [
            held(block, f32),
            held((sizes[0], SUM_ROWS, LANES), f32),
            held(block, f32),
            held((2, *block), bf16),
            held(block, f32),
            held(block, bf16),
        ],
        (back, query_hidden, qn, *map(kept, state), picked, positives, s_own, kept(s_swap), kept(s_relay), kept(s_far)),
        scalars=(neg_blocks,),
        scratch=[pltpu.VMEM((8, WIDTH), f32)],
        aliases={6: 0},
    )
    back_term = permute(t_back, [(i, back_source[i]) for i in devices])
    near_term = permute(t_near, swap_route)

    part = lax.all_to_all(part, AXES[0], 0, 0, tiled=True)
    part = call(sum_kernel, held((sizes[1], SUM_ROWS, LANES), f32), (part,))
    far_sum = call(add_kernel, held(block, bf16), (kept(t_far), near_term), after=(part,))
    far_term = permute(far_sum, [(i, far_source[i]) for i in devices])
    part = lax.all_to_all(part, AXES[1], 0, 0, tiled=True)
    part = call(sum_kernel, held((sizes[2], SUM_ROWS, LANES), f32), (part,))
    part = lax.all_to_all(part, AXES[2], 0, 0, tiled=True)
    grad = jax.ShapeDtypeStruct(block, bf16)
    grad_query = call(grad_query_kernel, grad, (query_hidden, gain, kept(gq)))
    grad_doc = call(grad_doc_kernel, grad, (doc_hidden, gain, kept(t_own), near_term, back_term, far_term))
    grad_gain, mean_loss = call(
        functools.partial(end_kernel, float(ROWS * count)),
        [jax.ShapeDtypeStruct((GAIN_ROWS, LANES), f32), jax.ShapeDtypeStruct((1, 1), f32)],
        (part,),
    )
    return mean_loss.reshape(()), grad_gain.reshape(WIDTH), grad_query, grad_doc


def grid_of(count):
    return (8, 12, 8) if count == 768 else (2, count // 16, 8)


def solution(mesh):
    devices = np.asarray(mesh.devices)
    inner = Mesh(devices.reshape(grid_of(devices.size)), AXES)
    placed = (P(AXES, None), P(AXES, None), P(), P(AXES), P(AXES, None))
    return jax.shard_map(
        body,
        mesh=inner,
        in_specs=placed,
        out_specs=(P(), P(), P(AXES, None), P(AXES, None)),
        check_vma=False,
    )
```

time: 311 us -> 128 us (0.41)
  blocking collectives: 104 us -> 19.2 us
  starting transfers between devices: 106 us -> 44.3 us
  Pallas kernels: 0 us -> 24.7 us
  other arithmetic: 23.1 us -> 0 us
  waiting for transfers between devices: 49.5 us -> 26.8 us
  matrix products: 17.8 us -> 0 us
  local copies, waits for them, and re-layouts: 0.56 us -> 11.3 us
  between operations: 8.2 us -> 0.82 us
    psum x1 -> x0, blocking collectives: 104 us -> none  [body(): lax.psum((gain_query + gain_doc, jnp.sum(losses)), 'dp')]
    ppermute x24 -> x7, starting transfers between devices: 106 us -> 35.9 us  [permute(): return lax.ppermute(x, AXES, route)]
    ppermute x24 -> x7, waiting for transfers between devices: 49.5 us -> 16.6 us  [permute(): return lax.ppermute(x, AXES, route)]
    pallas_call x0 -> x12, Pallas kernels: none -> 24.7 us  [call(): pl.pallas_call(run, in_specs=specs, out_specs=jax.tree.map(lambda _: in_v...]
    all_to_all x0 -> x1, blocking collectives: none -> 19.2 us  [body(): part = lax.all_to_all(part, AXES[1], 0, 0, tiled=True)]
    dot_general x12 -> x0, matrix products: 17.8 us -> none  [the longest x3 5.03 us: owner_terms(): jnp.dot(probs.T, arrived, preferred_element_type=jnp.float32)]
    reduce_sum x9 -> x0, other arithmetic: 12.9 us -> none  [the longest x1 6.4 us: head(): return values * factor * gain]
    unnamed x22 -> x28, local copies, waits for them, and re-layouts: 0.05 us -> 11.3 us
  transfers between devices with their start and end apart: 24 -> 9, of which waited for: 5 -> 4; matrix products, arithmetic and copies ran while one was open for 7% -> 0% of each run, Pallas kernels for 0% -> 12%
where the time goes in v1:
time: 128 us; the launch traced here: 127 us
  starting transfers between devices  44.3 us (35%)
  waiting for transfers between devices  26.8 us (21%)
  Pallas kernels  24.7 us (19%)
  blocking collectives  19.2 us (15%)
  local copies, waits for them, and re-layouts  11.3 us (9%)
    ppermute x7, starting transfers between devices, permute(): return lax.ppermute(x, AXES, route)  35.9 us
    pallas_call x12, Pallas kernels, call(): pl.pallas_call(run, in_specs=specs, out_specs=jax.tree.map(lambda _: in_v...  24.7 us
    all_to_all x1, blocking collectives, body(): part = lax.all_to_all(part, AXES[1], 0, 0, tiled=True)  19.2 us
    ppermute x7, waiting for transfers between devices, permute(): return lax.ppermute(x, AXES, route)  16.6 us
    unnamed x28, local copies, waits for them, and re-layouts  11.3 us
    all_to_all x1, waiting for transfers between devices, body(): part = lax.all_to_all(part, AXES[0], 0, 0, tiled=True)  6.59 us
    all_to_all x1, starting transfers between devices, body(): part = lax.all_to_all(part, AXES[2], 0, 0, tiled=True)  4.63 us
    all_to_all x1, starting transfers between devices, body(): part = lax.all_to_all(part, AXES[0], 0, 0, tiled=True)  3.81 us
  transfers between devices with their start and end apart: 9, of which 4 were waited for; matrix products, arithmetic and copies ran while one was open for 0% of the time, Pallas kernels for 12%

profile of v1, /device:TPU:1, one launch (start us, length us, event | category | flops | bytes accessed | tf_op | source)
XLA Modules:
  0.0 127.2 jit_solution(2622551122753300855)
XLA Ops:
  0.6 0.0 copy-start.10
  0.6 12.4 %collective-permute-start.2 = (bf16[128,3584]{1,0:T(8,128)(2,1)}, bf16[128,3584]{1,0:T(8,128)(2,1)S(1)}, u32[]{:S(2)}, u32[]{:S(2)}) collective-permute-start(bf16[128,3584]{1,0:T(8,128)(2,1)} %refs_0_.13), channel_id=1, source_target_pairs={{0,1},{1,0},{2,3},{3,2},{4,5},{5,4},{6,7},{7,6},{8,9},{9,8},{10,11... | collective-permute-start | bytes 2752520 | tf_op jit(solution)/shard_map/ppermute | solution.py:250
  13.1 1.9 %collective-permute-start.1 = (bf16[128,3584]{1,0:T(8,128)(2,1)}, bf16[128,3584]{1,0:T(8,128)(2,1)S(1)}, u32[]{:S(2)}, u32[]{:S(2)}) collective-permute-start(bf16[128,3584]{1,0:T(8,128)(2,1)} %refs_0_.13), channel_id=1, source_target_pairs={{2,0},{767,1},{4,2},{1,3},{6,4},{3,5},{8,6},{5,7},{10,8},{7,9},{12... | collective-permute-start | bytes 2752520 | tf_op jit(solution)/shard_map/ppermute | solution.py:250
  15.0 0.0 copy-start
  15.0 1.2 copy-done
  16.2 0.0 copy-start.2
  16.2 1.2 copy-done.2
  17.4 0.0 copy-start.8
  17.4 0.7 copy-done.8
  18.1 0.0 copy-start.11
  18.1 0.7 copy-done.11
  18.7 2.0 %shard_map.84 = (bf16[128,3584]{1,0:T(8,128)(2,1)S(1)}, bf16[128,3584]{1,0:T(8,128)(2,1)S(1)}, f32[128,128]{1,0:T(8,128)S(1)}, f32[128,128]{1,0:T(8,128)S(1)}, f...) custom-call(bf16[128,3584]{1,0:T(8,128)(2,1)S(1)} %copy-done, ...), custom_call_target="tpu_custom_call" | custom-call | tf_op jit(solution)/shard_map/pallas_call | solution.py:43
  20.7 0.0 collective-permute-done.2.refs_1_
  20.8 0.0 copy-done.10
  20.8 0.0 copy-start.9
  20.8 2.6 %shard_map.85 = (f32[128,128]{1,0:T(8,128)S(1)}, f32[128,128]{1,0:T(8,128)S(1)}, f32[128,128]{1,0:T(8,128)S(1)}, f32[128,3584]{1,0:T(8,128)S(1)}) custom-call(s32[1,4]{1,0:T(1,128)S(1)} %copy-done.10, bf16[128,3584]{1,0:T(8,128)(2,1)S(1)} %collective-permute-done.2.refs_1_, ...), custom_call_target="tpu_custom_call", output_to_operand_aliasing={{1}: (4, {}), {2}: (5, {}), {3}: (6, {})} | custom-call | tf_op jit(solution)/shard_map/pallas_call | solution.py:43
  23.4 11.0 %collective-permute-done.1.refs_0_ = bf16[128,3584]{1,0:T(8,128)(2,1)S(1)} collective-permute-done((bf16[128,3584]{1,0:T(8,128)(2,1)}, bf16[128,3584]{1,0:T(8,128)(2,1)S(1)}, u32[]{:S(2)}, u32[]{:S(2)}) %collective-permute-start.1) | collective-permute-done | bytes 917536 | tf_op jit(solution)/shard_map/ppermute | solution.py:250
  34.5 0.0 copy-done.9
  34.5 0.4 shard_map.86.refs_1_
  34.9 2.4 %collective-permute-start.3 = (bf16[128,3584]{1,0:T(8,128)(2,1)S(1)}, bf16[128,3584]{1,0:T(8,128)(2,1)S(1)}, u32[]{:S(2)}, u32[]{:S(2)}) collective-permute-start(bf16[128,3584]{1,0:T(8,128)(2,1)S(1)} %shard_map.86.refs_1_), channel_id=1, source_target_pairs={{0,1},{1,0},{2,3},{3,2},{4,5},{5,4},{6,7},{7,6},{8,9},{9,8},{10,11... | collective-permute-start | bytes 2752520 | tf_op jit(solution)/shard_map/ppermute | solution.py:250
  37.3 9.4 %collective-permute-start = (bf16[128,3584]{1,0:T(8,128)(2,1)S(1)}, bf16[128,3584]{1,0:T(8,128)(2,1)S(1)}, u32[]{:S(2)}, u32[]{:S(2)}) collective-permute-start(bf16[128,3584]{1,0:T(8,128)(2,1)S(1)} %get-tuple-element.31), channel_id=1, source_target_pairs={{766,0},{3,1},{0,2},{5,3},{2,4},{7,5},{4,6},{9,7},{6,8},{11,9},{8,... | collective-permute-start | bytes 2752520 | tf_op jit(solution)/shard_map/ppermute | solution.py:250
  46.8 2.4 %shard_map.87 = (f32[128,128]{1,0:T(8,128)S(1)}, f32[128,128]{1,0:T(8,128)S(1)}, f32[128,128]{1,0:T(8,128)S(1)}, f32[128,3584]{1,0:T(8,128)S(1)}) custom-call(s32[1,4]{1,0:T(1,128)S(1)} %copy-done.10, bf16[128,3584]{1,0:T(8,128)(2,1)S(1)} %shard_map.86.refs_1_, f32[28,128]{1,0:T(8,128)S(1)} %bitcast.7, ...), custom_call_target="tpu_custom_call", output_to_operand_aliasing={{1}: (4, {}), {2}: (5, {}), {3}: (6, {})} | custom-call | tf_op jit(solution)/shard_map/pallas_call | solution.py:43
  49.1 0.0 collective-permute-done.3.refs_1_
  49.1 0.0 copy-start.1
  49.2 0.0 copy-start.12
  49.2 2.4 %shard_map.88 = (f32[128,128]{1,0:T(8,128)S(1)}, f32[128,128]{1,0:T(8,128)S(1)}, f32[128,128]{1,0:T(8,128)S(1)}, f32[128,3584]{1,0:T(8,128)S(1)}) custom-call(s32[1,4]{1,0:T(1,128)S(1)} %copy-done.10, bf16[128,3584]{1,0:T(8,128)(2,1)S(1)} %collective-permute-done.3.refs_1_, ...), custom_call_target="tpu_custom_call", output_to_operand_aliasing={{1}: (4, {}), {2}: (5, {}), {3}: (6, {})} | custom-call | tf_op jit(solution)/shard_map/pallas_call | solution.py:43
  51.5 5.5 %collective-permute-done.refs_1_ = bf16[128,3584]{1,0:T(8,128)(2,1)S(1)} collective-permute-done((bf16[128,3584]{1,0:T(8,128)(2,1)S(1)}, bf16[128,3584]{1,0:T(8,128)(2,1)S(1)}, u32[]{:S(2)}, u32[]{:S(2)}) %collective-permute-start) | collective-permute-done | bytes 917536 | tf_op jit(solution)/shard_map/ppermute | solution.py:250
  57.1 0.0 copy-done.1
  57.1 0.0 copy-done.12
  57.1 5.2 %shard_map.89 = (f32[128,3584]{1,0:T(8,128)S(1)}, f32[8,32,128]{2,1,0:T(8,128)}, f32[128,3584]{1,0:T(8,128)S(1)}, bf16[2,128,3584]{2,1,0:T(8,128)(2,1)}, f32[128...) custom-call(s32[1,4]{1,0:T(1,128)S(1)} %copy-done.10, ...), custom_call_target="tpu_custom_call", output_to_operand_aliasing={{0}: (6, {})} | custom-call | tf_op jit(solution)/shard_map/pallas_call | solution.py:43
  62.3 0.0 copy-start.4
  62.3 1.3 copy-done.4
  63.5 0.0 copy-start.6
  63.5 1.2 copy-done.6
  64.8 0.0 copy-start.13
  64.8 0.9 copy-done.13
  65.7 3.2 %collective-permute-start.4 = (bf16[2,128,3584]{2,1,0:T(8,128)(2,1)}, bf16[2,128,3584]{2,1,0:T(8,128)(2,1)}, u32[]{:S(2)}, u32[]{:S(2)}) collective-permute-start(bf16[2,128,3584]{2,1,0:T(8,128)(2,1)} %get-tuple-element.55), channel_id=1, source_target_pairs={{0,1},{1,0},{2,3},{3,2},{4,5},{5,4},{6,7},{7,6},{8,9},{9,8},{10,11... | collective-permute-start | bytes 5505032 | tf_op jit(solution)/shard_map/ppermute | solution.py:250
  68.9 3.8 %all-to-all-start = ((f32[8,32,128]{2,1,0:T(8,128)}), f32[8,32,128]{2,1,0:T(8,128)S(1)}, u32[]{:S(2)}, u32[]{:S(2)}) async-start(f32[8,32,128]{2,1,0:T(8,128)} %get-tuple-element.50), calls=%async_computation | async-start | bytes 262144 | tf_op jit(solution)/shard_map/all_to_all | solution.py:298
  72.8 1.9 %collective-permute-start.5 = (bf16[128,3584]{1,0:T(8,128)(2,1)}, bf16[128,3584]{1,0:T(8,128)(2,1)}, u32[]{:S(2)}, u32[]{:S(2)}) collective-permute-start(bf16[128,3584]{1,0:T(8,128)(2,1)} %copy-done.13), channel_id=1, source_target_pairs={{0,766},{1,3},{2,0},{3,5},{4,2},{5,7},{6,4},{7,9},{8,6},{9,11},{10... | collective-permute-start | bytes 2752520 | tf_op jit(solution)/shard_map/ppermute | solution.py:250
  74.7 6.6 %all-to-all-done.refs_0_ = f32[8,32,128]{2,1,0:T(8,128)S(1)} async-done(((f32[8,32,128]{2,1,0:T(8,128)}), f32[8,32,128]{2,1,0:T(8,128)S(1)}, u32[]{:S(2)}, u32[]{:S(2)}) %all-to-all-start) | async-done | bytes 131104 | tf_op jit(solution)/shard_map/all_to_all | solution.py:298
  81.3 0.0 collective-permute-done.4.refs_1_.refs_3_
  81.3 0.0 copy-start.7
  81.3 1.5 %copy-done.7 = f32[128,3584]{1,0:T(8,128)S(1)} copy-done((f32[128,3584]{1,0:T(8,128)S(1)}, f32[128,3584]{1,0:T(8,128)}, u32[]{:S(2)}) %copy-start.7) | copy-done | bytes 1835032
  82.8 2.6 %shard_map.94 = bf16[128,3584]{1,0:T(8,128)(2,1)} custom-call(f32[128,3584]{1,0:T(8,128)S(1)} %copy-done.7, bf16[2,128,3584]{2,1,0:T(8,128)(2,1)} %collective-permute-done.4.refs_1_.refs_3_, f32[12,32,128]{2,1,0:T(8,128)S(1)} %shard_map.90.refs_2_), custom_call_target="tpu_custom_call" | custom-call | tf_op jit(solution)/shard_map/pallas_call | solution.py:43
  85.4 4.6 %collective-permute-start.6 = (bf16[128,3584]{1,0:T(8,128)(2,1)}, bf16[128,3584]{1,0:T(8,128)(2,1)}, u32[]{:S(2)}, u32[]{:S(2)}) collective-permute-start(bf16[128,3584]{1,0:T(8,128)(2,1)} %shard_map.94), channel_id=1, source_target_pairs={{0,2},{1,767},{2,4},{3,1},{4,6},{5,3},{6,8},{7,5},{8,10},{9,7},{10... | collective-permute-start | bytes 2752520 | tf_op jit(solution)/shard_map/ppermute | solution.py:250
  90.0 19.2 %all_to_all.15.refs_0_ = f32[12,32,128]{2,1,0:T(8,128)S(1)} all-to-all(f32[12,32,128]{2,1,0:T(8,128)S(1)} %shard_map.90.refs_2_), channel_id=1, replica_groups=mesh['y'=8,'z'=12,'row'=8] {'z'}, dimensions={0} | all-to-all | bytes 393216 | tf_op jit(solution)/shard_map/all_to_all | solution.py:302
  109.2 0.7 shard_map.91
  109.8 4.6 %all-to-all-start.2 = ((f32[8,32,128]{2,1,0:T(8,128)}), f32[8,32,128]{2,1,0:T(8,128)S(1)}, u32[]{:S(2)}, u32[]{:S(2)}) async-start(f32[8,32,128]{2,1,0:T(8,128)} %shard_map.91), calls=%async_computation.2 | async-start | bytes 262144 | tf_op jit(solution)/shard_map/all_to_all | solution.py:304
  114.5 1.7 %shard_map.93 = bf16[128,3584]{1,0:T(8,128)(2,1)} custom-call(bf16[128,3584]{1,0:T(8,128)(2,1)S(1)} %copy-done.1, f32[28,128]{1,0:T(8,128)S(1)} %bitcast.9, f32[128,3584]{1,0:T(8,128)S(1)} %get-tuple-element.53.refs_2_), custom_call_target="tpu_custom_call" | custom-call | tf_op jit(solution)/shard_map/pallas_call | solution.py:43
  116.1 3.6 %all-to-all-done.2.refs_0_ = f32[8,32,128]{2,1,0:T(8,128)S(1)} async-done(((f32[8,32,128]{2,1,0:T(8,128)}), f32[8,32,128]{2,1,0:T(8,128)S(1)}, u32[]{:S(2)}, u32[]{:S(2)}) %all-to-all-start.2) | async-done | bytes 131104 | tf_op jit(solution)/shard_map/all_to_all | solution.py:304
  119.7 0.6 shard_map.92
  120.4 0.0 collective-permute-done.5.refs_4_
  120.4 0.0 collective-permute-done.6.refs_5_
  120.4 0.0 copy-start.3
  120.4 1.2 copy-done.3
  121.6 0.0 copy-start.5
  121.6 1.5 %copy-done.5 = f32[128,3584]{1,0:T(8,128)S(1)} copy-done((f32[128,3584]{1,0:T(8,128)S(1)}, f32[128,3584]{1,0:T(8,128)}, u32[]{:S(2)}) %copy-start.5) | copy-done | bytes 1835032
  123.1 4.1 %shard_map.95 = bf16[128,3584]{1,0:T(8,128)(2,1)} custom-call(bf16[128,3584]{1,0:T(8,128)(2,1)S(1)} %copy-done.3, f32[28,128]{1,0:T(8,128)S(1)} %bitcast.10, f32[128,3584]{1,0:T(8,128)S(1)} %copy-done.5, bf16[2,128,3584]{2,1,0:T(8,128)(2,1)} %collective-permute-done.4.refs_1_.refs_3_, bf16[128,3584]{1,0:T(8,128)(2,1)} %collective-permute-done.5.refs_4_, ...), custom_call_target="tpu_custom_call" | custom-call | tf_op jit(solution)/shard_map/pallas_call | solution.py:43
  (1 shorter events, 0.0 us)
Async XLA Ops:
  0.6 20.1 %copy-start.10 = (s32[1,4]{1,0:T(1,128)S(1)}, s32[1,4]{1,0:T(1,128)}, u32[]{:S(2)}) copy-start(s32[1,4]{1,0:T(1,128)} %refs_0_.11) | copy-start | bytes 52
  0.6 20.1 %collective-permute-start.2 = (bf16[128,3584]{1,0:T(8,128)(2,1)}, bf16[128,3584]{1,0:T(8,128)(2,1)S(1)}, u32[]{:S(2)}, u32[]{:S(2)}) collective-permute-start(bf16[128,3584]{1,0:T(8,128)(2,1)} %refs_0_.13), channel_id=1, source_target_pairs={{0,1},{1,0},{2,3},{3,2},{4,5},{5,4},{6,7},{7,6},{8,9},{9,8},{10,11... | collective-permute-start | bytes 2752520 | tf_op jit(solution)/shard_map/ppermute | solution.py:250
  13.1 21.4 %collective-permute-start.1 = (bf16[128,3584]{1,0:T(8,128)(2,1)}, bf16[128,3584]{1,0:T(8,128)(2,1)S(1)}, u32[]{:S(2)}, u32[]{:S(2)}) collective-permute-start(bf16[128,3584]{1,0:T(8,128)(2,1)} %refs_0_.13), channel_id=1, source_target_pairs={{2,0},{767,1},{4,2},{1,3},{6,4},{3,5},{8,6},{5,7},{10,8},{7,9},{12... | collective-permute-start | bytes 2752520 | tf_op jit(solution)/shard_map/ppermute | solution.py:250
  15.0 1.2 copy-start
  16.2 1.2 copy-start.2
  17.4 0.7 copy-start.8
  18.1 0.7 copy-start.11
  20.8 13.7 %copy-start.9 = (f32[3584]{0:T(1024)S(1)}, f32[3584]{0:T(1024)}, u32[]{:S(2)}) copy-start(f32[3584]{0:T(1024)} %param.7) | copy-start | bytes 43012
  34.9 14.3 %collective-permute-start.3 = (bf16[128,3584]{1,0:T(8,128)(2,1)S(1)}, bf16[128,3584]{1,0:T(8,128)(2,1)S(1)}, u32[]{:S(2)}, u32[]{:S(2)}) collective-permute-start(bf16[128,3584]{1,0:T(8,128)(2,1)S(1)} %shard_map.86.refs_1_), channel_id=1, source_target_pairs={{0,1},{1,0},{2,3},{3,2},{4,5},{5,4},{6,7},{7,6},{8,9},{9,8},{10,11... | collective-permute-start | bytes 2752520 | tf_op jit(solution)/shard_map/ppermute | solution.py:250
  37.3 19.8 %collective-permute-start = (bf16[128,3584]{1,0:T(8,128)(2,1)S(1)}, bf16[128,3584]{1,0:T(8,128)(2,1)S(1)}, u32[]{:S(2)}, u32[]{:S(2)}) collective-permute-start(bf16[128,3584]{1,0:T(8,128)(2,1)S(1)} %get-tuple-element.31), channel_id=1, source_target_pairs={{766,0},{3,1},{0,2},{5,3},{2,4},{7,5},{4,6},{9,7},{6,8},{11,9},{8,... | collective-permute-start | bytes 2752520 | tf_op jit(solution)/shard_map/ppermute | solution.py:250
  49.1 7.9 %copy-start.1 = (bf16[128,3584]{1,0:T(8,128)(2,1)S(1)}, bf16[128,3584]{1,0:T(8,128)(2,1)}, u32[]{:S(2)}) copy-start(bf16[128,3584]{1,0:T(8,128)(2,1)} %refs_0_.12) | copy-start | bytes 2752516
  49.2 7.9 %copy-start.12 = (s32[128]{0:T(128)S(1)}, s32[128]{0:T(128)}, u32[]{:S(2)}) copy-start(s32[128]{0:T(128)} %param.8) | copy-start | bytes 1540
  62.3 1.3 copy-start.4
  63.5 1.2 copy-start.6
  64.8 0.9 copy-start.13
  65.7 15.6 %collective-permute-start.4 = (bf16[2,128,3584]{2,1,0:T(8,128)(2,1)}, bf16[2,128,3584]{2,1,0:T(8,128)(2,1)}, u32[]{:S(2)}, u32[]{:S(2)}) collective-permute-start(bf16[2,128,3584]{2,1,0:T(8,128)(2,1)} %get-tuple-element.55), channel_id=1, source_target_pairs={{0,1},{1,0},{2,3},{3,2},{4,5},{5,4},{6,7},{7,6},{8,9},{9,8},{10,11... | collective-permute-start | bytes 5505032 | tf_op jit(solution)/shard_map/ppermute | solution.py:250
  68.9 12.3 %all-to-all-start = ((f32[8,32,128]{2,1,0:T(8,128)}), f32[8,32,128]{2,1,0:T(8,128)S(1)}, u32[]{:S(2)}, u32[]{:S(2)}) async-start(f32[8,32,128]{2,1,0:T(8,128)} %get-tuple-element.50), calls=%async_computation | async-start | bytes 262144 | tf_op jit(solution)/shard_map/all_to_all | solution.py:298
  72.8 47.6 %collective-permute-start.5 = (bf16[128,3584]{1,0:T(8,128)(2,1)}, bf16[128,3584]{1,0:T(8,128)(2,1)}, u32[]{:S(2)}, u32[]{:S(2)}) collective-permute-start(bf16[128,3584]{1,0:T(8,128)(2,1)} %copy-done.13), channel_id=1, source_target_pairs={{0,766},{1,3},{2,0},{3,5},{4,2},{5,7},{6,4},{7,9},{8,6},{9,11},{10... | collective-permute-start | bytes 2752520 | tf_op jit(solution)/shard_map/ppermute | solution.py:250
  81.3 1.5 %copy-start.7 = (f32[128,3584]{1,0:T(8,128)S(1)}, f32[128,3584]{1,0:T(8,128)}, u32[]{:S(2)}) copy-start(f32[128,3584]{1,0:T(8,128)} %copy-done.6) | copy-start | bytes 5505028
  85.4 35.0 %collective-permute-start.6 = (bf16[128,3584]{1,0:T(8,128)(2,1)}, bf16[128,3584]{1,0:T(8,128)(2,1)}, u32[]{:S(2)}, u32[]{:S(2)}) collective-permute-start(bf16[128,3584]{1,0:T(8,128)(2,1)} %shard_map.94), channel_id=1, source_target_pairs={{0,2},{1,767},{2,4},{3,1},{4,6},{5,3},{6,8},{7,5},{8,10},{9,7},{10... | collective-permute-start | bytes 2752520 | tf_op jit(solution)/shard_map/ppermute | solution.py:250
  109.8 9.9 %all-to-all-start.2 = ((f32[8,32,128]{2,1,0:T(8,128)}), f32[8,32,128]{2,1,0:T(8,128)S(1)}, u32[]{:S(2)}, u32[]{:S(2)}) async-start(f32[8,32,128]{2,1,0:T(8,128)} %shard_map.91), calls=%async_computation.2 | async-start | bytes 262144 | tf_op jit(solution)/shard_map/all_to_all | solution.py:304
  120.4 1.2 copy-start.3
  121.6 1.5 %copy-start.5 = (f32[128,3584]{1,0:T(8,128)S(1)}, f32[128,3584]{1,0:T(8,128)}, u32[]{:S(2)}) copy-start(f32[128,3584]{1,0:T(8,128)} %copy-done.4) | copy-start | bytes 5505028

commit v2 on v1

v2 whole, which is shorter than its diff:
```python
import functools
import math

import jax
import jax.numpy as jnp
import numpy as np
from jax import lax
from jax.experimental import pallas as pl
from jax.experimental.pallas import tpu as pltpu
from jax.sharding import Mesh
from jax.sharding import PartitionSpec as P

logit_scale = 4.0
ROWS = 128
WIDTH = 3584
FACTOR = logit_scale / math.sqrt(WIDTH)
LANES = 128
GAIN_ROWS = WIDTH // LANES
SUM_ROWS = 32
CHUNK = 512
HIDDEN = -1e30
STEP = 16
PARTS = 4
PART = ROWS // PARTS
f32, bf16 = jnp.float32, jnp.bfloat16
AXES = ("y", "z", "row")

in_vmem = pl.BlockSpec(memory_space=pltpu.VMEM)
anywhere = pl.BlockSpec(memory_space=pl.ANY)
in_smem = pl.BlockSpec(memory_space=pltpu.SMEM)


def held(shape, dtype):
    return pltpu.VMEM(shape, dtype)


def call(kernel, out_shape, args, scratch=(), aliases=None, scalars=(), distant=(), after=()):
    given = len(scalars) + len(args) + len(distant)

    def run(*refs):
        kernel(*refs[:given], *refs[given + len(after) :])

    flat, tree = jax.tree.flatten(out_shape)
    outs = [anywhere if is_distant(x) else in_vmem for x in flat]
    return pl.pallas_call(
        run,
        in_specs=[in_smem] * len(scalars) + [in_vmem] * len(args) + [anywhere] * (len(distant) + len(after)),
        out_specs=jax.tree.unflatten(tree, outs),
        out_shape=out_shape,
        scratch_shapes=list(scratch),
        input_output_aliases=aliases or {},
        cost_estimate=pl.CostEstimate(flops=1000, bytes_accessed=1000, transcendentals=0),
        compiler_params=pltpu.CompilerParams(vmem_limit_bytes=15 * 2**20),
    )(*scalars, *args, *distant, *after)


def kept(x):
    return pltpu.with_memory_space_constraint(x, pltpu.VMEM)


def leave(x):
    return pltpu.with_memory_space_constraint(x, pltpu.HBM)


def distant_array(shape, dtype):
    return pltpu.HBM(shape, dtype)


def is_distant(shape):
    return getattr(shape, "memory_space", None) == pltpu.HBM


def factor_of(values):
    return lax.rsqrt(jnp.mean(values * values, axis=-1, keepdims=True) + 1e-06)


def head_into(hidden_ref, gain, out_ref):
    for i in range(0, ROWS, STEP):
        values = hidden_ref[i : i + STEP, :].astype(f32)
        out_ref[i : i + STEP, :] = (values * factor_of(values) * gain).astype(bf16)


def scores_of(queries, docs):
    dims = (((1,), (1,)), ((), ()))
    return FACTOR * lax.dot_general(queries, docs, dims, preferred_element_type=f32)


def across(column):
    return jnp.broadcast_to(column, (ROWS, LANES))


def onehot_of(positives_ref):
    slots = lax.broadcasted_iota(jnp.int32, (ROWS, ROWS), 0)
    return (slots == positives_ref[...]).astype(f32).T


def listed(neg_ref, distance):
    place, count = 0, 1
    for axis in AXES:
        place = place * lax.axis_size(axis) + lax.axis_index(axis)
        count = count * lax.axis_size(axis)
    sign = 1 - 2 * lax.rem(place, 2)
    block = lax.rem(place + sign * distance + count, count)
    found = neg_ref[0, 0] == block
    for i in range(1, neg_ref.shape[1]):
        found = jnp.logical_or(found, neg_ref[0, i] == block)
    return found


def own_kernel(
    q_hbm, d_hbm, gain_hbm, pos_hbm,
    qn_ref, dn_ref, gain_ref, s_ref, top_ref, total_ref, acc_ref, picked_ref,
    q_ref, d_ref, line_ref, pos_ref, sems,
):
    pairs = ((d_hbm, d_ref), (gain_hbm, line_ref), (q_hbm, q_ref), (pos_hbm, pos_ref))
    copies = [pltpu.make_async_copy(src, dst, sems.at[i]) for i, (src, dst) in enumerate(pairs)]
    for copy in copies:
        copy.start()
    copies[0].wait()
    copies[1].wait()
    gain = jnp.concatenate([line_ref[i : i + 1, :] for i in range(GAIN_ROWS)], axis=1)
    gain_ref[...] = gain
    head_into(d_ref, gain, dn_ref)
    copies[2].wait()
    copies[3].wait()
    head_into(q_ref, gain, qn_ref)
    scores = scores_of(qn_ref[...], dn_ref[...])
    top = jnp.max(scores, axis=1, keepdims=True)
    probs = jnp.exp(scores - top)
    s_ref[...] = scores
    top_ref[...] = across(top)
    total_ref[...] = across(jnp.sum(probs, axis=1, keepdims=True))
    probs = probs.astype(bf16)
    onehot = onehot_of(pos_ref).astype(bf16)
    for c in range(0, WIDTH, CHUNK):
        docs = dn_ref[:, c : c + CHUNK]
        acc_ref[:, c : c + CHUNK] = jnp.dot(probs, docs, preferred_element_type=f32)
        picked_ref[:, c : c + CHUNK] = jnp.dot(onehot, docs, preferred_element_type=f32).astype(bf16)


def head_kernel(x_ref, gain_ref, out_ref):
    head_into(x_ref, gain_ref[...], out_ref)


def fold(scores, dn_ref, top0_ref, total0_ref, acc0_ref):
    before = top0_ref[:, 0:1]
    top = jnp.maximum(before, jnp.max(scores, axis=1, keepdims=True))
    shrink = jnp.exp(before - top)
    probs = jnp.exp(scores - top)
    total = total0_ref[:, 0:1] * shrink + jnp.sum(probs, axis=1, keepdims=True)
    probs = probs.astype(bf16)

    def weighted(c):
        term = jnp.dot(probs, dn_ref[:, c : c + CHUNK], preferred_element_type=f32)
        return acc0_ref[:, c : c + CHUNK] * shrink + term

    return top, total, weighted


def step_kernel(distance, neg_ref, dn_ref, qn_ref, top0_ref, total0_ref, acc0_ref, s_ref, top_ref, total_ref, acc_ref):
    scores = jnp.where(listed(neg_ref, distance), scores_of(qn_ref[...], dn_ref[...]), HIDDEN)
    top, total, weighted = fold(scores, dn_ref, top0_ref, total0_ref, acc0_ref)
    s_ref[...] = scores
    for c in range(0, WIDTH, CHUNK):
        acc_ref[:, c : c + CHUNK] = weighted(c)
    top_ref[...] = across(top)
    total_ref[...] = across(total)


def last_kernel(
    distance, neg_ref, dn_ref, qn_ref, top0_ref, total0_ref, acc0_ref, picked_ref, s_own_ref, pos_hbm, q_hbm,
    s_ref, lse_ref, gq_ref, hot_ref, part_ref, q_ref, pos_ref, gain_sum, sems,
):
    copies = [pltpu.make_async_copy(q_hbm, q_ref, sems.at[0]), pltpu.make_async_copy(pos_hbm, pos_ref, sems.at[1])]
    for copy in copies:
        copy.start()
    scores = jnp.where(listed(neg_ref, distance), scores_of(qn_ref[...], dn_ref[...]), HIDDEN)
    top, total, weighted = fold(scores, dn_ref, top0_ref, total0_ref, acc0_ref)
    lse = top + jnp.log(total)
    s_ref[...] = scores
    lse_ref[...] = across(lse)
    for copy in copies:
        copy.wait()
    onehot = onehot_of(pos_ref)
    hot_ref[...] = onehot
    loss = jnp.sum(lse - jnp.sum(s_own_ref[...] * onehot, axis=1, keepdims=True))
    share = FACTOR / total
    for c in range(0, WIDTH, CHUNK):
        gq_ref[:, c : c + CHUNK] = weighted(c) * share - FACTOR * picked_ref[:, c : c + CHUNK].astype(f32)
    for i in range(0, ROWS, STEP):
        values = q_ref[i : i + STEP, :].astype(f32)
        added = gq_ref[i : i + STEP, :] * (values * factor_of(values))
        added = added[:8] + added[8:]
        gain_sum[...] = added if i == 0 else gain_sum[...] + added
    gain_part = 2.0 * jnp.sum(gain_sum[...], axis=0, keepdims=True)
    share_rows = part_ref.shape[1]
    for i in range(GAIN_ROWS):
        line = gain_part[:, i * LANES : (i + 1) * LANES]
        part_ref[i // share_rows, i % share_rows : i % share_rows + 1, :] = line
    for i in range(GAIN_ROWS, SUM_ROWS):
        part_ref[i // share_rows, i % share_rows : i % share_rows + 1, :] = jnp.full((1, LANES), loss, f32)


def term_kernel(
    qn_ref, gain_ref, gq_ref, lse_ref, hot_ref, s_own_ref, s_swap_ref, s_relay_ref, s_far_ref, s_back_ref, q_hbm,
    near_hbm, back_hbm, far_hbm, own_hbm, grad_hbm, q_ref, grad_ref, weight_ref, term_ref, sems, row_sems,
):
    incoming = pltpu.make_async_copy(q_hbm, q_ref, sems.at[0])
    incoming.start()
    blocks = (s_relay_ref, s_swap_ref, s_back_ref, s_far_ref, s_own_ref)
    for k, block_ref in enumerate(blocks):
        weight = jnp.exp(block_ref[...] - lse_ref[...])
        if block_ref is s_own_ref:
            weight = weight - hot_ref[...]
        weight_ref[k * ROWS : (k + 1) * ROWS, :] = weight.T.astype(bf16)
    targets = (near_hbm.at[0], near_hbm.at[1], back_hbm, far_hbm, own_hbm)
    outgoing = []
    for k, target in enumerate(targets):
        weight = weight_ref[k * ROWS : (k + 1) * ROWS, :]
        for c in range(0, WIDTH, CHUNK):
            cols = slice(c, c + CHUNK)
            term_ref[k, :, cols] = jnp.dot(weight, qn_ref[:, cols], preferred_element_type=f32).astype(bf16)
        copy = pltpu.make_async_copy(term_ref.at[k], target, sems.at[k + 1])
        copy.start()
        outgoing.append(copy)
    incoming.wait()
    gain = gain_ref[...]
    for part in range(PARTS):
        for i in range(part * PART, (part + 1) * PART, STEP):
            rows = slice(i, i + STEP)
            grad_ref[rows, :] = pull(q_ref[rows, :].astype(f32), gain, gq_ref[rows, :]).astype(bf16)
        rows = pl.ds(part * PART, PART)
        copy = pltpu.make_async_copy(grad_ref.at[rows, :], grad_hbm.at[rows, :], row_sems.at[part])
        copy.start()
        outgoing.append(copy)
    for copy in outgoing:
        copy.wait()


def pull(values, gain, cotangent):
    factor = factor_of(values)
    scaled = gain * cotangent
    inner = jnp.sum(values * scaled, axis=-1, keepdims=True) / WIDTH
    return factor * scaled - values * (factor * factor * factor * inner)


def by_parts(sources, target, buffers, out_ref, sems, work):
    def copies(part):
        rows = pl.ds(part * PART, PART)
        return [
            pltpu.make_async_copy(source.at[rows, :], buffers.at[k, rows, :], sems.at[k, part])
            for k, source in enumerate(sources)
        ]

    incoming = [copies(part) for part in range(PARTS)]
    for part in incoming:
        for copy in part:
            copy.start()
    outgoing = []
    for part in range(PARTS):
        for copy in incoming[part]:
            copy.wait()
        for i in range(part * PART, (part + 1) * PART, STEP):
            rows = slice(i, i + STEP)
            out_ref[rows, :] = work(*[buffers[k, rows, :].astype(f32) for k in range(len(sources))]).astype(bf16)
        rows = pl.ds(part * PART, PART)
        copy = pltpu.make_async_copy(out_ref.at[rows, :], target.at[rows, :], sems.at[len(sources), part])
        copy.start()
        outgoing.append(copy)
    for copy in outgoing:
        copy.wait()


def grad_doc_kernel(gain_ref, d_hbm, own_hbm, near_hbm, back_hbm, far_hbm, grad_hbm, buffers, out_ref, sems):
    gain = gain_ref[...]

    def work(values, own, near, back, far):
        return pull(values, gain, FACTOR * (own + near + back + far))

    by_parts((d_hbm, own_hbm, near_hbm.at[1], back_hbm, far_hbm), grad_hbm, buffers, out_ref, sems, work)


def add_kernel(far_hbm, near_hbm, sum_hbm, buffers, out_ref, sems):
    by_parts((far_hbm, near_hbm.at[0]), sum_hbm, buffers, out_ref, sems, lambda far, near: far + near)


def sum_kernel(in_ref, out_ref):
    total = jnp.sum(in_ref[...], axis=0)
    out_ref[...] = jnp.broadcast_to(total[None], out_ref.shape)


def end_kernel(denom, in_ref, gain_ref, loss_ref):
    rows = in_ref.shape[1]
    total = in_ref[...] / denom
    for i in range(GAIN_ROWS):
        gain_ref[i : i + 1, :] = total[i // rows, i % rows : i % rows + 1, :]
    loss_ref[...] = total[GAIN_ROWS // rows, GAIN_ROWS % rows : GAIN_ROWS % rows + 1, 0:1]


def body(query_hidden, doc_hidden, gain, positives, neg_blocks):
    count = lax.axis_size(AXES)
    gain = gain.reshape(GAIN_ROWS, LANES)
    positives = positives.reshape(1, ROWS)

    devices = range(count)
    far_source = [(i + 2 if i % 2 == 0 else i - 2) % count for i in devices]
    back_source = [(i - 2 if i % 2 == 0 else i + 2) % count for i in devices]

    def permute(x, route):
        return lax.ppermute(x, AXES, route)

    swap_route = [(i, i ^ 1) for i in devices]
    square, block = (ROWS, LANES), (ROWS, WIDTH)
    dma = pltpu.SemaphoreType.DMA
    far = permute(doc_hidden, [(far_source[i], i) for i in devices])
    qn, dn, gain_line, s_own, *state, picked = call(
        own_kernel,
        [held(block, bf16)] * 2
        + [held((1, WIDTH), f32)]
        + [held(square, f32)] * 3
        + [held(block, f32), held(block, bf16)],
        (),
        distant=(leave(query_hidden), leave(doc_hidden), leave(gain), leave(positives)),
        scratch=[
            pltpu.VMEM(block, bf16), pltpu.VMEM(block, bf16), pltpu.VMEM((GAIN_ROWS, LANES), f32),
            pltpu.VMEM((1, ROWS), jnp.int32), dma((4,)),
        ],
    )
    qn, gain_line, picked, s_own = kept(qn), kept(gain_line), kept(picked), kept(s_own)
    back = permute(dn, [(back_source[i], i) for i in devices])
    swap = permute(dn, swap_route)

    def step(distance, docs, state):
        return call(
            functools.partial(step_kernel, distance),
            [held(square, f32)] * 3 + [held(block, f32)],
            (docs, qn, *map(kept, state)),
            scalars=(neg_blocks,),
            aliases={3: 1, 4: 2, 5: 3},
        )

    far = call(head_kernel, held(block, bf16), (far, gain_line))
    relay = permute(far, swap_route)
    s_swap, *state = step(1, swap, state)
    s_far, *state = step(2, far, state)
    s_back, *state = step(-2, back, state)
    sizes = [lax.axis_size(a) for a in AXES]
    share = (SUM_ROWS // sizes[2], LANES)
    s_relay, lse, gq, hot, part = call(
        functools.partial(last_kernel, -1),
        [held(square, f32)] * 2 + [held(block, f32), held(square, f32), held((sizes[2], *share), f32)],
        (relay, qn, *map(kept, state), picked, s_own),
        scalars=(neg_blocks,),
        distant=(leave(positives), leave(query_hidden)),
        scratch=[pltpu.VMEM(block, bf16), pltpu.VMEM((1, ROWS), jnp.int32), pltpu.VMEM((8, WIDTH), f32), dma((2,))],
        aliases={5: 2},
    )

    def exchange(x, axis):
        return kept(lax.all_to_all(x, AXES[axis], 0, 0, tiled=True))

    def summed(x, axis):
        return call(sum_kernel, held((sizes[axis], *share), f32), (x,))

    part = summed(exchange(part, 2), 0)
    t_near, t_back, t_far, t_own, grad_query = call(
        term_kernel,
        [distant_array((2, *block), bf16)] + [distant_array(block, bf16)] * 4,
        (qn, gain_line, kept(gq), kept(lse), kept(hot), s_own, kept(s_swap), kept(s_relay), kept(s_far), kept(s_back)),
        distant=(leave(query_hidden),),
        after=(part,),
        scratch=[
            pltpu.VMEM(block, bf16), pltpu.VMEM(block, bf16), pltpu.VMEM((5 * ROWS, ROWS), bf16),
            pltpu.VMEM((5, *block), bf16), dma((6,)), dma((PARTS,)),
        ],
    )
    near_term = permute(t_near, swap_route)
    back_term = permute(t_back, [(i, back_source[i]) for i in devices])

    part = summed(exchange(part, 0), 1)
    far_sum = call(
        add_kernel,
        distant_array(block, bf16),
        (),
        distant=(leave(t_far), near_term),
        after=(part,),
        scratch=[pltpu.VMEM((2, *block), bf16), pltpu.VMEM(block, bf16), dma((3, PARTS))],
    )
    far_term = permute(far_sum, [(i, far_source[i]) for i in devices])
    part = summed(exchange(part, 1), 2)
    part = exchange(part, 2)
    grad_doc = call(
        grad_doc_kernel,
        distant_array(block, bf16),
        (gain_line,),
        distant=(leave(doc_hidden), leave(t_own), near_term, back_term, far_term),
        scratch=[pltpu.VMEM((5, *block), bf16), pltpu.VMEM(block, bf16), dma((6, PARTS))],
    )
    grad_gain, mean_loss = call(
        functools.partial(end_kernel, float(ROWS * count)),
        [jax.ShapeDtypeStruct((GAIN_ROWS, LANES), f32), jax.ShapeDtypeStruct((1, 1), f32)],
        (part,),
    )
    return mean_loss.reshape(()), grad_gain.reshape(WIDTH), grad_query, grad_doc


def grid_of(count):
    return (8, 12, 8) if count == 768 else (2, count // 16, 8)


def solution(mesh):
    devices = np.asarray(mesh.devices)
    inner = Mesh(devices.reshape(grid_of(devices.size)), AXES)
    placed = (P(AXES, None), P(AXES, None), P(), P(AXES), P(AXES, None))
    return jax.shard_map(
        body,
        mesh=inner,
        in_specs=placed,
        out_specs=(P(), P(), P(AXES, None), P(AXES, None)),
        check_vma=False,
    )
```

time: 128 us -> 115 us (0.90)
  waiting for transfers between devices: 26.8 us -> 6.61 us
  blocking collectives: 19.2 us -> 35.6 us
  local copies, waits for them, and re-layouts: 11.3 us -> 0.01 us
  Pallas kernels: 24.7 us -> 27.9 us
    all_to_all x1 -> x3, blocking collectives: 19.2 us -> 35.6 us  [exchange(): return kept(lax.all_to_all(x, AXES[axis], 0, 0, tiled=True))]
    ppermute x7, waiting for transfers between devices: 16.6 us -> 2.18 us  [permute(): return lax.ppermute(x, AXES, route)]
    unnamed x28 -> x2, local copies, waits for them, and re-layouts: 11.3 us -> 0.01 us
    all_to_all x2 -> x1, waiting for transfers between devices: 10.2 us -> 4.43 us  [exchange(): return kept(lax.all_to_all(x, AXES[axis], 0, 0, tiled=True))]
    all_to_all x2 -> x1, starting transfers between devices: 8.44 us -> 3.82 us  [exchange(): return kept(lax.all_to_all(x, AXES[axis], 0, 0, tiled=True))]
    ppermute x7, starting transfers between devices: 35.9 us -> 39.8 us  [permute(): return lax.ppermute(x, AXES, route)]
    pallas_call x12 -> x13, Pallas kernels: 24.7 us -> 27.9 us  [call(): pl.pallas_call(run, in_specs=[in_smem] * len(scalars) + [in_vmem] * len(a...]
  transfers between devices with their start and end apart: 9 -> 8, of which waited for: 4 -> 2; matrix products, arithmetic and copies ran while one was open for 0% -> 0% of each run, Pallas kernels for 12% -> 13%
where the time goes in v2:
time: 115 us
  starting transfers between devices  43.7 us (38%)
  blocking collectives  35.6 us (31%)
  Pallas kernels  27.9 us (24%)
  waiting for transfers between devices  6.61 us (6%)
    ppermute x7, starting transfers between devices, permute(): return lax.ppermute(x, AXES, route)  39.8 us
    all_to_all x3, blocking collectives, exchange(): return kept(lax.all_to_all(x, AXES[axis], 0, 0, tiled=True))  35.6 us
    pallas_call x13, Pallas kernels, call(): pl.pallas_call(run, in_specs=[in_smem] * len(scalars) + [in_vmem] * len(a...  27.9 us
    all_to_all x1, waiting for transfers between devices, exchange(): return kept(lax.all_to_all(x, AXES[axis], 0, 0, tiled=True))  4.43 us
    all_to_all x1, starting transfers between devices, exchange(): return kept(lax.all_to_all(x, AXES[axis], 0, 0, tiled=True))  3.82 us
  transfers between devices with their start and end apart: 8, of which 2 were waited for; matrix products, arithmetic and copies ran while one was open for 0% of the time, Pallas kernels for 13%

profile of v2, /device:TPU:1, one launch (start us, length us, event | category | flops | bytes accessed | tf_op | source)
XLA Modules:
  0.0 114.6 jit_solution(8063223370640895707)
XLA Ops:
  0.6 4.0 %collective-permute-start = (bf16[128,3584]{1,0:T(8,128)(2,1)}, bf16[128,3584]{1,0:T(8,128)(2,1)S(1)}, u32[]{:S(2)}, u32[]{:S(2)}) collective-permute-start(bf16[128,3584]{1,0:T(8,128)(2,1)} %refs_1_.3), channel_id=1, source_target_pairs={{2,0},{767,1},{4,2},{1,3},{6,4},{3,5},{8,6},{5,7},{10,8},{7,9},{12... | collective-permute-start | bytes 2752520 | tf_op jit(solution)/shard_map/ppermute | solution.py:310
  4.6 0.0 copy-start
  4.6 3.5 %shard_map.84 = (bf16[128,3584]{1,0:T(8,128)(2,1)S(1)}, bf16[128,3584]{1,0:T(8,128)(2,1)S(1)}, f32[1,3584]{1,0:T(1,128)S(1)}, f32[128,128]{1,0:T(8,128)S(1)}, f3...) custom-call(bf16[128,3584]{1,0:T(8,128)(2,1)} %refs_10_.1, ...), custom_call_target="tpu_custom_call" | custom-call | flops 1000 | bytes 1000 | tf_op jit(solution)/shard_map/pallas_call | solution.py:45
  8.1 19.1 %collective-permute-start.3 = (bf16[128,3584]{1,0:T(8,128)(2,1)S(1)}, bf16[128,3584]{1,0:T(8,128)(2,1)S(1)}, u32[]{:S(2)}, u32[]{:S(2)}) collective-permute-start(bf16[128,3584]{1,0:T(8,128)(2,1)S(1)} %get-tuple-element.38), channel_id=1, source_target_pairs={{0,1},{1,0},{2,3},{3,2},{4,5},{5,4},{6,7},{7,6},{8,9},{9,8},{10,11... | collective-permute-start | bytes 2752520 | tf_op jit(solution)/shard_map/ppermute | solution.py:310
  27.2 2.5 %collective-permute-start.2 = (bf16[128,3584]{1,0:T(8,128)(2,1)S(1)}, bf16[128,3584]{1,0:T(8,128)(2,1)S(1)}, u32[]{:S(2)}, u32[]{:S(2)}) collective-permute-start(bf16[128,3584]{1,0:T(8,128)(2,1)S(1)} %get-tuple-element.38), channel_id=1, source_target_pairs={{766,0},{3,1},{0,2},{5,3},{2,4},{7,5},{4,6},{9,7},{6,8},{11,9},{8,... | collective-permute-start | bytes 2752520 | tf_op jit(solution)/shard_map/ppermute | solution.py:310
  29.7 2.2 %collective-permute-done.refs_0_ = bf16[128,3584]{1,0:T(8,128)(2,1)S(1)} collective-permute-done((bf16[128,3584]{1,0:T(8,128)(2,1)}, bf16[128,3584]{1,0:T(8,128)(2,1)S(1)}, u32[]{:S(2)}, u32[]{:S(2)}) %collective-permute-start) | collective-permute-done | bytes 917536 | tf_op jit(solution)/shard_map/ppermute | solution.py:310
  31.9 0.4 shard_map.85.refs_1_
  32.3 5.4 %collective-permute-start.1 = (bf16[128,3584]{1,0:T(8,128)(2,1)S(1)}, bf16[128,3584]{1,0:T(8,128)(2,1)S(1)}, u32[]{:S(2)}, u32[]{:S(2)}) collective-permute-start(bf16[128,3584]{1,0:T(8,128)(2,1)S(1)} %shard_map.85.refs_1_), channel_id=1, source_target_pairs={{0,1},{1,0},{2,3},{3,2},{4,5},{5,4},{6,7},{7,6},{8,9},{9,8},{10,11... | collective-permute-start | bytes 2752520 | tf_op jit(solution)/shard_map/ppermute | solution.py:310
  37.7 0.0 collective-permute-done.3.refs_1_
  37.7 0.0 copy-done
  37.7 2.4 %shard_map.86 = (f32[128,128]{1,0:T(8,128)S(1)}, f32[128,128]{1,0:T(8,128)S(1)}, f32[128,128]{1,0:T(8,128)S(1)}, f32[128,3584]{1,0:T(8,128)S(1)}) custom-call(s32[1,4]{1,0:T(1,128)S(1)} %copy-done, bf16[128,3584]{1,0:T(8,128)(2,1)S(1)} %collective-permute-done.3.refs_1_, ...), custom_call_target="tpu_custom_call", output_to_operand_aliasing={{1}: (3, {}), {2}: (4, {}), {3}: (5, {})} | custom-call | flops 1000 | bytes 1000 | tf_op jit(solution)/shard_map/pallas_call | solution.py:45
  40.1 2.4 %shard_map.87 = (f32[128,128]{1,0:T(8,128)S(1)}, f32[128,128]{1,0:T(8,128)S(1)}, f32[128,128]{1,0:T(8,128)S(1)}, f32[128,3584]{1,0:T(8,128)S(1)}) custom-call(s32[1,4]{1,0:T(1,128)S(1)} %copy-done, bf16[128,3584]{1,0:T(8,128)(2,1)S(1)} %shard_map.85.refs_1_, ...), custom_call_target="tpu_custom_call", output_to_operand_aliasing={{1}: (3, {}), {2}: (4, {}), {3}: (5, {})} | custom-call | flops 1000 | bytes 1000 | tf_op jit(solution)/shard_map/pallas_call | solution.py:45
  42.4 0.0 collective-permute-done.2.refs_1_
  42.5 2.4 %shard_map.88 = (f32[128,128]{1,0:T(8,128)S(1)}, f32[128,128]{1,0:T(8,128)S(1)}, f32[128,128]{1,0:T(8,128)S(1)}, f32[128,3584]{1,0:T(8,128)S(1)}) custom-call(s32[1,4]{1,0:T(1,128)S(1)} %copy-done, bf16[128,3584]{1,0:T(8,128)(2,1)S(1)} %collective-permute-done.2.refs_1_, ...), custom_call_target="tpu_custom_call", output_to_operand_aliasing={{1}: (3, {}), {2}: (4, {}), {3}: (5, {})} | custom-call | flops 1000 | bytes 1000 | tf_op jit(solution)/shard_map/pallas_call | solution.py:45
  44.8 0.0 collective-permute-done.1.refs_1_
  44.8 4.2 %shard_map.89 = (f32[128,128]{1,0:T(8,128)S(1)}, f32[128,128]{1,0:T(8,128)S(1)}, f32[128,3584]{1,0:T(8,128)S(1)}, f32[128,128]{1,0:T(8,128)S(1)}, f32[8,4,128]{2,1,0:T(4,128)S(1)}) custom-call(s32[1,4]{1,0:T(1,128)S(1)} %copy-done, bf16[128,3584]{1,0:T(8,128)(2,1)S(1)} %collective-permute-done.1.refs_1_, ...), custom_call_target="tpu_custom_call", output_to_operand_aliasing={{2}: (5, {})} | custom-call | flops 1000 | bytes 1000 | tf_op jit(solution)/shard_map/pallas_call | solution.py:45
  49.0 12.5 %all_to_all.20.refs_0_ = f32[8,4,128]{2,1,0:T(4,128)S(1)} all-to-all(f32[8,4,128]{2,1,0:T(4,128)S(1)} %get-tuple-element.53), channel_id=1, replica_groups=mesh['y'=8,'z'=12,'row'=8] {'row'}, dimensions={0} | all-to-all | bytes 32768 | tf_op jit(solution)/shard_map/all_to_all | solution.py:360
  61.5 0.6 shard_map.90.refs_11_
  62.1 3.0 %shard_map.94 = (bf16[2,128,3584]{2,1,0:T(8,128)(2,1)}, bf16[128,3584]{1,0:T(8,128)(2,1)}, bf16[128,3584]{1,0:T(8,128)(2,1)}, bf16[128,3584]{1,0:T(8,128)(2,1)}, bf16[128,3584]{1,0:T(8,128)(2,1)}) custom-call(bf16[128,3584]{1,0:T(8,128)(2,1)S(1)} %get-tuple-element.37.refs_2_.refs_0_, f32[1,3584]{1,0:T(1,128)S(1)} %get-tuple-element.36.refs_1_.refs_0_, ...), custom_call_target="tpu_custom_call" | custom-call | flops 1000 | bytes 1000 | tf_op jit(solution)/shard_map/pallas_call | solution.py:45
  65.2 2.6 %collective-permute-start.4 = (bf16[2,128,3584]{2,1,0:T(8,128)(2,1)}, bf16[2,128,3584]{2,1,0:T(8,128)(2,1)S(1)}, u32[]{:S(2)}, u32[]{:S(2)}) collective-permute-start(bf16[2,128,3584]{2,1,0:T(8,128)(2,1)} %get-tuple-element.65), channel_id=1, source_target_pairs={{0,1},{1,0},{2,3},{3,2},{4,5},{5,4},{6,7},{7,6},{8,9},{9,8},{10,11... | collective-permute-start | bytes 5505032 | tf_op jit(solution)/shard_map/ppermute | solution.py:310
  67.8 3.8 %all-to-all-start.1 = ((f32[8,4,128]{2,1,0:T(4,128)}), f32[8,4,128]{2,1,0:T(4,128)S(1)}, u32[]{:S(2)}, u32[]{:S(2)}) async-start(f32[8,4,128]{2,1,0:T(4,128)} %shard_map.90.refs_11_), calls=%async_computation.1 | async-start | bytes 32768 | tf_op jit(solution)/shard_map/all_to_all | solution.py:360
  71.6 2.2 %collective-permute-start.5 = (bf16[128,3584]{1,0:T(8,128)(2,1)}, bf16[128,3584]{1,0:T(8,128)(2,1)S(1)}, u32[]{:S(2)}, u32[]{:S(2)}) collective-permute-start(bf16[128,3584]{1,0:T(8,128)(2,1)} %get-tuple-element.66), channel_id=1, source_target_pairs={{0,766},{1,3},{2,0},{3,5},{4,2},{5,7},{6,4},{7,9},{8,6},{9,11},{10... | collective-permute-start | bytes 2752520 | tf_op jit(solution)/shard_map/ppermute | solution.py:310
  73.8 4.4 %all-to-all-done.1.refs_0_ = f32[8,4,128]{2,1,0:T(4,128)S(1)} async-done(((f32[8,4,128]{2,1,0:T(4,128)}), f32[8,4,128]{2,1,0:T(4,128)S(1)}, u32[]{:S(2)}, u32[]{:S(2)}) %all-to-all-start.1) | async-done | bytes 16416 | tf_op jit(solution)/shard_map/all_to_all | solution.py:360
  78.3 0.0 collective-permute-done.4.refs_1_.refs_3_
  78.3 2.7 %shard_map.95 = bf16[128,3584]{1,0:T(8,128)(2,1)} custom-call(bf16[128,3584]{1,0:T(8,128)(2,1)} %get-tuple-element.67.refs_0_, bf16[2,128,3584]{2,1,0:T(8,128)(2,1)S(1)} %collective-permute-done.4.refs_1_.refs_3_, f32[12,4,128]{2,1,0:T(4,128)S(1)} %shard_map.91.refs_2_), custom_call_target="tpu_custom_call" | custom-call | flops 1000 | bytes 1000 | tf_op jit(solution)/shard_map/pallas_call | solution.py:45
  81.0 4.1 %collective-permute-start.6 = (bf16[128,3584]{1,0:T(8,128)(2,1)}, bf16[128,3584]{1,0:T(8,128)(2,1)S(1)}, u32[]{:S(2)}, u32[]{:S(2)}) collective-permute-start(bf16[128,3584]{1,0:T(8,128)(2,1)} %shard_map.95), channel_id=1, source_target_pairs={{0,2},{1,767},{2,4},{3,1},{4,6},{5,3},{6,8},{7,5},{8,10},{9,7},{10... | collective-permute-start | bytes 2752520 | tf_op jit(solution)/shard_map/ppermute | solution.py:310
  85.1 13.9 %all_to_all.21.refs_0_ = f32[12,4,128]{2,1,0:T(4,128)S(1)} all-to-all(f32[12,4,128]{2,1,0:T(4,128)S(1)} %shard_map.91.refs_2_), channel_id=1, replica_groups=mesh['y'=8,'z'=12,'row'=8] {'z'}, dimensions={0} | all-to-all | bytes 49152 | tf_op jit(solution)/shard_map/all_to_all | solution.py:360
  99.1 9.2 %all_to_all.22.refs_0_ = f32[8,4,128]{2,1,0:T(4,128)S(1)} all-to-all(f32[8,4,128]{2,1,0:T(4,128)S(1)} %shard_map.92), channel_id=1, replica_groups=mesh['y'=8,'z'=12,'row'=8] {'row'}, dimensions={0} | all-to-all | bytes 32768 | tf_op jit(solution)/shard_map/all_to_all | solution.py:360
  108.2 0.6 shard_map.93
  108.9 0.0 collective-permute-done.5.refs_4_
  108.9 0.0 collective-permute-done.6.refs_5_
  108.9 5.7 %shard_map.96 = bf16[128,3584]{1,0:T(8,128)(2,1)} custom-call(f32[1,3584]{1,0:T(1,128)S(1)} %get-tuple-element.36.refs_1_.refs_0_, bf16[128,3584]{1,0:T(8,128)(2,1)} %refs_1_.3, bf16[128,3584]{1,0:T(8,128)(2,1)} %get-tuple-element.64.refs_2_, bf16[2,128,3584]{2,1,0:T(8,128)(2,1)S(1)} %collective-permute-done.4.refs_1_.refs_3_, ...), custom_call_target="tpu_custom_call" | custom-call | flops 1000 | bytes 1000 | tf_op jit(solution)/shard_map/pallas_call | solution.py:45
  (2 shorter events, 0.0 us)
Async XLA Ops:
  0.6 31.2 %collective-permute-start = (bf16[128,3584]{1,0:T(8,128)(2,1)}, bf16[128,3584]{1,0:T(8,128)(2,1)S(1)}, u32[]{:S(2)}, u32[]{:S(2)}) collective-permute-start(bf16[128,3584]{1,0:T(8,128)(2,1)} %refs_1_.3), channel_id=1, source_target_pairs={{2,0},{767,1},{4,2},{1,3},{6,4},{3,5},{8,6},{5,7},{10,8},{7,9},{12... | collective-permute-start | bytes 2752520 | tf_op jit(solution)/shard_map/ppermute | solution.py:310
  4.6 33.1 %copy-start = (s32[1,4]{1,0:T(1,128)S(1)}, s32[1,4]{1,0:T(1,128)}, u32[]{:S(2)}) copy-start(s32[1,4]{1,0:T(1,128)} %refs_0_.9) | copy-start | bytes 52
  8.1 29.6 %collective-permute-start.3 = (bf16[128,3584]{1,0:T(8,128)(2,1)S(1)}, bf16[128,3584]{1,0:T(8,128)(2,1)S(1)}, u32[]{:S(2)}, u32[]{:S(2)}) collective-permute-start(bf16[128,3584]{1,0:T(8,128)(2,1)S(1)} %get-tuple-element.38), channel_id=1, source_target_pairs={{0,1},{1,0},{2,3},{3,2},{4,5},{5,4},{6,7},{7,6},{8,9},{9,8},{10,11... | collective-permute-start | bytes 2752520 | tf_op jit(solution)/shard_map/ppermute | solution.py:310
  27.2 15.2 %collective-permute-start.2 = (bf16[128,3584]{1,0:T(8,128)(2,1)S(1)}, bf16[128,3584]{1,0:T(8,128)(2,1)S(1)}, u32[]{:S(2)}, u32[]{:S(2)}) collective-permute-start(bf16[128,3584]{1,0:T(8,128)(2,1)S(1)} %get-tuple-element.38), channel_id=1, source_target_pairs={{766,0},{3,1},{0,2},{5,3},{2,4},{7,5},{4,6},{9,7},{6,8},{11,9},{8,... | collective-permute-start | bytes 2752520 | tf_op jit(solution)/shard_map/ppermute | solution.py:310
  32.3 12.6 %collective-permute-start.1 = (bf16[128,3584]{1,0:T(8,128)(2,1)S(1)}, bf16[128,3584]{1,0:T(8,128)(2,1)S(1)}, u32[]{:S(2)}, u32[]{:S(2)}) collective-permute-start(bf16[128,3584]{1,0:T(8,128)(2,1)S(1)} %shard_map.85.refs_1_), channel_id=1, source_target_pairs={{0,1},{1,0},{2,3},{3,2},{4,5},{5,4},{6,7},{7,6},{8,9},{9,8},{10,11... | collective-permute-start | bytes 2752520 | tf_op jit(solution)/shard_map/ppermute | solution.py:310
  65.2 13.1 %collective-permute-start.4 = (bf16[2,128,3584]{2,1,0:T(8,128)(2,1)}, bf16[2,128,3584]{2,1,0:T(8,128)(2,1)S(1)}, u32[]{:S(2)}, u32[]{:S(2)}) collective-permute-start(bf16[2,128,3584]{2,1,0:T(8,128)(2,1)} %get-tuple-element.65), channel_id=1, source_target_pairs={{0,1},{1,0},{2,3},{3,2},{4,5},{5,4},{6,7},{7,6},{8,9},{9,8},{10,11... | collective-permute-start | bytes 5505032 | tf_op jit(solution)/shard_map/ppermute | solution.py:310
  67.8 10.4 %all-to-all-start.1 = ((f32[8,4,128]{2,1,0:T(4,128)}), f32[8,4,128]{2,1,0:T(4,128)S(1)}, u32[]{:S(2)}, u32[]{:S(2)}) async-start(f32[8,4,128]{2,1,0:T(4,128)} %shard_map.90.refs_11_), calls=%async_computation.1 | async-start | bytes 32768 | tf_op jit(solution)/shard_map/all_to_all | solution.py:360
  71.6 37.2 %collective-permute-start.5 = (bf16[128,3584]{1,0:T(8,128)(2,1)}, bf16[128,3584]{1,0:T(8,128)(2,1)S(1)}, u32[]{:S(2)}, u32[]{:S(2)}) collective-permute-start(bf16[128,3584]{1,0:T(8,128)(2,1)} %get-tuple-element.66), channel_id=1, source_target_pairs={{0,766},{1,3},{2,0},{3,5},{4,2},{5,7},{6,4},{7,9},{8,6},{9,11},{10... | collective-permute-start | bytes 2752520 | tf_op jit(solution)/shard_map/ppermute | solution.py:310
  81.0 27.8 %collective-permute-start.6 = (bf16[128,3584]{1,0:T(8,128)(2,1)}, bf16[128,3584]{1,0:T(8,128)(2,1)S(1)}, u32[]{:S(2)}, u32[]{:S(2)}) collective-permute-start(bf16[128,3584]{1,0:T(8,128)(2,1)} %shard_map.95), channel_id=1, source_target_pairs={{0,2},{1,767},{2,4},{3,1},{4,6},{5,3},{6,8},{7,5},{8,10},{9,7},{10... | collective-permute-start | bytes 2752520 | tf_op jit(solution)/shard_map/ppermute | solution.py:310

commit v3 on v2

--- a/solution.py
+++ b/solution.py
@@ -21,6 +21,7 @@
 HIDDEN = -1e30
 STEP = 16
 PARTS = 4
+TERM_FLOPS, ADD_FLOPS, GRAD_FLOPS = 3_000_000_000, 1_500_000_000, 3_000_000_000
 PART = ROWS // PARTS
 f32, bf16 = jnp.float32, jnp.bfloat16
 AXES = ("y", "z", "row")
@@ -34,7 +35,7 @@
     return pltpu.VMEM(shape, dtype)
 
 
-def call(kernel, out_shape, args, scratch=(), aliases=None, scalars=(), distant=(), after=()):
+def call(kernel, out_shape, args, scratch=(), aliases=None, scalars=(), distant=(), after=(), flops=1000):
     given = len(scalars) + len(args) + len(distant)
 
     def run(*refs):
@@ -49,7 +50,7 @@
         out_shape=out_shape,
         scratch_shapes=list(scratch),
         input_output_aliases=aliases or {},
-        cost_estimate=pl.CostEstimate(flops=1000, bytes_accessed=1000, transcendentals=0),
+        cost_estimate=pl.CostEstimate(flops=flops, bytes_accessed=1000, transcendentals=0),
         compiler_params=pltpu.CompilerParams(vmem_limit_bytes=15 * 2**20),
     )(*scalars, *args, *distant, *after)
 
@@ -142,40 +143,51 @@
     head_into(x_ref, gain_ref[...], out_ref)
 
 
-def fold(scores, dn_ref, top0_ref, total0_ref, acc0_ref):
+def fold(blocks, top0_ref, total0_ref):
     before = top0_ref[:, 0:1]
-    top = jnp.maximum(before, jnp.max(scores, axis=1, keepdims=True))
+    top = before
+    for scores in blocks:
+        top = jnp.maximum(top, jnp.max(scores, axis=1, keepdims=True))
     shrink = jnp.exp(before - top)
-    probs = jnp.exp(scores - top)
-    total = total0_ref[:, 0:1] * shrink + jnp.sum(probs, axis=1, keepdims=True)
-    probs = probs.astype(bf16)
-
-    def weighted(c):
-        term = jnp.dot(probs, dn_ref[:, c : c + CHUNK], preferred_element_type=f32)
-        return acc0_ref[:, c : c + CHUNK] * shrink + term
-
-    return top, total, weighted
-
-
-def step_kernel(distance, neg_ref, dn_ref, qn_ref, top0_ref, total0_ref, acc0_ref, s_ref, top_ref, total_ref, acc_ref):
-    scores = jnp.where(listed(neg_ref, distance), scores_of(qn_ref[...], dn_ref[...]), HIDDEN)
-    top, total, weighted = fold(scores, dn_ref, top0_ref, total0_ref, acc0_ref)
-    s_ref[...] = scores
+    total = total0_ref[:, 0:1] * shrink
+    probs = []
+    for scores in blocks:
+        prob = jnp.exp(scores - top)
+        total = total + jnp.sum(prob, axis=1, keepdims=True)
+        probs.append(prob.astype(bf16))
+    return top, total, shrink, probs
+
+
+def pair_kernel(
+    distances, neg_ref, swap_ref, far_ref, qn_ref, top0_ref, total0_ref, acc0_ref,
+    s_swap_ref, s_far_ref, top_ref, total_ref, acc_ref,
+):
+    for distance, dn_ref, s_ref in zip(distances, (swap_ref, far_ref), (s_swap_ref, s_far_ref)):
+        s_ref[...] = jnp.where(listed(neg_ref, distance), scores_of(qn_ref[...], dn_ref[...]), HIDDEN)
+    top, total, shrink, probs = fold((s_swap_ref[...], s_far_ref[...]), top0_ref, total0_ref)
     for c in range(0, WIDTH, CHUNK):
-        acc_ref[:, c : c + CHUNK] = weighted(c)
+        cols = slice(c, c + CHUNK)
+        term = jnp.dot(probs[0], swap_ref[:, cols], preferred_element_type=f32)
+        term = term + jnp.dot(probs[1], far_ref[:, cols], preferred_element_type=f32)
+        acc_ref[:, cols] = acc0_ref[:, cols] * shrink + term
     top_ref[...] = across(top)
     total_ref[...] = across(total)
 
 
+def score_kernel(distance, neg_ref, dn_ref, qn_ref, s_ref):
+    s_ref[...] = jnp.where(listed(neg_ref, distance), scores_of(qn_ref[...], dn_ref[...]), HIDDEN)
+
+
 def last_kernel(
-    distance, neg_ref, dn_ref, qn_ref, top0_ref, total0_ref, acc0_ref, picked_ref, s_own_ref, pos_hbm, q_hbm,
-    s_ref, lse_ref, gq_ref, hot_ref, part_ref, q_ref, pos_ref, gain_sum, sems,
+    distance, neg_ref, dn_ref, back_ref, s_back_ref, qn_ref, top0_ref, total0_ref, acc0_ref, picked_ref, s_own_ref,
+    pos_hbm, q_hbm,
+    s_ref, lse_ref, gq_ref, hot_ref, part_ref, q_ref, pos_ref, lines, sems,
 ):
     copies = [pltpu.make_async_copy(q_hbm, q_ref, sems.at[0]), pltpu.make_async_copy(pos_hbm, pos_ref, sems.at[1])]
     for copy in copies:
         copy.start()
     scores = jnp.where(listed(neg_ref, distance), scores_of(qn_ref[...], dn_ref[...]), HIDDEN)
-    top, total, weighted = fold(scores, dn_ref, top0_ref, total0_ref, acc0_ref)
+    top, total, shrink, (probs, back_probs) = fold((scores, s_back_ref[...]), top0_ref, total0_ref)
     lse = top + jnp.log(total)
     s_ref[...] = scores
     lse_ref[...] = across(lse)
@@ -185,25 +197,27 @@
     hot_ref[...] = onehot
     loss = jnp.sum(lse - jnp.sum(s_own_ref[...] * onehot, axis=1, keepdims=True))
     share = FACTOR / total
+    kept_share = shrink * share
+    squares = [
+        jnp.sum(jnp.square(q_ref[i : i + STEP, :].astype(f32)), axis=-1, keepdims=True) for i in range(0, ROWS, STEP)
+    ]
+    factor = lax.rsqrt(jnp.concatenate(squares, axis=0) / WIDTH + 1e-06)
     for c in range(0, WIDTH, CHUNK):
-        gq_ref[:, c : c + CHUNK] = weighted(c) * share - FACTOR * picked_ref[:, c : c + CHUNK].astype(f32)
-    for i in range(0, ROWS, STEP):
-        values = q_ref[i : i + STEP, :].astype(f32)
-        added = gq_ref[i : i + STEP, :] * (values * factor_of(values))
-        added = added[:8] + added[8:]
-        gain_sum[...] = added if i == 0 else gain_sum[...] + added
-    gain_part = 2.0 * jnp.sum(gain_sum[...], axis=0, keepdims=True)
-    share_rows = part_ref.shape[1]
-    for i in range(GAIN_ROWS):
-        line = gain_part[:, i * LANES : (i + 1) * LANES]
-        part_ref[i // share_rows, i % share_rows : i % share_rows + 1, :] = line
-    for i in range(GAIN_ROWS, SUM_ROWS):
-        part_ref[i // share_rows, i % share_rows : i % share_rows + 1, :] = jnp.full((1, LANES), loss, f32)
+        cols = slice(c, c + CHUNK)
+        term = jnp.dot(probs, dn_ref[:, cols], preferred_element_type=f32)
+        term = term + jnp.dot(back_probs, back_ref[:, cols], preferred_element_type=f32)
+        gq = acc0_ref[:, cols] * kept_share + term * share - FACTOR * picked_ref[:, cols].astype(f32)
+        gq_ref[:, cols] = gq
+        added = 2.0 * jnp.sum(gq * (q_ref[:, cols].astype(f32) * factor), axis=0, keepdims=True)
+        for i in range(0, CHUNK, LANES):
+            lines[(c + i) // LANES : (c + i) // LANES + 1, :] = added[:, i : i + LANES]
+    lines[GAIN_ROWS:, :] = jnp.full((SUM_ROWS - GAIN_ROWS, LANES), loss, f32)
+    part_ref[...] = jnp.broadcast_to(lines[...][None], part_ref.shape)
 
 
 def term_kernel(
     qn_ref, gain_ref, gq_ref, lse_ref, hot_ref, s_own_ref, s_swap_ref, s_relay_ref, s_far_ref, s_back_ref, q_hbm,
-    near_hbm, back_hbm, far_hbm, own_hbm, grad_hbm, q_ref, grad_ref, weight_ref, term_ref, sems, row_sems,
+    near_hbm, back_hbm, far_hbm, own_hbm, grad_hbm, q_ref, grad_ref, weight_ref, term_ref, scaled_ref, sems, row_sems,
 ):
     incoming = pltpu.make_async_copy(q_hbm, q_ref, sems.at[0])
     incoming.start()
@@ -224,11 +238,16 @@
         copy.start()
         outgoing.append(copy)
     incoming.wait()
-    gain = gain_ref[...]
+
+    def values_at(rows, cols):
+        return q_ref[rows, cols].astype(f32)
+
+    def cotangent_at(rows, cols):
+        return gq_ref[rows, cols]
+
     for part in range(PARTS):
         for i in range(part * PART, (part + 1) * PART, STEP):
-            rows = slice(i, i + STEP)
-            grad_ref[rows, :] = pull(q_ref[rows, :].astype(f32), gain, gq_ref[rows, :]).astype(bf16)
+            pull(values_at, cotangent_at, gain_ref, scaled_ref, grad_ref, slice(i, i + STEP))
         rows = pl.ds(part * PART, PART)
         copy = pltpu.make_async_copy(grad_ref.at[rows, :], grad_hbm.at[rows, :], row_sems.at[part])
         copy.start()
@@ -237,11 +256,21 @@
         copy.wait()
 
 
-def pull(values, gain, cotangent):
-    factor = factor_of(values)
-    scaled = gain * cotangent
-    inner = jnp.sum(values * scaled, axis=-1, keepdims=True) / WIDTH
-    return factor * scaled - values * (factor * factor * factor * inner)
+def pull(values_at, cotangent_at, gain_ref, scaled_ref, out_ref, rows):
+    square = jnp.zeros((STEP, CHUNK), f32)
+    inner = jnp.zeros((STEP, CHUNK), f32)
+    chunks = [slice(c, c + CHUNK) for c in range(0, WIDTH, CHUNK)]
+    for cols in chunks:
+        values = values_at(rows, cols)
+        scaled = gain_ref[:, cols] * cotangent_at(rows, cols)
+        scaled_ref[:, cols] = scaled
+        square = square + values * values
+        inner = inner + values * scaled
+    factor = lax.rsqrt(jnp.sum(square, axis=-1, keepdims=True) / WIDTH + 1e-06)
+    inner = factor * factor * factor * (jnp.sum(inner, axis=-1, keepdims=True) / WIDTH)
+    for cols in chunks:
+        grad = factor * scaled_ref[:, cols] - values_at(rows, cols) * inner
+        out_ref[rows, cols] = grad.astype(bf16)
 
 
 def by_parts(sources, target, buffers, out_ref, sems, work):
@@ -261,8 +290,7 @@
         for copy in incoming[part]:
             copy.wait()
         for i in range(part * PART, (part + 1) * PART, STEP):
-            rows = slice(i, i + STEP)
-            out_ref[rows, :] = work(*[buffers[k, rows, :].astype(f32) for k in range(len(sources))]).astype(bf16)
+            work(slice(i, i + STEP))
         rows = pl.ds(part * PART, PART)
         copy = pltpu.make_async_copy(out_ref.at[rows, :], target.at[rows, :], sems.at[len(sources), part])
         copy.start()
@@ -271,17 +299,27 @@
         copy.wait()
 
 
-def grad_doc_kernel(gain_ref, d_hbm, own_hbm, near_hbm, back_hbm, far_hbm, grad_hbm, buffers, out_ref, sems):
-    gain = gain_ref[...]
-
-    def work(values, own, near, back, far):
-        return pull(values, gain, FACTOR * (own + near + back + far))
+def grad_doc_kernel(gain_ref, d_hbm, own_hbm, near_hbm, back_hbm, far_hbm, grad_hbm, buffers, out_ref, scaled_ref, sems):
+    def at(k, rows, cols):
+        return buffers[k, rows, cols].astype(f32)
+
+    def cotangent_at(rows, cols):
+        return FACTOR * ((at(1, rows, cols) + at(2, rows, cols)) + (at(3, rows, cols) + at(4, rows, cols)))
+
+    def work(rows):
+        pull(functools.partial(at, 0), cotangent_at, gain_ref, scaled_ref, out_ref, rows)
 
     by_parts((d_hbm, own_hbm, near_hbm.at[1], back_hbm, far_hbm), grad_hbm, buffers, out_ref, sems, work)
 
 
 def add_kernel(far_hbm, near_hbm, sum_hbm, buffers, out_ref, sems):
-    by_parts((far_hbm, near_hbm.at[0]), sum_hbm, buffers, out_ref, sems, lambda far, near: far + near)
+    def work(rows):
+        for c in range(0, WIDTH, CHUNK):
+            cols = slice(c, c + CHUNK)
+            total = buffers[0, rows, cols].astype(f32) + buffers[1, rows, cols].astype(f32)
+            out_ref[rows, cols] = total.astype(bf16)
+
+    by_parts((far_hbm, near_hbm.at[0]), sum_hbm, buffers, out_ref, sems, work)
 
 
 def sum_kernel(in_ref, out_ref):
@@ -290,11 +328,9 @@
 
 
 def end_kernel(denom, in_ref, gain_ref, loss_ref):
-    rows = in_ref.shape[1]
-    total = in_ref[...] / denom
-    for i in range(GAIN_ROWS):
-        gain_ref[i : i + 1, :] = total[i // rows, i % rows : i % rows + 1, :]
-    loss_ref[...] = total[GAIN_ROWS // rows, GAIN_ROWS % rows : GAIN_ROWS % rows + 1, 0:1]
+    total = jnp.sum(in_ref[...], axis=0) / denom
+    gain_ref[...] = total[:GAIN_ROWS]
+    loss_ref[...] = total[GAIN_ROWS : GAIN_ROWS + 1, 0:1]
 
 
 def body(query_hidden, doc_hidden, gain, positives, neg_blocks):
@@ -330,30 +366,28 @@
     back = permute(dn, [(back_source[i], i) for i in devices])
     swap = permute(dn, swap_route)
 
-    def step(distance, docs, state):
-        return call(
-            functools.partial(step_kernel, distance),
-            [held(square, f32)] * 3 + [held(block, f32)],
-            (docs, qn, *map(kept, state)),
-            scalars=(neg_blocks,),
-            aliases={3: 1, 4: 2, 5: 3},
-        )
-
     far = call(head_kernel, held(block, bf16), (far, gain_line))
     relay = permute(far, swap_route)
-    s_swap, *state = step(1, swap, state)
-    s_far, *state = step(2, far, state)
-    s_back, *state = step(-2, back, state)
+    s_swap, s_far, *state = call(
+        functools.partial(pair_kernel, (1, 2)),
+        [held(square, f32)] * 4 + [held(block, f32)],
+        (swap, far, qn, *map(kept, state)),
+        scalars=(neg_blocks,),
+        aliases={4: 2, 5: 3, 6: 4},
+    )
+    s_back = call(
+        functools.partial(score_kernel, -2), held(square, f32), (back, qn), scalars=(neg_blocks,), after=(s_far,)
+    )
     sizes = [lax.axis_size(a) for a in AXES]
-    share = (SUM_ROWS // sizes[2], LANES)
+    share = (SUM_ROWS, LANES)
     s_relay, lse, gq, hot, part = call(
         functools.partial(last_kernel, -1),
-        [held(square, f32)] * 2 + [held(block, f32), held(square, f32), held((sizes[2], *share), f32)],
-        (relay, qn, *map(kept, state), picked, s_own),
+        [held(square, f32)] * 2 + [held(block, f32), held(square, f32), held((sizes[0], *share), f32)],
+        (relay, back, kept(s_back), qn, *map(kept, state), picked, s_own),
         scalars=(neg_blocks,),
         distant=(leave(positives), leave(query_hidden)),
-        scratch=[pltpu.VMEM(block, bf16), pltpu.VMEM((1, ROWS), jnp.int32), pltpu.VMEM((8, WIDTH), f32), dma((2,))],
-        aliases={5: 2},
+        scratch=[pltpu.VMEM(block, bf16), pltpu.VMEM((1, ROWS), jnp.int32), pltpu.VMEM(share, f32), dma((2,))],
+        aliases={7: 2},
     )
 
     def exchange(x, axis):
@@ -362,21 +396,19 @@
     def summed(x, axis):
         return call(sum_kernel, held((sizes[axis], *share), f32), (x,))
 
-    part = summed(exchange(part, 2), 0)
     t_near, t_back, t_far, t_own, grad_query = call(
         term_kernel,
         [distant_array((2, *block), bf16)] + [distant_array(block, bf16)] * 4,
         (qn, gain_line, kept(gq), kept(lse), kept(hot), s_own, kept(s_swap), kept(s_relay), kept(s_far), kept(s_back)),
         distant=(leave(query_hidden),),
-        after=(part,),
         scratch=[
             pltpu.VMEM(block, bf16), pltpu.VMEM(block, bf16), pltpu.VMEM((5 * ROWS, ROWS), bf16),
-            pltpu.VMEM((5, *block), bf16), dma((6,)), dma((PARTS,)),
+            pltpu.VMEM((5, *block), bf16), pltpu.VMEM((STEP, WIDTH), f32), dma((6,)), dma((PARTS,)),
         ],
+        flops=TERM_FLOPS,
     )
     near_term = permute(t_near, swap_route)
     back_term = permute(t_back, [(i, back_source[i]) for i in devices])
-
     part = summed(exchange(part, 0), 1)
     far_sum = call(
         add_kernel,
@@ -385,6 +417,7 @@
         distant=(leave(t_far), near_term),
         after=(part,),
         scratch=[pltpu.VMEM((2, *block), bf16), pltpu.VMEM(block, bf16), dma((3, PARTS))],
+        flops=ADD_FLOPS,
     )
     far_term = permute(far_sum, [(i, far_source[i]) for i in devices])
     part = summed(exchange(part, 1), 2)
@@ -394,7 +427,10 @@
         distant_array(block, bf16),
         (gain_line,),
         distant=(leave(doc_hidden), leave(t_own), near_term, back_term, far_term),
-        scratch=[pltpu.VMEM((5, *block), bf16), pltpu.VMEM(block, bf16), dma((6, PARTS))],
+        scratch=[
+            pltpu.VMEM((5, *block), bf16), pltpu.VMEM(block, bf16), pltpu.VMEM((STEP, WIDTH), f32), dma((6, PARTS))
+        ],
+        flops=GRAD_FLOPS,
     )
     grad_gain, mean_loss = call(
         functools.partial(end_kernel, float(ROWS * count)),

time: 115 us -> 114 us (level)
  blocking collectives: 35.6 us -> 30.5 us
  waiting for transfers between devices: 6.61 us -> 11.3 us
  Pallas kernels: 27.9 us -> 24.1 us
  starting transfers between devices: 43.7 us -> 46.4 us
    all_to_all x3 -> x2, blocking collectives: 35.6 us -> 30.5 us  [exchange(): return kept(lax.all_to_all(x, AXES[axis], 0, 0, tiled=True))]
    pallas_call x13 -> x11, Pallas kernels: 27.9 us -> 24.1 us  [call(): pl.pallas_call(run, in_specs=[in_smem] * len(scalars) + [in_vmem] * len(a...]
    ppermute x7, starting transfers between devices: 39.8 us -> 42.6 us  [permute(): return lax.ppermute(x, AXES, route)]
    ppermute x7, waiting for transfers between devices: 2.18 us -> 4.68 us  [permute(): return lax.ppermute(x, AXES, route)]
    all_to_all x1, waiting for transfers between devices: 4.43 us -> 6.59 us  [exchange(): return kept(lax.all_to_all(x, AXES[axis], 0, 0, tiled=True))]
  transfers between devices with their start and end apart: 8 -> 8, of which waited for: 2 -> 3; matrix products, arithmetic and copies ran while one was open for 0% -> 0% of each run, Pallas kernels for 13% -> 9%
where the time goes in v3:
time: 114 us; the launch traced here: 113 us
  starting transfers between devices  46.4 us (41%)
  blocking collectives  30.5 us (27%)
  Pallas kernels  24.1 us (21%)
  waiting for transfers between devices  11.3 us (10%)
    ppermute x7, starting transfers between devices, permute(): return lax.ppermute(x, AXES, route)  42.6 us
    all_to_all x2, blocking collectives, exchange(): return kept(lax.all_to_all(x, AXES[axis], 0, 0, tiled=True))  30.5 us
    pallas_call x11, Pallas kernels, call(): pl.pallas_call(run, in_specs=[in_smem] * len(scalars) + [in_vmem] * len(a...  24.1 us
    all_to_all x1, waiting for transfers between devices, exchange(): return kept(lax.all_to_all(x, AXES[axis], 0, 0, tiled=True))  6.59 us
    ppermute x7, waiting for transfers between devices, permute(): return lax.ppermute(x, AXES, route)  4.68 us
    all_to_all x1, starting transfers between devices, exchange(): return kept(lax.all_to_all(x, AXES[axis], 0, 0, tiled=True))  3.81 us
  transfers between devices with their start and end apart: 8, of which 3 were waited for; matrix products, arithmetic and copies ran while one was open for 0% of the time, Pallas kernels for 9%

profile of v3, /device:TPU:1, one launch (start us, length us, event | category | flops | bytes accessed | tf_op | source)
XLA Modules:
  0.0 113.0 jit_solution(13395092577072839018)
XLA Ops:
  0.6 4.0 %collective-permute-start = (bf16[128,3584]{1,0:T(8,128)(2,1)}, bf16[128,3584]{1,0:T(8,128)(2,1)S(1)}, u32[]{:S(2)}, u32[]{:S(2)}) collective-permute-start(bf16[128,3584]{1,0:T(8,128)(2,1)} %refs_1_.3), channel_id=1, source_target_pairs={{2,0},{767,1},{4,2},{1,3},{6,4},{3,5},{8,6},{5,7},{10,8},{7,9},{12... | collective-permute-start | bytes 2752520 | tf_op jit(solution)/shard_map/ppermute | solution.py:346
  4.6 0.0 copy-start
  4.6 3.5 %shard_map.84 = (bf16[128,3584]{1,0:T(8,128)(2,1)S(1)}, bf16[128,3584]{1,0:T(8,128)(2,1)S(1)}, f32[1,3584]{1,0:T(1,128)S(1)}, f32[128,128]{1,0:T(8,128)S(1)}, f3...) custom-call(bf16[128,3584]{1,0:T(8,128)(2,1)} %refs_10_.1, ...), custom_call_target="tpu_custom_call" | custom-call | flops 1000 | bytes 1000 | tf_op jit(solution)/shard_map/pallas_call | solution.py:46
  8.1 19.1 %collective-permute-start.3 = (bf16[128,3584]{1,0:T(8,128)(2,1)S(1)}, bf16[128,3584]{1,0:T(8,128)(2,1)S(1)}, u32[]{:S(2)}, u32[]{:S(2)}) collective-permute-start(bf16[128,3584]{1,0:T(8,128)(2,1)S(1)} %get-tuple-element.30), channel_id=1, source_target_pairs={{0,1},{1,0},{2,3},{3,2},{4,5},{5,4},{6,7},{7,6},{8,9},{9,8},{10,11... | collective-permute-start | bytes 2752520 | tf_op jit(solution)/shard_map/ppermute | solution.py:346
  27.2 2.5 %collective-permute-start.2 = (bf16[128,3584]{1,0:T(8,128)(2,1)S(1)}, bf16[128,3584]{1,0:T(8,128)(2,1)S(1)}, u32[]{:S(2)}, u32[]{:S(2)}) collective-permute-start(bf16[128,3584]{1,0:T(8,128)(2,1)S(1)} %get-tuple-element.30), channel_id=1, source_target_pairs={{766,0},{3,1},{0,2},{5,3},{2,4},{7,5},{4,6},{9,7},{6,8},{11,9},{8,... | collective-permute-start | bytes 2752520 | tf_op jit(solution)/shard_map/ppermute | solution.py:346
  29.7 2.2 %collective-permute-done.refs_0_ = bf16[128,3584]{1,0:T(8,128)(2,1)S(1)} collective-permute-done((bf16[128,3584]{1,0:T(8,128)(2,1)}, bf16[128,3584]{1,0:T(8,128)(2,1)S(1)}, u32[]{:S(2)}, u32[]{:S(2)}) %collective-permute-start) | collective-permute-done | bytes 917536 | tf_op jit(solution)/shard_map/ppermute | solution.py:346
  31.9 0.4 shard_map.85.refs_2_
  32.3 5.4 %collective-permute-start.1 = (bf16[128,3584]{1,0:T(8,128)(2,1)S(1)}, bf16[128,3584]{1,0:T(8,128)(2,1)S(1)}, u32[]{:S(2)}, u32[]{:S(2)}) collective-permute-start(bf16[128,3584]{1,0:T(8,128)(2,1)S(1)} %shard_map.85.refs_2_), channel_id=1, source_target_pairs={{0,1},{1,0},{2,3},{3,2},{4,5},{5,4},{6,7},{7,6},{8,9},{9,8},{10,11... | collective-permute-start | bytes 2752520 | tf_op jit(solution)/shard_map/ppermute | solution.py:346
  37.7 0.0 collective-permute-done.3.refs_1_
  37.7 0.0 copy-done
  37.7 2.2 %shard_map.86 = (f32[128,128]{1,0:T(8,128)S(1)}, f32[128,128]{1,0:T(8,128)S(1)}, f32[128,128]{1,0:T(8,128)S(1)}, f32[128,128]{1,0:T(8,128)S(1)}, f32[128,3584]{1,0:T(8,128)S(1)}) custom-call(s32[1,4]{1,0:T(1,128)S(1)} %copy-done, bf16[128,3584]{1,0:T(8,128)(2,1)S(1)} %collective-permute-done.3.refs_1_, ...), custom_call_target="tpu_custom_call", output_to_operand_aliasing={{2}: (4, {}), {3}: (5, {}), {4}: (6, {})} | custom-call | flops 1000 | bytes 1000 | tf_op jit(solution)/shard_map/pallas_call | solution.py:46
  39.9 2.5 %collective-permute-done.2.refs_1_.refs_2_ = bf16[128,3584]{1,0:T(8,128)(2,1)S(1)} collective-permute-done((bf16[128,3584]{1,0:T(8,128)(2,1)S(1)}, bf16[128,3584]{1,0:T(8,128)(2,1)S(1)}, u32[]{:S(2)}, u32[]{:S(2)}) %collective-permute-start.2) | collective-permute-done | bytes 917536 | tf_op jit(solution)/shard_map/ppermute | solution.py:346
  42.4 0.9 shard_map.87.refs_3_.refs_9_
  43.3 0.0 collective-permute-done.1.refs_1_
  43.3 4.9 %shard_map.88 = (f32[128,128]{1,0:T(8,128)S(1)}, f32[128,128]{1,0:T(8,128)S(1)}, f32[128,3584]{1,0:T(8,128)S(1)}, f32[128,128]{1,0:T(8,128)S(1)}, f32[8,32,128]{2,1,0:T(8,128)}) custom-call(s32[1,4]{1,0:T(1,128)S(1)} %copy-done, bf16[128,3584]{1,0:T(8,128)(2,1)S(1)} %collective-permute-done.1.refs_1_, ...), custom_call_target="tpu_custom_call", output_to_operand_aliasing={{2}: (7, {})} | custom-call | flops 1000 | bytes 1000 | tf_op jit(solution)/shard_map/pallas_call | solution.py:46
  48.2 3.0 %shard_map.92 = (bf16[2,128,3584]{2,1,0:T(8,128)(2,1)}, bf16[128,3584]{1,0:T(8,128)(2,1)}, bf16[128,3584]{1,0:T(8,128)(2,1)}, bf16[128,3584]{1,0:T(8,128)(2,1)}, bf16[128,3584]{1,0:T(8,128)(2,1)}) custom-call(bf16[128,3584]{1,0:T(8,128)(2,1)S(1)} %get-tuple-element.31.refs_3_.refs_2_.refs_4_.refs_0_, f32[1,3584]{1,0:T(1,128)S(1)} %get-tuple-element.29.refs_1_.refs_0_, ...), custom_call_target="tpu_custom_call" | custom-call | flops 3000000000 | bytes 1000 | tf_op jit(solution)/shard_map/pallas_call | solution.py:46
  51.2 7.5 %collective-permute-start.4 = (bf16[2,128,3584]{2,1,0:T(8,128)(2,1)}, bf16[2,128,3584]{2,1,0:T(8,128)(2,1)S(1)}, u32[]{:S(2)}, u32[]{:S(2)}) collective-permute-start(bf16[2,128,3584]{2,1,0:T(8,128)(2,1)} %get-tuple-element.51), channel_id=1, source_target_pairs={{0,1},{1,0},{2,3},{3,2},{4,5},{5,4},{6,7},{7,6},{8,9},{9,8},{10,11... | collective-permute-start | bytes 5505032 | tf_op jit(solution)/shard_map/ppermute | solution.py:346
  58.7 3.8 %all-to-all-start = ((f32[8,32,128]{2,1,0:T(8,128)}), f32[8,32,128]{2,1,0:T(8,128)S(1)}, u32[]{:S(2)}, u32[]{:S(2)}) async-start(f32[8,32,128]{2,1,0:T(8,128)} %get-tuple-element.41), calls=%async_computation | async-start | bytes 262144 | tf_op jit(solution)/shard_map/all_to_all | solution.py:394
  62.5 1.9 %collective-permute-start.5 = (bf16[128,3584]{1,0:T(8,128)(2,1)}, bf16[128,3584]{1,0:T(8,128)(2,1)S(1)}, u32[]{:S(2)}, u32[]{:S(2)}) collective-permute-start(bf16[128,3584]{1,0:T(8,128)(2,1)} %get-tuple-element.52), channel_id=1, source_target_pairs={{0,766},{1,3},{2,0},{3,5},{4,2},{5,7},{6,4},{7,9},{8,6},{9,11},{10... | collective-permute-start | bytes 2752520 | tf_op jit(solution)/shard_map/ppermute | solution.py:346
  64.5 6.6 %all-to-all-done.refs_0_ = f32[8,32,128]{2,1,0:T(8,128)S(1)} async-done(((f32[8,32,128]{2,1,0:T(8,128)}), f32[8,32,128]{2,1,0:T(8,128)S(1)}, u32[]{:S(2)}, u32[]{:S(2)}) %all-to-all-start) | async-done | bytes 131104 | tf_op jit(solution)/shard_map/all_to_all | solution.py:394
  71.1 0.0 collective-permute-done.4.refs_1_.refs_3_
  71.1 2.7 %shard_map.93 = bf16[128,3584]{1,0:T(8,128)(2,1)} custom-call(bf16[128,3584]{1,0:T(8,128)(2,1)} %get-tuple-element.53.refs_0_, bf16[2,128,3584]{2,1,0:T(8,128)(2,1)S(1)} %collective-permute-done.4.refs_1_.refs_3_, f32[12,32,128]{2,1,0:T(8,128)S(1)} %shard_map.89.refs_2_), custom_call_target="tpu_custom_call" | custom-call | flops 1500000000 | bytes 1000 | tf_op jit(solution)/shard_map/pallas_call | solution.py:46
  73.8 2.2 %collective-permute-start.6 = (bf16[128,3584]{1,0:T(8,128)(2,1)}, bf16[128,3584]{1,0:T(8,128)(2,1)S(1)}, u32[]{:S(2)}, u32[]{:S(2)}) collective-permute-start(bf16[128,3584]{1,0:T(8,128)(2,1)} %shard_map.93), channel_id=1, source_target_pairs={{0,2},{1,767},{2,4},{3,1},{4,6},{5,3},{6,8},{7,5},{8,10},{9,7},{10... | collective-permute-start | bytes 2752520 | tf_op jit(solution)/shard_map/ppermute | solution.py:346
  76.1 19.6 %all_to_all.15.refs_0_ = f32[12,32,128]{2,1,0:T(8,128)S(1)} all-to-all(f32[12,32,128]{2,1,0:T(8,128)S(1)} %shard_map.89.refs_2_), channel_id=1, replica_groups=mesh['y'=8,'z'=12,'row'=8] {'z'}, dimensions={0} | all-to-all | bytes 393216 | tf_op jit(solution)/shard_map/all_to_all | solution.py:394
  95.7 10.9 %all_to_all.16.refs_0_ = f32[8,32,128]{2,1,0:T(8,128)S(1)} all-to-all(f32[8,32,128]{2,1,0:T(8,128)S(1)} %shard_map.90), channel_id=1, replica_groups=mesh['y'=8,'z'=12,'row'=8] {'row'}, dimensions={0} | all-to-all | bytes 262144 | tf_op jit(solution)/shard_map/all_to_all | solution.py:394
  106.6 0.6 shard_map.91
  107.2 0.0 collective-permute-done.5.refs_4_
  107.2 0.0 collective-permute-done.6.refs_5_
  107.2 5.8 %shard_map.94 = bf16[128,3584]{1,0:T(8,128)(2,1)} custom-call(f32[1,3584]{1,0:T(1,128)S(1)} %get-tuple-element.29.refs_1_.refs_0_, bf16[128,3584]{1,0:T(8,128)(2,1)} %refs_1_.3, bf16[128,3584]{1,0:T(8,128)(2,1)} %get-tuple-element.50.refs_2_, bf16[2,128,3584]{2,1,0:T(8,128)(2,1)S(1)} %collective-permute-done.4.refs_1_.refs_3_, ...), custom_call_target="tpu_custom_call" | custom-call | flops 3000000000 | bytes 1000 | tf_op jit(solution)/shard_map/pallas_call | solution.py:46
  (2 shorter events, 0.0 us)
Async XLA Ops:
  0.6 31.2 %collective-permute-start = (bf16[128,3584]{1,0:T(8,128)(2,1)}, bf16[128,3584]{1,0:T(8,128)(2,1)S(1)}, u32[]{:S(2)}, u32[]{:S(2)}) collective-permute-start(bf16[128,3584]{1,0:T(8,128)(2,1)} %refs_1_.3), channel_id=1, source_target_pairs={{2,0},{767,1},{4,2},{1,3},{6,4},{3,5},{8,6},{5,7},{10,8},{7,9},{12... | collective-permute-start | bytes 2752520 | tf_op jit(solution)/shard_map/ppermute | solution.py:346
  4.6 33.1 %copy-start = (s32[1,4]{1,0:T(1,128)S(1)}, s32[1,4]{1,0:T(1,128)}, u32[]{:S(2)}) copy-start(s32[1,4]{1,0:T(1,128)} %refs_0_.7) | copy-start | bytes 52
  8.1 29.6 %collective-permute-start.3 = (bf16[128,3584]{1,0:T(8,128)(2,1)S(1)}, bf16[128,3584]{1,0:T(8,128)(2,1)S(1)}, u32[]{:S(2)}, u32[]{:S(2)}) collective-permute-start(bf16[128,3584]{1,0:T(8,128)(2,1)S(1)} %get-tuple-element.30), channel_id=1, source_target_pairs={{0,1},{1,0},{2,3},{3,2},{4,5},{5,4},{6,7},{7,6},{8,9},{9,8},{10,11... | collective-permute-start | bytes 2752520 | tf_op jit(solution)/shard_map/ppermute | solution.py:346
  27.2 15.1 %collective-permute-start.2 = (bf16[128,3584]{1,0:T(8,128)(2,1)S(1)}, bf16[128,3584]{1,0:T(8,128)(2,1)S(1)}, u32[]{:S(2)}, u32[]{:S(2)}) collective-permute-start(bf16[128,3584]{1,0:T(8,128)(2,1)S(1)} %get-tuple-element.30), channel_id=1, source_target_pairs={{766,0},{3,1},{0,2},{5,3},{2,4},{7,5},{4,6},{9,7},{6,8},{11,9},{8,... | collective-permute-start | bytes 2752520 | tf_op jit(solution)/shard_map/ppermute | solution.py:346
  32.3 11.0 %collective-permute-start.1 = (bf16[128,3584]{1,0:T(8,128)(2,1)S(1)}, bf16[128,3584]{1,0:T(8,128)(2,1)S(1)}, u32[]{:S(2)}, u32[]{:S(2)}) collective-permute-start(bf16[128,3584]{1,0:T(8,128)(2,1)S(1)} %shard_map.85.refs_2_), channel_id=1, source_target_pairs={{0,1},{1,0},{2,3},{3,2},{4,5},{5,4},{6,7},{7,6},{8,9},{9,8},{10,11... | collective-permute-start | bytes 2752520 | tf_op jit(solution)/shard_map/ppermute | solution.py:346
  51.2 19.9 %collective-permute-start.4 = (bf16[2,128,3584]{2,1,0:T(8,128)(2,1)}, bf16[2,128,3584]{2,1,0:T(8,128)(2,1)S(1)}, u32[]{:S(2)}, u32[]{:S(2)}) collective-permute-start(bf16[2,128,3584]{2,1,0:T(8,128)(2,1)} %get-tuple-element.51), channel_id=1, source_target_pairs={{0,1},{1,0},{2,3},{3,2},{4,5},{5,4},{6,7},{7,6},{8,9},{9,8},{10,11... | collective-permute-start | bytes 5505032 | tf_op jit(solution)/shard_map/ppermute | solution.py:346
  58.7 12.3 %all-to-all-start = ((f32[8,32,128]{2,1,0:T(8,128)}), f32[8,32,128]{2,1,0:T(8,128)S(1)}, u32[]{:S(2)}, u32[]{:S(2)}) async-start(f32[8,32,128]{2,1,0:T(8,128)} %get-tuple-element.41), calls=%async_computation | async-start | bytes 262144 | tf_op jit(solution)/shard_map/all_to_all | solution.py:394
  62.5 44.7 %collective-permute-start.5 = (bf16[128,3584]{1,0:T(8,128)(2,1)}, bf16[128,3584]{1,0:T(8,128)(2,1)S(1)}, u32[]{:S(2)}, u32[]{:S(2)}) collective-permute-start(bf16[128,3584]{1,0:T(8,128)(2,1)} %get-tuple-element.52), channel_id=1, source_target_pairs={{0,766},{1,3},{2,0},{3,5},{4,2},{5,7},{6,4},{7,9},{8,6},{9,11},{10... | collective-permute-start | bytes 2752520 | tf_op jit(solution)/shard_map/ppermute | solution.py:346
  73.8 33.4 %collective-permute-start.6 = (bf16[128,3584]{1,0:T(8,128)(2,1)}, bf16[128,3584]{1,0:T(8,128)(2,1)S(1)}, u32[]{:S(2)}, u32[]{:S(2)}) collective-permute-start(bf16[128,3584]{1,0:T(8,128)(2,1)} %shard_map.93), channel_id=1, source_target_pairs={{0,2},{1,767},{2,4},{3,1},{4,6},{5,3},{6,8},{7,5},{8,10},{9,7},{10... | collective-permute-start | bytes 2752520 | tf_op jit(solution)/shard_map/ppermute | solution.py:346

commit v4 on v3

--- a/solution.py
+++ b/solution.py
@@ -21,7 +21,6 @@
 HIDDEN = -1e30
 STEP = 16
 PARTS = 4
-TERM_FLOPS, ADD_FLOPS, GRAD_FLOPS = 3_000_000_000, 1_500_000_000, 3_000_000_000
 PART = ROWS // PARTS
 f32, bf16 = jnp.float32, jnp.bfloat16
 AXES = ("y", "z", "row")
@@ -35,7 +34,7 @@
     return pltpu.VMEM(shape, dtype)
 
 
-def call(kernel, out_shape, args, scratch=(), aliases=None, scalars=(), distant=(), after=(), flops=1000):
+def call(kernel, out_shape, args, scratch=(), aliases=None, scalars=(), distant=(), after=()):
     given = len(scalars) + len(args) + len(distant)
 
     def run(*refs):
@@ -50,7 +49,7 @@
         out_shape=out_shape,
         scratch_shapes=list(scratch),
         input_output_aliases=aliases or {},
-        cost_estimate=pl.CostEstimate(flops=flops, bytes_accessed=1000, transcendentals=0),
+        cost_estimate=pl.CostEstimate(flops=1000, bytes_accessed=1000, transcendentals=0),
         compiler_params=pltpu.CompilerParams(vmem_limit_bytes=15 * 2**20),
     )(*scalars, *args, *distant, *after)
 
@@ -181,7 +180,7 @@
 def last_kernel(
     distance, neg_ref, dn_ref, back_ref, s_back_ref, qn_ref, top0_ref, total0_ref, acc0_ref, picked_ref, s_own_ref,
     pos_hbm, q_hbm,
-    s_ref, lse_ref, gq_ref, hot_ref, part_ref, q_ref, pos_ref, lines, sems,
+    s_ref, lse_ref, gq_ref, hot_ref, lines, q_ref, pos_ref, sems,
 ):
     copies = [pltpu.make_async_copy(q_hbm, q_ref, sems.at[0]), pltpu.make_async_copy(pos_hbm, pos_ref, sems.at[1])]
     for copy in copies:
@@ -212,31 +211,44 @@
         for i in range(0, CHUNK, LANES):
             lines[(c + i) // LANES : (c + i) // LANES + 1, :] = added[:, i : i + LANES]
     lines[GAIN_ROWS:, :] = jnp.full((SUM_ROWS - GAIN_ROWS, LANES), loss, f32)
-    part_ref[...] = jnp.broadcast_to(lines[...][None], part_ref.shape)
-
-
-def term_kernel(
-    qn_ref, gain_ref, gq_ref, lse_ref, hot_ref, s_own_ref, s_swap_ref, s_relay_ref, s_far_ref, s_back_ref, q_hbm,
-    near_hbm, back_hbm, far_hbm, own_hbm, grad_hbm, q_ref, grad_ref, weight_ref, term_ref, scaled_ref, sems, row_sems,
+
+
+def turned(block_ref, lse_ref, hot_ref=None):
+    weight = jnp.exp(block_ref[...] - lse_ref[...])
+    if hot_ref is not None:
+        weight = weight - hot_ref[...]
+    return weight.T.astype(bf16)
+
+
+def near_kernel(qn_ref, lse_ref, s_relay_ref, s_swap_ref, lines_ref, near_ref, part_ref):
+    weights = [turned(block_ref, lse_ref) for block_ref in (s_relay_ref, s_swap_ref)]
+    for c in range(0, WIDTH, CHUNK):
+        cols = slice(c, c + CHUNK)
+        for k, weight in enumerate(weights):
+            near_ref[k, :, cols] = jnp.dot(weight, qn_ref[:, cols], preferred_element_type=f32).astype(bf16)
+    part_ref[...] = jnp.broadcast_to(lines_ref[...][None], part_ref.shape)
+
+
+def far_kernel(qn_ref, lse_ref, s_back_ref, s_far_ref, near_ref, back_ref, far_ref):
+    w_back, w_far = (turned(block_ref, lse_ref) for block_ref in (s_back_ref, s_far_ref))
+    for c in range(0, WIDTH, CHUNK):
+        cols = slice(c, c + CHUNK)
+        queries = qn_ref[:, cols]
+        back_ref[:, cols] = jnp.dot(w_back, queries, preferred_element_type=f32).astype(bf16)
+        term = jnp.dot(w_far, queries, preferred_element_type=f32)
+        far_ref[:, cols] = (term + near_ref[0, :, cols].astype(f32)).astype(bf16)
+
+
+def home_kernel(
+    qn_ref, lse_ref, s_own_ref, hot_ref, near_ref, gain_ref, gq_ref, q_hbm, own_ref, grad_hbm, q_ref, grad_ref, scaled_ref, sems
 ):
-    incoming = pltpu.make_async_copy(q_hbm, q_ref, sems.at[0])
+    incoming = pltpu.make_async_copy(q_hbm, q_ref, sems.at[PARTS])
     incoming.start()
-    blocks = (s_relay_ref, s_swap_ref, s_back_ref, s_far_ref, s_own_ref)
-    for k, block_ref in enumerate(blocks):
-        weight = jnp.exp(block_ref[...] - lse_ref[...])
-        if block_ref is s_own_ref:
-            weight = weight - hot_ref[...]
-        weight_ref[k * ROWS : (k + 1) * ROWS, :] = weight.T.astype(bf16)
-    targets = (near_hbm.at[0], near_hbm.at[1], back_hbm, far_hbm, own_hbm)
-    outgoing = []
-    for k, target in enumerate(targets):
-        weight = weight_ref[k * ROWS : (k + 1) * ROWS, :]
-        for c in range(0, WIDTH, CHUNK):
-            cols = slice(c, c + CHUNK)
-            term_ref[k, :, cols] = jnp.dot(weight, qn_ref[:, cols], preferred_element_type=f32).astype(bf16)
-        copy = pltpu.make_async_copy(term_ref.at[k], target, sems.at[k + 1])
-        copy.start()
-        outgoing.append(copy)
+    weight = turned(s_own_ref, lse_ref, hot_ref)
+    for c in range(0, WIDTH, CHUNK):
+        cols = slice(c, c + CHUNK)
+        term = jnp.dot(weight, qn_ref[:, cols], preferred_element_type=f32)
+        own_ref[:, cols] = term + near_ref[1, :, cols].astype(f32)
     incoming.wait()
 
     def values_at(rows, cols):
@@ -245,11 +257,39 @@
     def cotangent_at(rows, cols):
         return gq_ref[rows, cols]
 
+    send_parts(lambda rows: pull(values_at, cotangent_at, gain_ref, scaled_ref, grad_ref, rows), grad_ref, grad_hbm, sems)
+
+
+def grad_doc_kernel(gain_ref, own_ref, back_ref, far_ref, d_hbm, grad_hbm, d_ref, grad_ref, scaled_ref, sems, in_sems):
+    incoming = []
+    for part in range(PARTS):
+        rows = pl.ds(part * PART, PART)
+        copy = pltpu.make_async_copy(d_hbm.at[rows, :], d_ref.at[rows, :], in_sems.at[part])
+        copy.start()
+        incoming.append(copy)
+
+    def values_at(rows, cols):
+        return d_ref[rows, cols].astype(f32)
+
+    def cotangent_at(rows, cols):
+        total = own_ref[rows, cols] + back_ref[rows, cols].astype(f32) + far_ref[rows, cols].astype(f32)
+        return FACTOR * total
+
+    def work(rows):
+        if rows.start % PART == 0:
+            incoming[rows.start // PART].wait()
+        pull(values_at, cotangent_at, gain_ref, scaled_ref, grad_ref, rows)
+
+    send_parts(work, grad_ref, grad_hbm, sems)
+
+
+def send_parts(work, out_ref, target, sems):
+    outgoing = []
     for part in range(PARTS):
         for i in range(part * PART, (part + 1) * PART, STEP):
-            pull(values_at, cotangent_at, gain_ref, scaled_ref, grad_ref, slice(i, i + STEP))
+            work(slice(i, i + STEP))
         rows = pl.ds(part * PART, PART)
-        copy = pltpu.make_async_copy(grad_ref.at[rows, :], grad_hbm.at[rows, :], row_sems.at[part])
+        copy = pltpu.make_async_copy(out_ref.at[rows, :], target.at[rows, :], sems.at[part])
         copy.start()
         outgoing.append(copy)
     for copy in outgoing:
@@ -271,55 +311,6 @@
     for cols in chunks:
         grad = factor * scaled_ref[:, cols] - values_at(rows, cols) * inner
         out_ref[rows, cols] = grad.astype(bf16)
-
-
-def by_parts(sources, target, buffers, out_ref, sems, work):
-    def copies(part):
-        rows = pl.ds(part * PART, PART)
-        return [
-            pltpu.make_async_copy(source.at[rows, :], buffers.at[k, rows, :], sems.at[k, part])
-            for k, source in enumerate(sources)
-        ]
-
-    incoming = [copies(part) for part in range(PARTS)]
-    for part in incoming:
-        for copy in part:
-            copy.start()
-    outgoing = []
-    for part in range(PARTS):
-        for copy in incoming[part]:
-            copy.wait()
-        for i in range(part * PART, (part + 1) * PART, STEP):
-            work(slice(i, i + STEP))
-        rows = pl.ds(part * PART, PART)
-        copy = pltpu.make_async_copy(out_ref.at[rows, :], target.at[rows, :], sems.at[len(sources), part])
-        copy.start()
-        outgoing.append(copy)
-    for copy in outgoing:
-        copy.wait()
-
-
-def grad_doc_kernel(gain_ref, d_hbm, own_hbm, near_hbm, back_hbm, far_hbm, grad_hbm, buffers, out_ref, scaled_ref, sems):
-    def at(k, rows, cols):
-        return buffers[k, rows, cols].astype(f32)
-
-    def cotangent_at(rows, cols):
-        return FACTOR * ((at(1, rows, cols) + at(2, rows, cols)) + (at(3, rows, cols) + at(4, rows, cols)))
-
-    def work(rows):
-        pull(functools.partial(at, 0), cotangent_at, gain_ref, scaled_ref, out_ref, rows)
-
-    by_parts((d_hbm, own_hbm, near_hbm.at[1], back_hbm, far_hbm), grad_hbm, buffers, out_ref, sems, work)
-
-
-def add_kernel(far_hbm, near_hbm, sum_hbm, buffers, out_ref, sems):
-    def work(rows):
-        for c in range(0, WIDTH, CHUNK):
-            cols = slice(c, c + CHUNK)
-            total = buffers[0, rows, cols].astype(f32) + buffers[1, rows, cols].astype(f32)
-            out_ref[rows, cols] = total.astype(bf16)
-
-    by_parts((far_hbm, near_hbm.at[0]), sum_hbm, buffers, out_ref, sems, work)
 
 
 def sum_kernel(in_ref, out_ref):
@@ -380,15 +371,16 @@
     )
     sizes = [lax.axis_size(a) for a in AXES]
     share = (SUM_ROWS, LANES)
-    s_relay, lse, gq, hot, part = call(
+    s_relay, lse, gq, hot, lines = call(
         functools.partial(last_kernel, -1),
-        [held(square, f32)] * 2 + [held(block, f32), held(square, f32), held((sizes[0], *share), f32)],
+        [held(square, f32)] * 2 + [held(block, f32), held(square, f32), held(share, f32)],
         (relay, back, kept(s_back), qn, *map(kept, state), picked, s_own),
         scalars=(neg_blocks,),
         distant=(leave(positives), leave(query_hidden)),
-        scratch=[pltpu.VMEM(block, bf16), pltpu.VMEM((1, ROWS), jnp.int32), pltpu.VMEM(share, f32), dma((2,))],
+        scratch=[pltpu.VMEM(block, bf16), pltpu.VMEM((1, ROWS), jnp.int32), dma((2,))],
         aliases={7: 2},
     )
+    lse = kept(lse)
 
     def exchange(x, axis):
         return kept(lax.all_to_all(x, AXES[axis], 0, 0, tiled=True))
@@ -396,41 +388,35 @@
     def summed(x, axis):
         return call(sum_kernel, held((sizes[axis], *share), f32), (x,))
 
-    t_near, t_back, t_far, t_own, grad_query = call(
-        term_kernel,
-        [distant_array((2, *block), bf16)] + [distant_array(block, bf16)] * 4,
-        (qn, gain_line, kept(gq), kept(lse), kept(hot), s_own, kept(s_swap), kept(s_relay), kept(s_far), kept(s_back)),
+    t_near, part = call(
+        near_kernel,
+        [held((2, *block), bf16), held((sizes[1], *share), f32)],
+        (qn, lse, kept(s_relay), kept(s_swap), kept(lines)),
+    )
+    near_term = permute(t_near, swap_route)
+    part = summed(exchange(part, 1), 0)
+    t_back, far_sum = call(
+        far_kernel, [held(block, bf16)] * 2, (qn, lse, kept(s_back), kept(s_far), near_term), after=(part,)
+    )
+    far_term = permute(far_sum, [(i, far_source[i]) for i in devices])
+    back_term = permute(t_back, [(i, back_source[i]) for i in devices])
+    t_own, grad_query = call(
+        home_kernel,
+        [held(block, f32), distant_array(block, bf16)],
+        (qn, lse, s_own, kept(hot), near_term, gain_line, kept(gq)),
         distant=(leave(query_hidden),),
-        scratch=[
-            pltpu.VMEM(block, bf16), pltpu.VMEM(block, bf16), pltpu.VMEM((5 * ROWS, ROWS), bf16),
-            pltpu.VMEM((5, *block), bf16), pltpu.VMEM((STEP, WIDTH), f32), dma((6,)), dma((PARTS,)),
-        ],
-        flops=TERM_FLOPS,
-    )
-    near_term = permute(t_near, swap_route)
-    back_term = permute(t_back, [(i, back_source[i]) for i in devices])
-    part = summed(exchange(part, 0), 1)
-    far_sum = call(
-        add_kernel,
-        distant_array(block, bf16),
-        (),
-        distant=(leave(t_far), near_term),
-        after=(part,),
-        scratch=[pltpu.VMEM((2, *block), bf16), pltpu.VMEM(block, bf16), dma((3, PARTS))],
-        flops=ADD_FLOPS,
-    )
-    far_term = permute(far_sum, [(i, far_source[i]) for i in devices])
-    part = summed(exchange(part, 1), 2)
+        scratch=[pltpu.VMEM(block, bf16), pltpu.VMEM(block, bf16), pltpu.VMEM((STEP, WIDTH), f32), dma((PARTS + 1,))],
+    )
+    part = summed(exchange(part, 0), 2)
     part = exchange(part, 2)
     grad_doc = call(
         grad_doc_kernel,
         distant_array(block, bf16),
-        (gain_line,),
-        distant=(leave(doc_hidden), leave(t_own), near_term, back_term, far_term),
+        (gain_line, kept(t_own), back_term, far_term),
+        distant=(leave(doc_hidden),),
         scratch=[
-            pltpu.VMEM((5, *block), bf16), pltpu.VMEM(block, bf16), pltpu.VMEM((STEP, WIDTH), f32), dma((6, PARTS))
+            pltpu.VMEM(block, bf16), pltpu.VMEM(block, bf16), pltpu.VMEM((STEP, WIDTH), f32), dma((PARTS,)), dma((PARTS,))
         ],
-        flops=GRAD_FLOPS,
     )
     grad_gain, mean_loss = call(
         functools.partial(end_kernel, float(ROWS * count)),

time: 114 us -> 119 us (1.044)
  blocking collectives: 30.5 us -> 44.7 us
  waiting for transfers between devices: 11.3 us -> 4.68 us
  Pallas kernels: 24.1 us -> 18.6 us
  starting transfers between devices: 46.4 us -> 49.1 us
    all_to_all x2 -> x3, blocking collectives: 30.5 us -> 44.7 us  [exchange(): return kept(lax.all_to_all(x, AXES[axis], 0, 0, tiled=True))]
    all_to_all x1 -> x0, waiting for transfers between devices: 6.59 us -> none  [exchange(): return kept(lax.all_to_all(x, AXES[axis], 0, 0, tiled=True))]
    ppermute x7, starting transfers between devices: 42.6 us -> 49.1 us  [permute(): return lax.ppermute(x, AXES, route)]
    pallas_call x11 -> x12, Pallas kernels: 24.1 us -> 18.6 us  [call(): pl.pallas_call(run, in_specs=[in_smem] * len(scalars) + [in_vmem] * len(a...]
    all_to_all x1 -> x0, starting transfers between devices: 3.81 us -> none  [exchange(): return kept(lax.all_to_all(x, AXES[axis], 0, 0, tiled=True))]
  transfers between devices with their start and end apart: 8 -> 7, of which waited for: 3 -> 2; matrix products, arithmetic and copies ran while one was open for 0% -> 0% of each run, Pallas kernels for 9% -> 9%
where the time goes in v4:
time: 119 us; the launch traced here: 118 us
  starting transfers between devices  49.1 us (41%)
  blocking collectives  44.7 us (38%)
  Pallas kernels  18.6 us (16%)
  waiting for transfers between devices  4.68 us (4%)
    ppermute x7, starting transfers between devices, permute(): return lax.ppermute(x, AXES, route)  49.1 us
    all_to_all x3, blocking collectives, exchange(): return kept(lax.all_to_all(x, AXES[axis], 0, 0, tiled=True))  44.7 us
    pallas_call x12, Pallas kernels, call(): pl.pallas_call(run, in_specs=[in_smem] * len(scalars) + [in_vmem] * len(a...  18.6 us
    ppermute x7, waiting for transfers between devices, permute(): return lax.ppermute(x, AXES, route)  4.68 us
  transfers between devices with their start and end apart: 7, of which 2 were waited for; matrix products, arithmetic and copies ran while one was open for 0% of the time, Pallas kernels for 9%

profile of v4, /device:TPU:1, one launch (start us, length us, event | category | flops | bytes accessed | tf_op | source)
XLA Modules:
  0.0 118.0 jit_solution(6135460371093218461)
XLA Ops:
  0.6 4.0 %collective-permute-start = (bf16[128,3584]{1,0:T(8,128)(2,1)}, bf16[128,3584]{1,0:T(8,128)(2,1)S(1)}, u32[]{:S(2)}, u32[]{:S(2)}) collective-permute-start(bf16[128,3584]{1,0:T(8,128)(2,1)} %refs_4_.1), channel_id=1, source_target_pairs={{2,0},{767,1},{4,2},{1,3},{6,4},{3,5},{8,6},{5,7},{10,8},{7,9},{12... | collective-permute-start | bytes 2752520 | tf_op jit(solution)/shard_map/ppermute | solution.py:337
  4.6 0.0 copy-start
  4.6 3.5 %shard_map.84 = (bf16[128,3584]{1,0:T(8,128)(2,1)S(1)}, bf16[128,3584]{1,0:T(8,128)(2,1)S(1)}, f32[1,3584]{1,0:T(1,128)S(1)}, f32[128,128]{1,0:T(8,128)S(1)}, f3...) custom-call(bf16[128,3584]{1,0:T(8,128)(2,1)} %refs_7_.1, ...), custom_call_target="tpu_custom_call" | custom-call | flops 1000 | bytes 1000 | tf_op jit(solution)/shard_map/pallas_call | solution.py:45
  8.1 19.1 %collective-permute-start.3 = (bf16[128,3584]{1,0:T(8,128)(2,1)S(1)}, bf16[128,3584]{1,0:T(8,128)(2,1)S(1)}, u32[]{:S(2)}, u32[]{:S(2)}) collective-permute-start(bf16[128,3584]{1,0:T(8,128)(2,1)S(1)} %get-tuple-element.32), channel_id=1, source_target_pairs={{0,1},{1,0},{2,3},{3,2},{4,5},{5,4},{6,7},{7,6},{8,9},{9,8},{10,11... | collective-permute-start | bytes 2752520 | tf_op jit(solution)/shard_map/ppermute | solution.py:337
  27.2 2.5 %collective-permute-start.2 = (bf16[128,3584]{1,0:T(8,128)(2,1)S(1)}, bf16[128,3584]{1,0:T(8,128)(2,1)S(1)}, u32[]{:S(2)}, u32[]{:S(2)}) collective-permute-start(bf16[128,3584]{1,0:T(8,128)(2,1)S(1)} %get-tuple-element.32), channel_id=1, source_target_pairs={{766,0},{3,1},{0,2},{5,3},{2,4},{7,5},{4,6},{9,7},{6,8},{11,9},{8,... | collective-permute-start | bytes 2752520 | tf_op jit(solution)/shard_map/ppermute | solution.py:337
  29.7 2.2 %collective-permute-done.refs_0_ = bf16[128,3584]{1,0:T(8,128)(2,1)S(1)} collective-permute-done((bf16[128,3584]{1,0:T(8,128)(2,1)}, bf16[128,3584]{1,0:T(8,128)(2,1)S(1)}, u32[]{:S(2)}, u32[]{:S(2)}) %collective-permute-start) | collective-permute-done | bytes 917536 | tf_op jit(solution)/shard_map/ppermute | solution.py:337
  31.9 0.4 shard_map.85.refs_2_
  32.3 5.4 %collective-permute-start.1 = (bf16[128,3584]{1,0:T(8,128)(2,1)S(1)}, bf16[128,3584]{1,0:T(8,128)(2,1)S(1)}, u32[]{:S(2)}, u32[]{:S(2)}) collective-permute-start(bf16[128,3584]{1,0:T(8,128)(2,1)S(1)} %shard_map.85.refs_2_), channel_id=1, source_target_pairs={{0,1},{1,0},{2,3},{3,2},{4,5},{5,4},{6,7},{7,6},{8,9},{9,8},{10,11... | collective-permute-start | bytes 2752520 | tf_op jit(solution)/shard_map/ppermute | solution.py:337
  37.7 0.0 collective-permute-done.3.refs_1_
  37.7 0.0 copy-done
  37.7 2.2 %shard_map.86 = (f32[128,128]{1,0:T(8,128)S(1)}, f32[128,128]{1,0:T(8,128)S(1)}, f32[128,128]{1,0:T(8,128)S(1)}, f32[128,128]{1,0:T(8,128)S(1)}, f32[128,3584]{1,0:T(8,128)S(1)}) custom-call(s32[1,4]{1,0:T(1,128)S(1)} %copy-done, bf16[128,3584]{1,0:T(8,128)(2,1)S(1)} %collective-permute-done.3.refs_1_, ...), custom_call_target="tpu_custom_call", output_to_operand_aliasing={{2}: (4, {}), {3}: (5, {}), {4}: (6, {})} | custom-call | flops 1000 | bytes 1000 | tf_op jit(solution)/shard_map/pallas_call | solution.py:45
  39.9 2.5 %collective-permute-done.2.refs_1_.refs_2_ = bf16[128,3584]{1,0:T(8,128)(2,1)S(1)} collective-permute-done((bf16[128,3584]{1,0:T(8,128)(2,1)S(1)}, bf16[128,3584]{1,0:T(8,128)(2,1)S(1)}, u32[]{:S(2)}, u32[]{:S(2)}) %collective-permute-start.2) | collective-permute-done | bytes 917536 | tf_op jit(solution)/shard_map/ppermute | solution.py:337
  42.4 0.9 shard_map.87.refs_3_.refs_2_
  43.3 0.0 collective-permute-done.1.refs_1_
  43.3 4.2 %shard_map.88 = (f32[128,128]{1,0:T(8,128)S(1)}, f32[128,128]{1,0:T(8,128)S(1)}, f32[128,3584]{1,0:T(8,128)S(1)}, f32[128,128]{1,0:T(8,128)S(1)}, f32[32,128]{1,0:T(8,128)S(1)}) custom-call(s32[1,4]{1,0:T(1,128)S(1)} %copy-done, bf16[128,3584]{1,0:T(8,128)(2,1)S(1)} %collective-permute-done.1.refs_1_, ...), custom_call_target="tpu_custom_call", output_to_operand_aliasing={{2}: (7, {})} | custom-call | flops 1000 | bytes 1000 | tf_op jit(solution)/shard_map/pallas_call | solution.py:45
  47.6 0.7 shard_map.89
  48.3 7.5 %collective-permute-start.4 = (bf16[2,128,3584]{2,1,0:T(8,128)(2,1)S(1)}, bf16[2,128,3584]{2,1,0:T(8,128)(2,1)S(1)}, u32[]{:S(2)}, u32[]{:S(2)}) collective-permute-start(bf16[2,128,3584]{2,1,0:T(8,128)(2,1)S(1)} %get-tuple-element.50), channel_id=1, source_target_pairs={{0,1},{1,0},{2,3},{3,2},{4,5},{5,4},{6,7},{7,6},{8,9},{9,8},{10,11... | collective-permute-start | bytes 5505032 | tf_op jit(solution)/shard_map/ppermute | solution.py:337
  55.7 15.6 %all_to_all.15.refs_0_ = f32[12,32,128]{2,1,0:T(8,128)S(1)} all-to-all(f32[12,32,128]{2,1,0:T(8,128)S(1)} %get-tuple-element.46), channel_id=1, replica_groups=mesh['y'=8,'z'=12,'row'=8] {'z'}, dimensions={0} | all-to-all | bytes 393216 | tf_op jit(solution)/shard_map/all_to_all | solution.py:386
  71.4 0.0 collective-permute-done.4.refs_4_
  71.4 0.7 shard_map.94
  72.1 1.9 %collective-permute-start.5 = (bf16[128,3584]{1,0:T(8,128)(2,1)S(1)}, bf16[128,3584]{1,0:T(8,128)(2,1)S(1)}, u32[]{:S(2)}, u32[]{:S(2)}) collective-permute-start(bf16[128,3584]{1,0:T(8,128)(2,1)S(1)} %get-tuple-element.54), channel_id=1, source_target_pairs={{0,766},{1,3},{2,0},{3,5},{4,2},{5,7},{6,4},{7,9},{8,6},{9,11},{10... | collective-permute-start | bytes 2752520 | tf_op jit(solution)/shard_map/ppermute | solution.py:337
  74.1 8.8 %collective-permute-start.6 = (bf16[128,3584]{1,0:T(8,128)(2,1)S(1)}, bf16[128,3584]{1,0:T(8,128)(2,1)S(1)}, u32[]{:S(2)}, u32[]{:S(2)}) collective-permute-start(bf16[128,3584]{1,0:T(8,128)(2,1)S(1)} %get-tuple-element.55), channel_id=1, source_target_pairs={{0,2},{1,767},{2,4},{3,1},{4,6},{5,3},{6,8},{7,5},{8,10},{9,7},{10... | collective-permute-start | bytes 2752520 | tf_op jit(solution)/shard_map/ppermute | solution.py:337
  82.9 11.8 %all_to_all.16.refs_0_ = f32[8,32,128]{2,1,0:T(8,128)S(1)} all-to-all(f32[8,32,128]{2,1,0:T(8,128)S(1)} %shard_map.90.refs_5_), channel_id=1, replica_groups=mesh['y'=8,'z'=12,'row'=8] {'y'}, dimensions={0} | all-to-all | bytes 262144 | tf_op jit(solution)/shard_map/all_to_all | solution.py:386
  94.7 17.3 %all_to_all.17.refs_0_ = f32[8,32,128]{2,1,0:T(8,128)S(1)} all-to-all(f32[8,32,128]{2,1,0:T(8,128)S(1)} %shard_map.91), channel_id=1, replica_groups=mesh['y'=8,'z'=12,'row'=8] {'row'}, dimensions={0} | all-to-all | bytes 262144 | tf_op jit(solution)/shard_map/all_to_all | solution.py:386
  112.0 0.6 shard_map.92
  112.6 2.6 %shard_map.93 = (f32[128,3584]{1,0:T(8,128)S(1)}, bf16[128,3584]{1,0:T(8,128)(2,1)}) custom-call(bf16[128,3584]{1,0:T(8,128)(2,1)S(1)} %get-tuple-element.30.refs_3_.refs_2_.refs_4_.refs_0_, f32[128,128]{1,0:T(8,128)S(1)} %get-tuple-element.42.refs_1_, f32[128,128]{1,0:T(8,128)S(1)} %get-tuple-element.41.refs_9_.refs_2_, ...), custom_call_target="tpu_custom_call" | custom-call | flops 1000 | bytes 1000 | tf_op jit(solution)/shard_map/pallas_call | solution.py:45
  115.1 0.0 collective-permute-done.5.refs_2_
  115.2 0.0 collective-permute-done.6.refs_3_
  115.2 2.8 %shard_map.95 = bf16[128,3584]{1,0:T(8,128)(2,1)} custom-call(f32[1,3584]{1,0:T(1,128)S(1)} %get-tuple-element.31.refs_1_.refs_5_.refs_0_, f32[128,3584]{1,0:T(8,128)S(1)} %get-tuple-element.53.refs_1_, bf16[128,3584]{1,0:T(8,128)(2,1)S(1)} %collective-permute-done.5.refs_2_, bf16[128,3584]{1,0:T(8,128)(2,1)S(1)} %collective-permute-done.6.refs_3_, ...), custom_call_target="tpu_custom_call" | custom-call | flops 1000 | bytes 1000 | tf_op jit(solution)/shard_map/pallas_call | solution.py:45
  (2 shorter events, 0.0 us)
Async XLA Ops:
  0.6 31.2 %collective-permute-start = (bf16[128,3584]{1,0:T(8,128)(2,1)}, bf16[128,3584]{1,0:T(8,128)(2,1)S(1)}, u32[]{:S(2)}, u32[]{:S(2)}) collective-permute-start(bf16[128,3584]{1,0:T(8,128)(2,1)} %refs_4_.1), channel_id=1, source_target_pairs={{2,0},{767,1},{4,2},{1,3},{6,4},{3,5},{8,6},{5,7},{10,8},{7,9},{12... | collective-permute-start | bytes 2752520 | tf_op jit(solution)/shard_map/ppermute | solution.py:337
  4.6 33.1 %copy-start = (s32[1,4]{1,0:T(1,128)S(1)}, s32[1,4]{1,0:T(1,128)}, u32[]{:S(2)}) copy-start(s32[1,4]{1,0:T(1,128)} %refs_0_.7) | copy-start | bytes 52
  8.1 29.6 %collective-permute-start.3 = (bf16[128,3584]{1,0:T(8,128)(2,1)S(1)}, bf16[128,3584]{1,0:T(8,128)(2,1)S(1)}, u32[]{:S(2)}, u32[]{:S(2)}) collective-permute-start(bf16[128,3584]{1,0:T(8,128)(2,1)S(1)} %get-tuple-element.32), channel_id=1, source_target_pairs={{0,1},{1,0},{2,3},{3,2},{4,5},{5,4},{6,7},{7,6},{8,9},{9,8},{10,11... | collective-permute-start | bytes 2752520 | tf_op jit(solution)/shard_map/ppermute | solution.py:337
  27.2 15.2 %collective-permute-start.2 = (bf16[128,3584]{1,0:T(8,128)(2,1)S(1)}, bf16[128,3584]{1,0:T(8,128)(2,1)S(1)}, u32[]{:S(2)}, u32[]{:S(2)}) collective-permute-start(bf16[128,3584]{1,0:T(8,128)(2,1)S(1)} %get-tuple-element.32), channel_id=1, source_target_pairs={{766,0},{3,1},{0,2},{5,3},{2,4},{7,5},{4,6},{9,7},{6,8},{11,9},{8,... | collective-permute-start | bytes 2752520 | tf_op jit(solution)/shard_map/ppermute | solution.py:337
  32.3 11.0 %collective-permute-start.1 = (bf16[128,3584]{1,0:T(8,128)(2,1)S(1)}, bf16[128,3584]{1,0:T(8,128)(2,1)S(1)}, u32[]{:S(2)}, u32[]{:S(2)}) collective-permute-start(bf16[128,3584]{1,0:T(8,128)(2,1)S(1)} %shard_map.85.refs_2_), channel_id=1, source_target_pairs={{0,1},{1,0},{2,3},{3,2},{4,5},{5,4},{6,7},{7,6},{8,9},{9,8},{10,11... | collective-permute-start | bytes 2752520 | tf_op jit(solution)/shard_map/ppermute | solution.py:337
  48.3 23.2 %collective-permute-start.4 = (bf16[2,128,3584]{2,1,0:T(8,128)(2,1)S(1)}, bf16[2,128,3584]{2,1,0:T(8,128)(2,1)S(1)}, u32[]{:S(2)}, u32[]{:S(2)}) collective-permute-start(bf16[2,128,3584]{2,1,0:T(8,128)(2,1)S(1)} %get-tuple-element.50), channel_id=1, source_target_pairs={{0,1},{1,0},{2,3},{3,2},{4,5},{5,4},{6,7},{7,6},{8,9},{9,8},{10,11... | collective-permute-start | bytes 5505032 | tf_op jit(solution)/shard_map/ppermute | solution.py:337
  72.1 43.0 %collective-permute-start.5 = (bf16[128,3584]{1,0:T(8,128)(2,1)S(1)}, bf16[128,3584]{1,0:T(8,128)(2,1)S(1)}, u32[]{:S(2)}, u32[]{:S(2)}) collective-permute-start(bf16[128,3584]{1,0:T(8,128)(2,1)S(1)} %get-tuple-element.54), channel_id=1, source_target_pairs={{0,766},{1,3},{2,0},{3,5},{4,2},{5,7},{6,4},{7,9},{8,6},{9,11},{10... | collective-permute-start | bytes 2752520 | tf_op jit(solution)/shard_map/ppermute | solution.py:337
  74.1 41.1 %collective-permute-start.6 = (bf16[128,3584]{1,0:T(8,128)(2,1)S(1)}, bf16[128,3584]{1,0:T(8,128)(2,1)S(1)}, u32[]{:S(2)}, u32[]{:S(2)}) collective-permute-start(bf16[128,3584]{1,0:T(8,128)(2,1)S(1)} %get-tuple-element.55), channel_id=1, source_target_pairs={{0,2},{1,767},{2,4},{3,1},{4,6},{5,3},{6,8},{7,5},{8,10},{9,7},{10... | collective-permute-start | bytes 2752520 | tf_op jit(solution)/shard_map/ppermute | solution.py:337

commit v5 on v4

--- a/solution.py
+++ b/solution.py
@@ -74,8 +74,8 @@
     return lax.rsqrt(jnp.mean(values * values, axis=-1, keepdims=True) + 1e-06)
 
 
-def head_into(hidden_ref, gain, out_ref):
-    for i in range(0, ROWS, STEP):
+def head_into(hidden_ref, gain, out_ref, first=0, rows=ROWS):
+    for i in range(first, first + rows, STEP):
         values = hidden_ref[i : i + STEP, :].astype(f32)
         out_ref[i : i + STEP, :] = (values * factor_of(values) * gain).astype(bf16)
 
@@ -112,18 +112,22 @@
     qn_ref, dn_ref, gain_ref, s_ref, top_ref, total_ref, acc_ref, picked_ref,
     q_ref, d_ref, line_ref, pos_ref, sems,
 ):
-    pairs = ((d_hbm, d_ref), (gain_hbm, line_ref), (q_hbm, q_ref), (pos_hbm, pos_ref))
-    copies = [pltpu.make_async_copy(src, dst, sems.at[i]) for i, (src, dst) in enumerate(pairs)]
+    copies = [pltpu.make_async_copy(gain_hbm, line_ref, sems.at[2 * PARTS])]
+    for k, (src, dst) in enumerate(((d_hbm, d_ref), (q_hbm, q_ref))):
+        for part in range(PARTS):
+            rows = pl.ds(part * PART, PART)
+            copies.append(pltpu.make_async_copy(src.at[rows, :], dst.at[rows, :], sems.at[k * PARTS + part]))
+    copies.append(pltpu.make_async_copy(pos_hbm, pos_ref, sems.at[2 * PARTS + 1]))
     for copy in copies:
         copy.start()
     copies[0].wait()
-    copies[1].wait()
     gain = jnp.concatenate([line_ref[i : i + 1, :] for i in range(GAIN_ROWS)], axis=1)
     gain_ref[...] = gain
-    head_into(d_ref, gain, dn_ref)
-    copies[2].wait()
-    copies[3].wait()
-    head_into(q_ref, gain, qn_ref)
+    for k, (hidden_ref, out_ref) in enumerate(((d_ref, dn_ref), (q_ref, qn_ref))):
+        for part in range(PARTS):
+            copies[1 + k * PARTS + part].wait()
+            head_into(hidden_ref, gain, out_ref, part * PART, PART)
+    copies[-1].wait()
     scores = scores_of(qn_ref[...], dn_ref[...])
     top = jnp.max(scores, axis=1, keepdims=True)
     probs = jnp.exp(scores - top)
@@ -220,22 +224,22 @@
     return weight.T.astype(bf16)
 
 
-def near_kernel(qn_ref, lse_ref, s_relay_ref, s_swap_ref, lines_ref, near_ref, part_ref):
-    weights = [turned(block_ref, lse_ref) for block_ref in (s_relay_ref, s_swap_ref)]
-    for c in range(0, WIDTH, CHUNK):
-        cols = slice(c, c + CHUNK)
-        for k, weight in enumerate(weights):
-            near_ref[k, :, cols] = jnp.dot(weight, qn_ref[:, cols], preferred_element_type=f32).astype(bf16)
-    part_ref[...] = jnp.broadcast_to(lines_ref[...][None], part_ref.shape)
-
-
-def far_kernel(qn_ref, lse_ref, s_back_ref, s_far_ref, near_ref, back_ref, far_ref):
-    w_back, w_far = (turned(block_ref, lse_ref) for block_ref in (s_back_ref, s_far_ref))
+def near_kernel(qn_ref, lse_ref, s_relay_ref, s_swap_ref, s_back_ref, lines_ref, near_ref, back_ref, part_ref):
+    w_relay, w_swap, w_back = (turned(block_ref, lse_ref) for block_ref in (s_relay_ref, s_swap_ref, s_back_ref))
     for c in range(0, WIDTH, CHUNK):
         cols = slice(c, c + CHUNK)
         queries = qn_ref[:, cols]
+        near_ref[0, :, cols] = jnp.dot(w_relay, queries, preferred_element_type=f32).astype(bf16)
+        near_ref[1, :, cols] = jnp.dot(w_swap, queries, preferred_element_type=f32).astype(bf16)
         back_ref[:, cols] = jnp.dot(w_back, queries, preferred_element_type=f32).astype(bf16)
-        term = jnp.dot(w_far, queries, preferred_element_type=f32)
+    part_ref[...] = jnp.broadcast_to(lines_ref[...][None], part_ref.shape)
+
+
+def far_kernel(qn_ref, lse_ref, s_far_ref, near_ref, far_ref):
+    weight = turned(s_far_ref, lse_ref)
+    for c in range(0, WIDTH, CHUNK):
+        cols = slice(c, c + CHUNK)
+        term = jnp.dot(weight, qn_ref[:, cols], preferred_element_type=f32)
         far_ref[:, cols] = (term + near_ref[0, :, cols].astype(f32)).astype(bf16)
 
 
@@ -350,7 +354,7 @@
         distant=(leave(query_hidden), leave(doc_hidden), leave(gain), leave(positives)),
         scratch=[
             pltpu.VMEM(block, bf16), pltpu.VMEM(block, bf16), pltpu.VMEM((GAIN_ROWS, LANES), f32),
-            pltpu.VMEM((1, ROWS), jnp.int32), dma((4,)),
+            pltpu.VMEM((1, ROWS), jnp.int32), dma((2 * PARTS + 2,)),
         ],
     )
     qn, gain_line, picked, s_own = kept(qn), kept(gain_line), kept(picked), kept(s_own)
@@ -385,21 +389,19 @@
     def exchange(x, axis):
         return kept(lax.all_to_all(x, AXES[axis], 0, 0, tiled=True))
 
-    def summed(x, axis):
-        return call(sum_kernel, held((sizes[axis], *share), f32), (x,))
-
-    t_near, part = call(
+    def summed(x, axis, after=()):
+        return call(sum_kernel, held((sizes[axis], *share), f32), (x,), after=after)
+
+    t_near, t_back, part = call(
         near_kernel,
-        [held((2, *block), bf16), held((sizes[1], *share), f32)],
-        (qn, lse, kept(s_relay), kept(s_swap), kept(lines)),
+        [held((2, *block), bf16), held(block, bf16), held((sizes[0], *share), f32)],
+        (qn, lse, kept(s_relay), kept(s_swap), kept(s_back), kept(lines)),
     )
     near_term = permute(t_near, swap_route)
-    part = summed(exchange(part, 1), 0)
-    t_back, far_sum = call(
-        far_kernel, [held(block, bf16)] * 2, (qn, lse, kept(s_back), kept(s_far), near_term), after=(part,)
-    )
+    back_term = permute(t_back, [(i, back_source[i]) for i in devices])
+    part = summed(exchange(part, 0), 1, after=(back_term,))
+    far_sum = call(far_kernel, held(block, bf16), (qn, lse, kept(s_far), near_term), after=(part,))
     far_term = permute(far_sum, [(i, far_source[i]) for i in devices])
-    back_term = permute(t_back, [(i, back_source[i]) for i in devices])
     t_own, grad_query = call(
         home_kernel,
         [held(block, f32), distant_array(block, bf16)],
@@ -407,7 +409,7 @@
         distant=(leave(query_hidden),),
         scratch=[pltpu.VMEM(block, bf16), pltpu.VMEM(block, bf16), pltpu.VMEM((STEP, WIDTH), f32), dma((PARTS + 1,))],
     )
-    part = summed(exchange(part, 0), 2)
+    part = summed(exchange(part, 1), 2)
     part = exchange(part, 2)
     grad_doc = call(
         grad_doc_kernel,

time: 119 us -> 112 us (0.941)
  starting transfers between devices: 49.1 us -> 42.3 us
  blocking collectives: 44.7 us -> 38.5 us
  waiting for transfers between devices: 4.68 us -> 10.7 us
    ppermute x7, starting transfers between devices: 49.1 us -> 42.3 us  [permute(): return lax.ppermute(x, AXES, route)]
    all_to_all x3, blocking collectives: 44.7 us -> 38.5 us  [exchange(): return kept(lax.all_to_all(x, AXES[axis], 0, 0, tiled=True))]
    ppermute x7, waiting for transfers between devices: 4.68 us -> 10.7 us  [permute(): return lax.ppermute(x, AXES, route)]
  transfers between devices with their start and end apart: 7 -> 7, of which waited for: 2 -> 3; matrix products, arithmetic and copies ran while one was open for 0% -> 0% of each run, Pallas kernels for 9% -> 10%
where the time goes in v5:
time: 112 us; the launch traced here: 111 us
  starting transfers between devices  42.3 us (38%)
  blocking collectives  38.5 us (34%)
  Pallas kernels  19.1 us (17%)
  waiting for transfers between devices  10.7 us (10%)
    ppermute x7, starting transfers between devices, permute(): return lax.ppermute(x, AXES, route)  42.3 us
    all_to_all x3, blocking collectives, exchange(): return kept(lax.all_to_all(x, AXES[axis], 0, 0, tiled=True))  38.5 us
    pallas_call x12, Pallas kernels, call(): pl.pallas_call(run, in_specs=[in_smem] * len(scalars) + [in_vmem] * len(a...  19.1 us
    ppermute x7, waiting for transfers between devices, permute(): return lax.ppermute(x, AXES, route)  10.7 us
  transfers between devices with their start and end apart: 7, of which 3 were waited for; matrix products, arithmetic and copies ran while one was open for 0% of the time, Pallas kernels for 10%

profile of v5, /device:TPU:1, one launch (start us, length us, event | category | flops | bytes accessed | tf_op | source)
XLA Modules:
  0.0 111.4 jit_solution(13402439195395860337)
XLA Ops:
  0.6 4.0 %collective-permute-start = (bf16[128,3584]{1,0:T(8,128)(2,1)}, bf16[128,3584]{1,0:T(8,128)(2,1)S(1)}, u32[]{:S(2)}, u32[]{:S(2)}) collective-permute-start(bf16[128,3584]{1,0:T(8,128)(2,1)} %refs_4_.1), channel_id=1, source_target_pairs={{2,0},{767,1},{4,2},{1,3},{6,4},{3,5},{8,6},{5,7},{10,8},{7,9},{12... | collective-permute-start | bytes 2752520 | tf_op jit(solution)/shard_map/ppermute | solution.py:341
  4.6 0.0 copy-start
  4.6 3.9 %shard_map.84 = (bf16[128,3584]{1,0:T(8,128)(2,1)S(1)}, bf16[128,3584]{1,0:T(8,128)(2,1)S(1)}, f32[1,3584]{1,0:T(1,128)S(1)}, f32[128,128]{1,0:T(8,128)S(1)}, f3...) custom-call(bf16[128,3584]{1,0:T(8,128)(2,1)} %refs_7_.1, ...), custom_call_target="tpu_custom_call" | custom-call | flops 1000 | bytes 1000 | tf_op jit(solution)/shard_map/pallas_call | solution.py:45
  8.5 19.1 %collective-permute-start.3 = (bf16[128,3584]{1,0:T(8,128)(2,1)S(1)}, bf16[128,3584]{1,0:T(8,128)(2,1)S(1)}, u32[]{:S(2)}, u32[]{:S(2)}) collective-permute-start(bf16[128,3584]{1,0:T(8,128)(2,1)S(1)} %get-tuple-element.31), channel_id=1, source_target_pairs={{0,1},{1,0},{2,3},{3,2},{4,5},{5,4},{6,7},{7,6},{8,9},{9,8},{10,11... | collective-permute-start | bytes 2752520 | tf_op jit(solution)/shard_map/ppermute | solution.py:341
  27.7 2.5 %collective-permute-start.2 = (bf16[128,3584]{1,0:T(8,128)(2,1)S(1)}, bf16[128,3584]{1,0:T(8,128)(2,1)S(1)}, u32[]{:S(2)}, u32[]{:S(2)}) collective-permute-start(bf16[128,3584]{1,0:T(8,128)(2,1)S(1)} %get-tuple-element.31), channel_id=1, source_target_pairs={{766,0},{3,1},{0,2},{5,3},{2,4},{7,5},{4,6},{9,7},{6,8},{11,9},{8,... | collective-permute-start | bytes 2752520 | tf_op jit(solution)/shard_map/ppermute | solution.py:341
  30.2 1.7 %collective-permute-done.refs_0_ = bf16[128,3584]{1,0:T(8,128)(2,1)S(1)} collective-permute-done((bf16[128,3584]{1,0:T(8,128)(2,1)}, bf16[128,3584]{1,0:T(8,128)(2,1)S(1)}, u32[]{:S(2)}, u32[]{:S(2)}) %collective-permute-start) | collective-permute-done | bytes 917536 | tf_op jit(solution)/shard_map/ppermute | solution.py:341
  31.9 0.4 shard_map.85.refs_2_
  32.3 4.9 %collective-permute-start.1 = (bf16[128,3584]{1,0:T(8,128)(2,1)S(1)}, bf16[128,3584]{1,0:T(8,128)(2,1)S(1)}, u32[]{:S(2)}, u32[]{:S(2)}) collective-permute-start(bf16[128,3584]{1,0:T(8,128)(2,1)S(1)} %shard_map.85.refs_2_), channel_id=1, source_target_pairs={{0,1},{1,0},{2,3},{3,2},{4,5},{5,4},{6,7},{7,6},{8,9},{9,8},{10,11... | collective-permute-start | bytes 2752520 | tf_op jit(solution)/shard_map/ppermute | solution.py:341
  37.2 0.0 collective-permute-done.3.refs_1_
  37.2 0.0 copy-done
  37.2 2.2 %shard_map.86 = (f32[128,128]{1,0:T(8,128)S(1)}, f32[128,128]{1,0:T(8,128)S(1)}, f32[128,128]{1,0:T(8,128)S(1)}, f32[128,128]{1,0:T(8,128)S(1)}, f32[128,3584]{1,0:T(8,128)S(1)}) custom-call(s32[1,4]{1,0:T(1,128)S(1)} %copy-done, bf16[128,3584]{1,0:T(8,128)(2,1)S(1)} %collective-permute-done.3.refs_1_, ...), custom_call_target="tpu_custom_call", output_to_operand_aliasing={{2}: (4, {}), {3}: (5, {}), {4}: (6, {})} | custom-call | flops 1000 | bytes 1000 | tf_op jit(solution)/shard_map/pallas_call | solution.py:45
  39.4 3.0 %collective-permute-done.2.refs_1_.refs_2_ = bf16[128,3584]{1,0:T(8,128)(2,1)S(1)} collective-permute-done((bf16[128,3584]{1,0:T(8,128)(2,1)S(1)}, bf16[128,3584]{1,0:T(8,128)(2,1)S(1)}, u32[]{:S(2)}, u32[]{:S(2)}) %collective-permute-start.2) | collective-permute-done | bytes 917536 | tf_op jit(solution)/shard_map/ppermute | solution.py:341
  42.4 0.9 shard_map.87.refs_3_.refs_4_
  43.3 0.0 collective-permute-done.1.refs_1_
  43.3 4.2 %shard_map.88 = (f32[128,128]{1,0:T(8,128)S(1)}, f32[128,128]{1,0:T(8,128)S(1)}, f32[128,3584]{1,0:T(8,128)S(1)}, f32[128,128]{1,0:T(8,128)S(1)}, f32[32,128]{1,0:T(8,128)S(1)}) custom-call(s32[1,4]{1,0:T(1,128)S(1)} %copy-done, bf16[128,3584]{1,0:T(8,128)(2,1)S(1)} %collective-permute-done.1.refs_1_, ...), custom_call_target="tpu_custom_call", output_to_operand_aliasing={{2}: (7, {})} | custom-call | flops 1000 | bytes 1000 | tf_op jit(solution)/shard_map/pallas_call | solution.py:45
  47.6 0.9 shard_map.89
  48.5 8.0 %collective-permute-start.5 = (bf16[2,128,3584]{2,1,0:T(8,128)(2,1)S(1)}, bf16[2,128,3584]{2,1,0:T(8,128)(2,1)S(1)}, u32[]{:S(2)}, u32[]{:S(2)}) collective-permute-start(bf16[2,128,3584]{2,1,0:T(8,128)(2,1)S(1)} %get-tuple-element.50), channel_id=1, source_target_pairs={{0,1},{1,0},{2,3},{3,2},{4,5},{5,4},{6,7},{7,6},{8,9},{9,8},{10,11... | collective-permute-start | bytes 5505032 | tf_op jit(solution)/shard_map/ppermute | solution.py:341
  56.5 1.9 %collective-permute-start.4 = (bf16[128,3584]{1,0:T(8,128)(2,1)S(1)}, bf16[128,3584]{1,0:T(8,128)(2,1)S(1)}, u32[]{:S(2)}, u32[]{:S(2)}) collective-permute-start(bf16[128,3584]{1,0:T(8,128)(2,1)S(1)} %get-tuple-element.46), channel_id=1, source_target_pairs={{0,766},{1,3},{2,0},{3,5},{4,2},{5,7},{6,4},{7,9},{8,6},{9,11},{10... | collective-permute-start | bytes 2752520 | tf_op jit(solution)/shard_map/ppermute | solution.py:341
  58.4 11.6 %all_to_all.15.refs_0_ = f32[8,32,128]{2,1,0:T(8,128)S(1)} all-to-all(f32[8,32,128]{2,1,0:T(8,128)S(1)} %get-tuple-element.45), channel_id=1, replica_groups=mesh['y'=8,'z'=12,'row'=8] {'y'}, dimensions={0} | all-to-all | bytes 262144 | tf_op jit(solution)/shard_map/all_to_all | solution.py:390
  70.0 6.0 %collective-permute-done.4.refs_1_.refs_2_ = bf16[128,3584]{1,0:T(8,128)(2,1)S(1)} collective-permute-done((bf16[128,3584]{1,0:T(8,128)(2,1)S(1)}, bf16[128,3584]{1,0:T(8,128)(2,1)S(1)}, u32[]{:S(2)}, u32[]{:S(2)}) %collective-permute-start.4) | collective-permute-done | bytes 917536 | tf_op jit(solution)/shard_map/ppermute | solution.py:341
  76.1 0.0 collective-permute-done.5.refs_4_.refs_3_
  76.1 0.5 shard_map.94
  76.5 1.9 %collective-permute-start.6 = (bf16[128,3584]{1,0:T(8,128)(2,1)S(1)}, bf16[128,3584]{1,0:T(8,128)(2,1)S(1)}, u32[]{:S(2)}, u32[]{:S(2)}) collective-permute-start(bf16[128,3584]{1,0:T(8,128)(2,1)S(1)} %shard_map.94), channel_id=1, source_target_pairs={{0,2},{1,767},{2,4},{3,1},{4,6},{5,3},{6,8},{7,5},{8,10},{9,7},{10... | collective-permute-start | bytes 2752520 | tf_op jit(solution)/shard_map/ppermute | solution.py:341
  78.5 16.6 %all_to_all.16.refs_0_ = f32[12,32,128]{2,1,0:T(8,128)S(1)} all-to-all(f32[12,32,128]{2,1,0:T(8,128)S(1)} %shard_map.90.refs_4_), channel_id=1, replica_groups=mesh['y'=8,'z'=12,'row'=8] {'z'}, dimensions={0} | all-to-all | bytes 393216 | tf_op jit(solution)/shard_map/all_to_all | solution.py:390
  95.1 10.3 %all_to_all.17.refs_0_ = f32[8,32,128]{2,1,0:T(8,128)S(1)} all-to-all(f32[8,32,128]{2,1,0:T(8,128)S(1)} %shard_map.91), channel_id=1, replica_groups=mesh['y'=8,'z'=12,'row'=8] {'row'}, dimensions={0} | all-to-all | bytes 262144 | tf_op jit(solution)/shard_map/all_to_all | solution.py:390
  105.4 0.6 shard_map.92
  106.0 2.6 %shard_map.93 = (f32[128,3584]{1,0:T(8,128)S(1)}, bf16[128,3584]{1,0:T(8,128)(2,1)}) custom-call(bf16[128,3584]{1,0:T(8,128)(2,1)S(1)} %get-tuple-element.29.refs_3_.refs_2_.refs_4_.refs_0_, f32[128,128]{1,0:T(8,128)S(1)} %get-tuple-element.41.refs_1_, f32[128,128]{1,0:T(8,128)S(1)} %get-tuple-element.40.refs_9_.refs_2_, ...), custom_call_target="tpu_custom_call" | custom-call | flops 1000 | bytes 1000 | tf_op jit(solution)/shard_map/pallas_call | solution.py:45
  108.6 0.0 collective-permute-done.6.refs_3_
  108.6 2.8 %shard_map.95 = bf16[128,3584]{1,0:T(8,128)(2,1)} custom-call(f32[1,3584]{1,0:T(1,128)S(1)} %get-tuple-element.30.refs_1_.refs_5_.refs_0_, f32[128,3584]{1,0:T(8,128)S(1)} %get-tuple-element.53.refs_1_, bf16[128,3584]{1,0:T(8,128)(2,1)S(1)} %collective-permute-done.4.refs_1_.refs_2_, bf16[128,3584]{1,0:T(8,128)(2,1)S(1)} %collective-permute-done.6.refs_3_, ...), custom_call_target="tpu_custom_call" | custom-call | flops 1000 | bytes 1000 | tf_op jit(solution)/shard_map/pallas_call | solution.py:45
  (2 shorter events, 0.0 us)
Async XLA Ops:
  0.6 31.2 %collective-permute-start = (bf16[128,3584]{1,0:T(8,128)(2,1)}, bf16[128,3584]{1,0:T(8,128)(2,1)S(1)}, u32[]{:S(2)}, u32[]{:S(2)}) collective-permute-start(bf16[128,3584]{1,0:T(8,128)(2,1)} %refs_4_.1), channel_id=1, source_target_pairs={{2,0},{767,1},{4,2},{1,3},{6,4},{3,5},{8,6},{5,7},{10,8},{7,9},{12... | collective-permute-start | bytes 2752520 | tf_op jit(solution)/shard_map/ppermute | solution.py:341
  4.6 32.6 %copy-start = (s32[1,4]{1,0:T(1,128)S(1)}, s32[1,4]{1,0:T(1,128)}, u32[]{:S(2)}) copy-start(s32[1,4]{1,0:T(1,128)} %refs_0_.7) | copy-start | bytes 52
  8.5 28.6 %collective-permute-start.3 = (bf16[128,3584]{1,0:T(8,128)(2,1)S(1)}, bf16[128,3584]{1,0:T(8,128)(2,1)S(1)}, u32[]{:S(2)}, u32[]{:S(2)}) collective-permute-start(bf16[128,3584]{1,0:T(8,128)(2,1)S(1)} %get-tuple-element.31), channel_id=1, source_target_pairs={{0,1},{1,0},{2,3},{3,2},{4,5},{5,4},{6,7},{7,6},{8,9},{9,8},{10,11... | collective-permute-start | bytes 2752520 | tf_op jit(solution)/shard_map/ppermute | solution.py:341
  27.7 14.7 %collective-permute-start.2 = (bf16[128,3584]{1,0:T(8,128)(2,1)S(1)}, bf16[128,3584]{1,0:T(8,128)(2,1)S(1)}, u32[]{:S(2)}, u32[]{:S(2)}) collective-permute-start(bf16[128,3584]{1,0:T(8,128)(2,1)S(1)} %get-tuple-element.31), channel_id=1, source_target_pairs={{766,0},{3,1},{0,2},{5,3},{2,4},{7,5},{4,6},{9,7},{6,8},{11,9},{8,... | collective-permute-start | bytes 2752520 | tf_op jit(solution)/shard_map/ppermute | solution.py:341
  32.3 11.0 %collective-permute-start.1 = (bf16[128,3584]{1,0:T(8,128)(2,1)S(1)}, bf16[128,3584]{1,0:T(8,128)(2,1)S(1)}, u32[]{:S(2)}, u32[]{:S(2)}) collective-permute-start(bf16[128,3584]{1,0:T(8,128)(2,1)S(1)} %shard_map.85.refs_2_), channel_id=1, source_target_pairs={{0,1},{1,0},{2,3},{3,2},{4,5},{5,4},{6,7},{7,6},{8,9},{9,8},{10,11... | collective-permute-start | bytes 2752520 | tf_op jit(solution)/shard_map/ppermute | solution.py:341
  48.5 27.6 %collective-permute-start.5 = (bf16[2,128,3584]{2,1,0:T(8,128)(2,1)S(1)}, bf16[2,128,3584]{2,1,0:T(8,128)(2,1)S(1)}, u32[]{:S(2)}, u32[]{:S(2)}) collective-permute-start(bf16[2,128,3584]{2,1,0:T(8,128)(2,1)S(1)} %get-tuple-element.50), channel_id=1, source_target_pairs={{0,1},{1,0},{2,3},{3,2},{4,5},{5,4},{6,7},{7,6},{8,9},{9,8},{10,11... | collective-permute-start | bytes 5505032 | tf_op jit(solution)/shard_map/ppermute | solution.py:341
  56.5 19.6 %collective-permute-start.4 = (bf16[128,3584]{1,0:T(8,128)(2,1)S(1)}, bf16[128,3584]{1,0:T(8,128)(2,1)S(1)}, u32[]{:S(2)}, u32[]{:S(2)}) collective-permute-start(bf16[128,3584]{1,0:T(8,128)(2,1)S(1)} %get-tuple-element.46), channel_id=1, source_target_pairs={{0,766},{1,3},{2,0},{3,5},{4,2},{5,7},{6,4},{7,9},{8,6},{9,11},{10... | collective-permute-start | bytes 2752520 | tf_op jit(solution)/shard_map/ppermute | solution.py:341
  76.5 32.0 %collective-permute-start.6 = (bf16[128,3584]{1,0:T(8,128)(2,1)S(1)}, bf16[128,3584]{1,0:T(8,128)(2,1)S(1)}, u32[]{:S(2)}, u32[]{:S(2)}) collective-permute-start(bf16[128,3584]{1,0:T(8,128)(2,1)S(1)} %shard_map.94), channel_id=1, source_target_pairs={{0,2},{1,767},{2,4},{3,1},{4,6},{5,3},{6,8},{7,5},{8,10},{9,7},{10... | collective-permute-start | bytes 2752520 | tf_op jit(solution)/shard_map/ppermute | solution.py:341

commit v6 on v5

--- a/solution.py
+++ b/solution.py
@@ -74,8 +74,8 @@
     return lax.rsqrt(jnp.mean(values * values, axis=-1, keepdims=True) + 1e-06)
 
 
-def head_into(hidden_ref, gain, out_ref, first=0, rows=ROWS):
-    for i in range(first, first + rows, STEP):
+def head_into(hidden_ref, gain, out_ref):
+    for i in range(0, ROWS, STEP):
         values = hidden_ref[i : i + STEP, :].astype(f32)
         out_ref[i : i + STEP, :] = (values * factor_of(values) * gain).astype(bf16)
 
@@ -107,27 +107,26 @@
     return found
 
 
-def own_kernel(
-    q_hbm, d_hbm, gain_hbm, pos_hbm,
-    qn_ref, dn_ref, gain_ref, s_ref, top_ref, total_ref, acc_ref, picked_ref,
-    q_ref, d_ref, line_ref, pos_ref, sems,
-):
-    copies = [pltpu.make_async_copy(gain_hbm, line_ref, sems.at[2 * PARTS])]
-    for k, (src, dst) in enumerate(((d_hbm, d_ref), (q_hbm, q_ref))):
-        for part in range(PARTS):
-            rows = pl.ds(part * PART, PART)
-            copies.append(pltpu.make_async_copy(src.at[rows, :], dst.at[rows, :], sems.at[k * PARTS + part]))
-    copies.append(pltpu.make_async_copy(pos_hbm, pos_ref, sems.at[2 * PARTS + 1]))
+def doc_kernel(d_hbm, gain_hbm, dn_ref, gain_ref, d_ref, line_ref, sems):
+    copies = [pltpu.make_async_copy(d_hbm, d_ref, sems.at[0]), pltpu.make_async_copy(gain_hbm, line_ref, sems.at[1])]
     for copy in copies:
         copy.start()
-    copies[0].wait()
+    for copy in copies:
+        copy.wait()
     gain = jnp.concatenate([line_ref[i : i + 1, :] for i in range(GAIN_ROWS)], axis=1)
     gain_ref[...] = gain
-    for k, (hidden_ref, out_ref) in enumerate(((d_ref, dn_ref), (q_ref, qn_ref))):
-        for part in range(PARTS):
-            copies[1 + k * PARTS + part].wait()
-            head_into(hidden_ref, gain, out_ref, part * PART, PART)
-    copies[-1].wait()
+    head_into(d_ref, gain, dn_ref)
+
+
+def own_kernel(
+    dn_ref, gain_ref, q_hbm, pos_hbm, qn_ref, s_ref, top_ref, total_ref, acc_ref, picked_ref, hot_ref, q_ref, pos_ref, sems
+):
+    copies = [pltpu.make_async_copy(q_hbm, q_ref, sems.at[0]), pltpu.make_async_copy(pos_hbm, pos_ref, sems.at[1])]
+    for copy in copies:
+        copy.start()
+    for copy in copies:
+        copy.wait()
+    head_into(q_ref, gain_ref[...], qn_ref)
     scores = scores_of(qn_ref[...], dn_ref[...])
     top = jnp.max(scores, axis=1, keepdims=True)
     probs = jnp.exp(scores - top)
@@ -135,7 +134,9 @@
     top_ref[...] = across(top)
     total_ref[...] = across(jnp.sum(probs, axis=1, keepdims=True))
     probs = probs.astype(bf16)
-    onehot = onehot_of(pos_ref).astype(bf16)
+    onehot = onehot_of(pos_ref)
+    hot_ref[...] = onehot
+    onehot = onehot.astype(bf16)
     for c in range(0, WIDTH, CHUNK):
         docs = dn_ref[:, c : c + CHUNK]
         acc_ref[:, c : c + CHUNK] = jnp.dot(probs, docs, preferred_element_type=f32)
@@ -183,22 +184,17 @@
 
 def last_kernel(
     distance, neg_ref, dn_ref, back_ref, s_back_ref, qn_ref, top0_ref, total0_ref, acc0_ref, picked_ref, s_own_ref,
-    pos_hbm, q_hbm,
-    s_ref, lse_ref, gq_ref, hot_ref, lines, q_ref, pos_ref, sems,
+    hot_ref, q_hbm, s_ref, lse_ref, gq_ref, lines, q_ref, sems,
 ):
-    copies = [pltpu.make_async_copy(q_hbm, q_ref, sems.at[0]), pltpu.make_async_copy(pos_hbm, pos_ref, sems.at[1])]
-    for copy in copies:
-        copy.start()
+    incoming = pltpu.make_async_copy(q_hbm, q_ref, sems.at[0])
+    incoming.start()
     scores = jnp.where(listed(neg_ref, distance), scores_of(qn_ref[...], dn_ref[...]), HIDDEN)
     top, total, shrink, (probs, back_probs) = fold((scores, s_back_ref[...]), top0_ref, total0_ref)
     lse = top + jnp.log(total)
     s_ref[...] = scores
     lse_ref[...] = across(lse)
-    for copy in copies:
-        copy.wait()
-    onehot = onehot_of(pos_ref)
-    hot_ref[...] = onehot
-    loss = jnp.sum(lse - jnp.sum(s_own_ref[...] * onehot, axis=1, keepdims=True))
+    incoming.wait()
+    loss = jnp.sum(lse - jnp.sum(s_own_ref[...] * hot_ref[...], axis=1, keepdims=True))
     share = FACTOR / total
     kept_share = shrink * share
     squares = [
@@ -244,7 +240,7 @@
 
 
 def home_kernel(
-    qn_ref, lse_ref, s_own_ref, hot_ref, near_ref, gain_ref, gq_ref, q_hbm, own_ref, grad_hbm, q_ref, grad_ref, scaled_ref, sems
+    qn_ref, lse_ref, s_own_ref, hot_ref, near_ref, back_ref, gain_ref, gq_ref, q_hbm, own_ref, grad_hbm, q_ref, grad_ref, scaled_ref, sems
 ):
     incoming = pltpu.make_async_copy(q_hbm, q_ref, sems.at[PARTS])
     incoming.start()
@@ -252,7 +248,7 @@
     for c in range(0, WIDTH, CHUNK):
         cols = slice(c, c + CHUNK)
         term = jnp.dot(weight, qn_ref[:, cols], preferred_element_type=f32)
-        own_ref[:, cols] = term + near_ref[1, :, cols].astype(f32)
+        own_ref[:, cols] = term + near_ref[1, :, cols].astype(f32) + back_ref[:, cols].astype(f32)
     incoming.wait()
 
     def values_at(rows, cols):
@@ -264,7 +260,7 @@
     send_parts(lambda rows: pull(values_at, cotangent_at, gain_ref, scaled_ref, grad_ref, rows), grad_ref, grad_hbm, sems)
 
 
-def grad_doc_kernel(gain_ref, own_ref, back_ref, far_ref, d_hbm, grad_hbm, d_ref, grad_ref, scaled_ref, sems, in_sems):
+def grad_doc_kernel(gain_ref, own_ref, far_ref, d_hbm, grad_hbm, d_ref, grad_ref, scaled_ref, sems, in_sems):
     incoming = []
     for part in range(PARTS):
         rows = pl.ds(part * PART, PART)
@@ -276,8 +272,7 @@
         return d_ref[rows, cols].astype(f32)
 
     def cotangent_at(rows, cols):
-        total = own_ref[rows, cols] + back_ref[rows, cols].astype(f32) + far_ref[rows, cols].astype(f32)
-        return FACTOR * total
+        return FACTOR * (own_ref[rows, cols] + far_ref[rows, cols].astype(f32))
 
     def work(rows):
         if rows.start % PART == 0:
@@ -344,24 +339,25 @@
     square, block = (ROWS, LANES), (ROWS, WIDTH)
     dma = pltpu.SemaphoreType.DMA
     far = permute(doc_hidden, [(far_source[i], i) for i in devices])
-    qn, dn, gain_line, s_own, *state, picked = call(
-        own_kernel,
-        [held(block, bf16)] * 2
-        + [held((1, WIDTH), f32)]
-        + [held(square, f32)] * 3
-        + [held(block, f32), held(block, bf16)],
+    dn, gain_line = call(
+        doc_kernel,
+        [held(block, bf16), held((1, WIDTH), f32)],
         (),
-        distant=(leave(query_hidden), leave(doc_hidden), leave(gain), leave(positives)),
-        scratch=[
-            pltpu.VMEM(block, bf16), pltpu.VMEM(block, bf16), pltpu.VMEM((GAIN_ROWS, LANES), f32),
-            pltpu.VMEM((1, ROWS), jnp.int32), dma((2 * PARTS + 2,)),
-        ],
-    )
-    qn, gain_line, picked, s_own = kept(qn), kept(gain_line), kept(picked), kept(s_own)
+        distant=(leave(doc_hidden), leave(gain)),
+        scratch=[pltpu.VMEM(block, bf16), pltpu.VMEM((GAIN_ROWS, LANES), f32), dma((2,))],
+    )
+    gain_line = kept(gain_line)
     back = permute(dn, [(back_source[i], i) for i in devices])
     swap = permute(dn, swap_route)
-
-    far = call(head_kernel, held(block, bf16), (far, gain_line))
+    qn, s_own, *state, picked, hot = call(
+        own_kernel,
+        [held(block, bf16)] + [held(square, f32)] * 3 + [held(block, f32), held(block, bf16), held(square, f32)],
+        (kept(dn), gain_line),
+        distant=(leave(query_hidden), leave(positives)),
+        scratch=[pltpu.VMEM(block, bf16), pltpu.VMEM((1, ROWS), jnp.int32), dma((2,))],
+    )
+    qn, picked, s_own, hot = kept(qn), kept(picked), kept(s_own), kept(hot)
+    far = call(head_kernel, held(block, bf16), (far, gain_line), after=(s_own,))
     relay = permute(far, swap_route)
     s_swap, s_far, *state = call(
         functools.partial(pair_kernel, (1, 2)),
@@ -375,13 +371,13 @@
     )
     sizes = [lax.axis_size(a) for a in AXES]
     share = (SUM_ROWS, LANES)
-    s_relay, lse, gq, hot, lines = call(
+    s_relay, lse, gq, lines = call(
         functools.partial(last_kernel, -1),
-        [held(square, f32)] * 2 + [held(block, f32), held(square, f32), held(share, f32)],
-        (relay, back, kept(s_back), qn, *map(kept, state), picked, s_own),
+        [held(square, f32)] * 2 + [held(block, f32), held(share, f32)],
+        (relay, back, kept(s_back), qn, *map(kept, state), picked, s_own, hot),
         scalars=(neg_blocks,),
-        distant=(leave(positives), leave(query_hidden)),
-        scratch=[pltpu.VMEM(block, bf16), pltpu.VMEM((1, ROWS), jnp.int32), dma((2,))],
+        distant=(leave(query_hidden),),
+        scratch=[pltpu.VMEM(block, bf16), dma((1,))],
         aliases={7: 2},
     )
     lse = kept(lse)
@@ -399,22 +395,24 @@
     )
     near_term = permute(t_near, swap_route)
     back_term = permute(t_back, [(i, back_source[i]) for i in devices])
-    part = summed(exchange(part, 0), 1, after=(back_term,))
+    part = exchange(part, 0)
     far_sum = call(far_kernel, held(block, bf16), (qn, lse, kept(s_far), near_term), after=(part,))
     far_term = permute(far_sum, [(i, far_source[i]) for i in devices])
     t_own, grad_query = call(
         home_kernel,
         [held(block, f32), distant_array(block, bf16)],
-        (qn, lse, s_own, kept(hot), near_term, gain_line, kept(gq)),
+        (qn, lse, s_own, hot, near_term, back_term, gain_line, kept(gq)),
         distant=(leave(query_hidden),),
+        after=(far_sum,),
         scratch=[pltpu.VMEM(block, bf16), pltpu.VMEM(block, bf16), pltpu.VMEM((STEP, WIDTH), f32), dma((PARTS + 1,))],
     )
+    part = summed(part, 1, after=(t_own,))
     part = summed(exchange(part, 1), 2)
     part = exchange(part, 2)
     grad_doc = call(
         grad_doc_kernel,
         distant_array(block, bf16),
-        (gain_line, kept(t_own), back_term, far_term),
+        (gain_line, kept(t_own), far_term),
         distant=(leave(doc_hidden),),
         scratch=[
             pltpu.VMEM(block, bf16), pltpu.VMEM(block, bf16), pltpu.VMEM((STEP, WIDTH), f32), dma((PARTS,)), dma((PARTS,))

time: 112 us -> 110 us (0.982); the launches traced: 111 us -> 108 us
  waiting for transfers between devices: 10.7 us -> 1.69 us
  starting transfers between devices: 42.3 us -> 46.6 us
    ppermute x7, waiting for transfers between devices: 10.7 us -> 1.69 us  [permute(): return lax.ppermute(x, AXES, route)]
    ppermute x7, starting transfers between devices: 42.3 us -> 46.6 us  [permute(): return lax.ppermute(x, AXES, route)]
    pallas_call x12 -> x13, Pallas kernels: 19.1 us -> 19.5 us  [call(): pl.pallas_call(run, in_specs=[in_smem] * len(scalars) + [in_vmem] * len(a...]
  transfers between devices with their start and end apart: 7 -> 7, of which waited for: 3 -> 2; matrix products, arithmetic and copies ran while one was open for 0% -> 0% of each run, Pallas kernels for 10% -> 11%
where the time goes in v6:
time: 110 us; the launch traced here: 108 us
  starting transfers between devices  46.6 us (42%)
  blocking collectives  39.4 us (36%)
  Pallas kernels  19.5 us (18%)
  waiting for transfers between devices  1.69 us (2%)
    ppermute x7, starting transfers between devices, permute(): return lax.ppermute(x, AXES, route)  46.6 us
    all_to_all x3, blocking collectives, exchange(): return kept(lax.all_to_all(x, AXES[axis], 0, 0, tiled=True))  39.4 us
    pallas_call x13, Pallas kernels, call(): pl.pallas_call(run, in_specs=[in_smem] * len(scalars) + [in_vmem] * len(a...  19.5 us
  transfers between devices with their start and end apart: 7, of which 2 were waited for; matrix products, arithmetic and copies ran while one was open for 0% of the time, Pallas kernels for 11%

profile of v6, /device:TPU:1, one launch (start us, length us, event | category | flops | bytes accessed | tf_op | source)
XLA Modules:
  0.0 108.0 jit_solution(12133603476166014549)
XLA Ops:
  0.6 4.0 %collective-permute-start = (bf16[128,3584]{1,0:T(8,128)(2,1)}, bf16[128,3584]{1,0:T(8,128)(2,1)S(1)}, u32[]{:S(2)}, u32[]{:S(2)}) collective-permute-start(bf16[128,3584]{1,0:T(8,128)(2,1)} %refs_3_.1), channel_id=1, source_target_pairs={{2,0},{767,1},{4,2},{1,3},{6,4},{3,5},{8,6},{5,7},{10,8},{7,9},{12... | collective-permute-start | bytes 2752520 | tf_op jit(solution)/shard_map/ppermute | solution.py:336
  4.6 1.6 %shard_map.84 = (bf16[128,3584]{1,0:T(8,128)(2,1)S(1)}, f32[1,3584]{1,0:T(1,128)S(1)}) custom-call(bf16[128,3584]{1,0:T(8,128)(2,1)} %refs_3_.1, f32[28,128]{1,0:T(8,128)} %bitcast.4), custom_call_target="tpu_custom_call" | custom-call | flops 1000 | bytes 1000 | tf_op jit(solution)/shard_map/pallas_call | solution.py:45
  6.2 19.1 %collective-permute-start.3 = (bf16[128,3584]{1,0:T(8,128)(2,1)S(1)}, bf16[128,3584]{1,0:T(8,128)(2,1)S(1)}, u32[]{:S(2)}, u32[]{:S(2)}) collective-permute-start(bf16[128,3584]{1,0:T(8,128)(2,1)S(1)} %get-tuple-element.29.refs_0_), channel_id=1, source_target_pairs={{0,1},{1,0},{2,3},{3,2},{4,5},{5,4},{6,7},{7,6},{8,9},{9,8},{10,11... | collective-permute-start | bytes 2752520 | tf_op jit(solution)/shard_map/ppermute | solution.py:336
  25.4 2.5 %collective-permute-start.2 = (bf16[128,3584]{1,0:T(8,128)(2,1)S(1)}, bf16[128,3584]{1,0:T(8,128)(2,1)S(1)}, u32[]{:S(2)}, u32[]{:S(2)}) collective-permute-start(bf16[128,3584]{1,0:T(8,128)(2,1)S(1)} %get-tuple-element.29.refs_0_), channel_id=1, source_target_pairs={{766,0},{3,1},{0,2},{5,3},{2,4},{7,5},{4,6},{9,7},{6,8},{11,9},{8,... | collective-permute-start | bytes 2752520 | tf_op jit(solution)/shard_map/ppermute | solution.py:336
  27.9 0.0 copy-start
  27.9 3.0 %shard_map.85 = (bf16[128,3584]{1,0:T(8,128)(2,1)S(1)}, f32[128,128]{1,0:T(8,128)S(1)}, f32[128,128]{1,0:T(8,128)S(1)}, f32[128,128]{1,0:T(8,128)S(1)}, f32[128,...) custom-call(bf16[128,3584]{1,0:T(8,128)(2,1)S(1)} %get-tuple-element.29.refs_0_, ...), custom_call_target="tpu_custom_call" | custom-call | flops 1000 | bytes 1000 | tf_op jit(solution)/shard_map/pallas_call | solution.py:45
  30.8 1.0 collective-permute-done.refs_0_
  31.9 0.4 shard_map.86.refs_2_
  32.3 7.2 %collective-permute-start.1 = (bf16[128,3584]{1,0:T(8,128)(2,1)S(1)}, bf16[128,3584]{1,0:T(8,128)(2,1)S(1)}, u32[]{:S(2)}, u32[]{:S(2)}) collective-permute-start(bf16[128,3584]{1,0:T(8,128)(2,1)S(1)} %shard_map.86.refs_2_), channel_id=1, source_target_pairs={{0,1},{1,0},{2,3},{3,2},{4,5},{5,4},{6,7},{7,6},{8,9},{9,8},{10,11... | collective-permute-start | bytes 2752520 | tf_op jit(solution)/shard_map/ppermute | solution.py:336
  39.5 0.0 collective-permute-done.3.refs_1_
  39.5 0.0 copy-done
  39.5 2.2 %shard_map.87 = (f32[128,128]{1,0:T(8,128)S(1)}, f32[128,128]{1,0:T(8,128)S(1)}, f32[128,128]{1,0:T(8,128)S(1)}, f32[128,128]{1,0:T(8,128)S(1)}, f32[128,3584]{1,0:T(8,128)S(1)}) custom-call(s32[1,4]{1,0:T(1,128)S(1)} %copy-done, bf16[128,3584]{1,0:T(8,128)(2,1)S(1)} %collective-permute-done.3.refs_1_, ...), custom_call_target="tpu_custom_call", output_to_operand_aliasing={{2}: (4, {}), {3}: (5, {}), {4}: (6, {})} | custom-call | flops 1000 | bytes 1000 | tf_op jit(solution)/shard_map/pallas_call | solution.py:45
  41.7 0.7 collective-permute-done.2.refs_1_.refs_2_
  42.4 0.9 shard_map.88.refs_3_.refs_4_
  43.3 0.0 collective-permute-done.1.refs_1_
  43.3 4.0 %shard_map.89 = (f32[128,128]{1,0:T(8,128)S(1)}, f32[128,128]{1,0:T(8,128)S(1)}, f32[128,3584]{1,0:T(8,128)S(1)}, f32[32,128]{1,0:T(8,128)S(1)}) custom-call(s32[1,4]{1,0:T(1,128)S(1)} %copy-done, bf16[128,3584]{1,0:T(8,128)(2,1)S(1)} %collective-permute-done.1.refs_1_, ...), custom_call_target="tpu_custom_call", output_to_operand_aliasing={{2}: (7, {})} | custom-call | flops 1000 | bytes 1000 | tf_op jit(solution)/shard_map/pallas_call | solution.py:45
  47.3 0.9 shard_map.90
  48.3 5.7 %collective-permute-start.4 = (bf16[2,128,3584]{2,1,0:T(8,128)(2,1)S(1)}, bf16[2,128,3584]{2,1,0:T(8,128)(2,1)S(1)}, u32[]{:S(2)}, u32[]{:S(2)}) collective-permute-start(bf16[2,128,3584]{2,1,0:T(8,128)(2,1)S(1)} %get-tuple-element.47), channel_id=1, source_target_pairs={{0,1},{1,0},{2,3},{3,2},{4,5},{5,4},{6,7},{7,6},{8,9},{9,8},{10,11... | collective-permute-start | bytes 5505032 | tf_op jit(solution)/shard_map/ppermute | solution.py:336
  53.9 1.9 %collective-permute-start.5 = (bf16[128,3584]{1,0:T(8,128)(2,1)S(1)}, bf16[128,3584]{1,0:T(8,128)(2,1)S(1)}, u32[]{:S(2)}, u32[]{:S(2)}) collective-permute-start(bf16[128,3584]{1,0:T(8,128)(2,1)S(1)} %get-tuple-element.48), channel_id=1, source_target_pairs={{0,766},{1,3},{2,0},{3,5},{4,2},{5,7},{6,4},{7,9},{8,6},{9,11},{10... | collective-permute-start | bytes 2752520 | tf_op jit(solution)/shard_map/ppermute | solution.py:336
  55.9 11.5 %all_to_all.15.refs_4_.refs_0_ = f32[8,32,128]{2,1,0:T(8,128)S(1)} all-to-all(f32[8,32,128]{2,1,0:T(8,128)S(1)} %get-tuple-element.46), channel_id=1, replica_groups=mesh['y'=8,'z'=12,'row'=8] {'y'}, dimensions={0} | all-to-all | bytes 262144 | tf_op jit(solution)/shard_map/all_to_all | solution.py:386
  67.4 0.0 collective-permute-done.4.refs_3_.refs_4_
  67.4 0.4 shard_map.91.refs_9_
  67.9 6.3 %collective-permute-start.6 = (bf16[128,3584]{1,0:T(8,128)(2,1)S(1)}, bf16[128,3584]{1,0:T(8,128)(2,1)S(1)}, u32[]{:S(2)}, u32[]{:S(2)}) collective-permute-start(bf16[128,3584]{1,0:T(8,128)(2,1)S(1)} %shard_map.91.refs_9_), channel_id=1, source_target_pairs={{0,2},{1,767},{2,4},{3,1},{4,6},{5,3},{6,8},{7,5},{8,10},{9,7},{10... | collective-permute-start | bytes 2752520 | tf_op jit(solution)/shard_map/ppermute | solution.py:336
  74.2 0.0 collective-permute-done.5.refs_5_
  74.2 2.6 %shard_map.92 = (f32[128,3584]{1,0:T(8,128)S(1)}, bf16[128,3584]{1,0:T(8,128)(2,1)}) custom-call(bf16[128,3584]{1,0:T(8,128)(2,1)S(1)} %get-tuple-element.31.refs_3_.refs_2_.refs_4_.refs_0_, f32[128,128]{1,0:T(8,128)S(1)} %get-tuple-element.42.refs_1_, f32[128,128]{1,0:T(8,128)S(1)} %get-tuple-element.32.refs_2_.refs_9_, ...), custom_call_target="tpu_custom_call" | custom-call | flops 1000 | bytes 1000 | tf_op jit(solution)/shard_map/pallas_call | solution.py:45
  76.8 14.2 %all_to_all.16.refs_0_ = f32[12,32,128]{2,1,0:T(8,128)S(1)} all-to-all(f32[12,32,128]{2,1,0:T(8,128)S(1)} %shard_map.93), channel_id=1, replica_groups=mesh['y'=8,'z'=12,'row'=8] {'z'}, dimensions={0} | all-to-all | bytes 393216 | tf_op jit(solution)/shard_map/all_to_all | solution.py:386
  91.0 13.7 %all_to_all.17.refs_0_ = f32[8,32,128]{2,1,0:T(8,128)S(1)} all-to-all(f32[8,32,128]{2,1,0:T(8,128)S(1)} %shard_map.94), channel_id=1, replica_groups=mesh['y'=8,'z'=12,'row'=8] {'row'}, dimensions={0} | all-to-all | bytes 262144 | tf_op jit(solution)/shard_map/all_to_all | solution.py:386
  104.7 0.6 shard_map.95
  105.3 0.0 collective-permute-done.6.refs_2_
  105.3 2.7 %shard_map.96 = bf16[128,3584]{1,0:T(8,128)(2,1)} custom-call(f32[1,3584]{1,0:T(1,128)S(1)} %get-tuple-element.30.refs_1_.refs_6_.refs_0_, f32[128,3584]{1,0:T(8,128)S(1)} %get-tuple-element.50.refs_1_, bf16[128,3584]{1,0:T(8,128)(2,1)S(1)} %collective-permute-done.6.refs_2_, bf16[128,3584]{1,0:T(8,128)(2,1)} %refs_3_.1), custom_call_target="tpu_custom_call" | custom-call | flops 1000 | bytes 1000 | tf_op jit(solution)/shard_map/pallas_call | solution.py:45
  (2 shorter events, 0.0 us)
Async XLA Ops:
  0.6 31.2 %collective-permute-start = (bf16[128,3584]{1,0:T(8,128)(2,1)}, bf16[128,3584]{1,0:T(8,128)(2,1)S(1)}, u32[]{:S(2)}, u32[]{:S(2)}) collective-permute-start(bf16[128,3584]{1,0:T(8,128)(2,1)} %refs_3_.1), channel_id=1, source_target_pairs={{2,0},{767,1},{4,2},{1,3},{6,4},{3,5},{8,6},{5,7},{10,8},{7,9},{12... | collective-permute-start | bytes 2752520 | tf_op jit(solution)/shard_map/ppermute | solution.py:336
  6.2 33.3 %collective-permute-start.3 = (bf16[128,3584]{1,0:T(8,128)(2,1)S(1)}, bf16[128,3584]{1,0:T(8,128)(2,1)S(1)}, u32[]{:S(2)}, u32[]{:S(2)}) collective-permute-start(bf16[128,3584]{1,0:T(8,128)(2,1)S(1)} %get-tuple-element.29.refs_0_), channel_id=1, source_target_pairs={{0,1},{1,0},{2,3},{3,2},{4,5},{5,4},{6,7},{7,6},{8,9},{9,8},{10,11... | collective-permute-start | bytes 2752520 | tf_op jit(solution)/shard_map/ppermute | solution.py:336
  25.4 17.0 %collective-permute-start.2 = (bf16[128,3584]{1,0:T(8,128)(2,1)S(1)}, bf16[128,3584]{1,0:T(8,128)(2,1)S(1)}, u32[]{:S(2)}, u32[]{:S(2)}) collective-permute-start(bf16[128,3584]{1,0:T(8,128)(2,1)S(1)} %get-tuple-element.29.refs_0_), channel_id=1, source_target_pairs={{766,0},{3,1},{0,2},{5,3},{2,4},{7,5},{4,6},{9,7},{6,8},{11,9},{8,... | collective-permute-start | bytes 2752520 | tf_op jit(solution)/shard_map/ppermute | solution.py:336
  27.9 11.7 %copy-start = (s32[1,4]{1,0:T(1,128)S(1)}, s32[1,4]{1,0:T(1,128)}, u32[]{:S(2)}) copy-start(s32[1,4]{1,0:T(1,128)} %refs_0_.7) | copy-start | bytes 52
  32.3 11.0 %collective-permute-start.1 = (bf16[128,3584]{1,0:T(8,128)(2,1)S(1)}, bf16[128,3584]{1,0:T(8,128)(2,1)S(1)}, u32[]{:S(2)}, u32[]{:S(2)}) collective-permute-start(bf16[128,3584]{1,0:T(8,128)(2,1)S(1)} %shard_map.86.refs_2_), channel_id=1, source_target_pairs={{0,1},{1,0},{2,3},{3,2},{4,5},{5,4},{6,7},{7,6},{8,9},{9,8},{10,11... | collective-permute-start | bytes 2752520 | tf_op jit(solution)/shard_map/ppermute | solution.py:336
  48.3 19.1 %collective-permute-start.4 = (bf16[2,128,3584]{2,1,0:T(8,128)(2,1)S(1)}, bf16[2,128,3584]{2,1,0:T(8,128)(2,1)S(1)}, u32[]{:S(2)}, u32[]{:S(2)}) collective-permute-start(bf16[2,128,3584]{2,1,0:T(8,128)(2,1)S(1)} %get-tuple-element.47), channel_id=1, source_target_pairs={{0,1},{1,0},{2,3},{3,2},{4,5},{5,4},{6,7},{7,6},{8,9},{9,8},{10,11... | collective-permute-start | bytes 5505032 | tf_op jit(solution)/shard_map/ppermute | solution.py:336
  53.9 20.2 %collective-permute-start.5 = (bf16[128,3584]{1,0:T(8,128)(2,1)S(1)}, bf16[128,3584]{1,0:T(8,128)(2,1)S(1)}, u32[]{:S(2)}, u32[]{:S(2)}) collective-permute-start(bf16[128,3584]{1,0:T(8,128)(2,1)S(1)} %get-tuple-element.48), channel_id=1, source_target_pairs={{0,766},{1,3},{2,0},{3,5},{4,2},{5,7},{6,4},{7,9},{8,6},{9,11},{10... | collective-permute-start | bytes 2752520 | tf_op jit(solution)/shard_map/ppermute | solution.py:336
  67.9 37.5 %collective-permute-start.6 = (bf16[128,3584]{1,0:T(8,128)(2,1)S(1)}, bf16[128,3584]{1,0:T(8,128)(2,1)S(1)}, u32[]{:S(2)}, u32[]{:S(2)}) collective-permute-start(bf16[128,3584]{1,0:T(8,128)(2,1)S(1)} %shard_map.91.refs_9_), channel_id=1, source_target_pairs={{0,2},{1,767},{2,4},{3,1},{4,6},{5,3},{6,8},{7,5},{8,10},{9,7},{10... | collective-permute-start | bytes 2752520 | tf_op jit(solution)/shard_map/ppermute | solution.py:336

commit v7 on v6

--- a/solution.py
+++ b/solution.py
@@ -34,7 +34,7 @@
     return pltpu.VMEM(shape, dtype)
 
 
-def call(kernel, out_shape, args, scratch=(), aliases=None, scalars=(), distant=(), after=()):
+def call(kernel, out_shape, args, scratch=(), aliases=None, scalars=(), distant=(), after=(), flops=1000):
     given = len(scalars) + len(args) + len(distant)
 
     def run(*refs):
@@ -49,7 +49,7 @@
         out_shape=out_shape,
         scratch_shapes=list(scratch),
         input_output_aliases=aliases or {},
-        cost_estimate=pl.CostEstimate(flops=1000, bytes_accessed=1000, transcendentals=0),
+        cost_estimate=pl.CostEstimate(flops=flops, bytes_accessed=1000, transcendentals=0),
         compiler_params=pltpu.CompilerParams(vmem_limit_bytes=15 * 2**20),
     )(*scalars, *args, *distant, *after)
 
@@ -119,14 +119,19 @@
 
 
 def own_kernel(
-    dn_ref, gain_ref, q_hbm, pos_hbm, qn_ref, s_ref, top_ref, total_ref, acc_ref, picked_ref, hot_ref, q_ref, pos_ref, sems
+    dn_ref, gain_ref, q_hbm, pos_hbm, qn_ref, s_ref, top_ref, total_ref, acc_ref, picked_ref, hot_ref, scaled_ref, q_ref, pos_ref, sems
 ):
     copies = [pltpu.make_async_copy(q_hbm, q_ref, sems.at[0]), pltpu.make_async_copy(pos_hbm, pos_ref, sems.at[1])]
     for copy in copies:
         copy.start()
     for copy in copies:
         copy.wait()
-    head_into(q_ref, gain_ref[...], qn_ref)
+    gain = gain_ref[...]
+    for i in range(0, ROWS, STEP):
+        values = q_ref[i : i + STEP, :].astype(f32)
+        scaled = values * factor_of(values)
+        scaled_ref[i : i + STEP, :] = scaled
+        qn_ref[i : i + STEP, :] = (scaled * gain).astype(bf16)
     scores = scores_of(qn_ref[...], dn_ref[...])
     top = jnp.max(scores, axis=1, keepdims=True)
     probs = jnp.exp(scores - top)
@@ -184,33 +189,32 @@
 
 def last_kernel(
     distance, neg_ref, dn_ref, back_ref, s_back_ref, qn_ref, top0_ref, total0_ref, acc0_ref, picked_ref, s_own_ref,
-    hot_ref, q_hbm, s_ref, lse_ref, gq_ref, lines, q_ref, sems,
+    hot_ref, scaled_ref, s_ref, lse_ref, gq_ref, lines,
 ):
-    incoming = pltpu.make_async_copy(q_hbm, q_ref, sems.at[0])
-    incoming.start()
     scores = jnp.where(listed(neg_ref, distance), scores_of(qn_ref[...], dn_ref[...]), HIDDEN)
     top, total, shrink, (probs, back_probs) = fold((scores, s_back_ref[...]), top0_ref, total0_ref)
     lse = top + jnp.log(total)
     s_ref[...] = scores
     lse_ref[...] = across(lse)
-    incoming.wait()
     loss = jnp.sum(lse - jnp.sum(s_own_ref[...] * hot_ref[...], axis=1, keepdims=True))
     share = FACTOR / total
     kept_share = shrink * share
-    squares = [
-        jnp.sum(jnp.square(q_ref[i : i + STEP, :].astype(f32)), axis=-1, keepdims=True) for i in range(0, ROWS, STEP)
-    ]
-    factor = lax.rsqrt(jnp.concatenate(squares, axis=0) / WIDTH + 1e-06)
     for c in range(0, WIDTH, CHUNK):
         cols = slice(c, c + CHUNK)
         term = jnp.dot(probs, dn_ref[:, cols], preferred_element_type=f32)
         term = term + jnp.dot(back_probs, back_ref[:, cols], preferred_element_type=f32)
         gq = acc0_ref[:, cols] * kept_share + term * share - FACTOR * picked_ref[:, cols].astype(f32)
         gq_ref[:, cols] = gq
-        added = 2.0 * jnp.sum(gq * (q_ref[:, cols].astype(f32) * factor), axis=0, keepdims=True)
+        added = 2.0 * jnp.sum(gq * scaled_ref[:, cols], axis=0, keepdims=True)
         for i in range(0, CHUNK, LANES):
             lines[(c + i) // LANES : (c + i) // LANES + 1, :] = added[:, i : i + LANES]
-    lines[GAIN_ROWS:, :] = jnp.full((SUM_ROWS - GAIN_ROWS, LANES), loss, f32)
+    lines[GAIN_ROWS:, :] = in_two(jnp.full((SUM_ROWS - GAIN_ROWS, LANES), loss, f32))
+
+
+def in_two(value):
+    head = value.astype(bf16).astype(f32)
+    row = lax.broadcasted_iota(jnp.int32, value.shape, 0)
+    return jnp.where(row == 0, head, jnp.where(row == 1, value - head, 0.0))
 
 
 def turned(block_ref, lse_ref, hot_ref=None):
@@ -228,7 +232,7 @@
         near_ref[0, :, cols] = jnp.dot(w_relay, queries, preferred_element_type=f32).astype(bf16)
         near_ref[1, :, cols] = jnp.dot(w_swap, queries, preferred_element_type=f32).astype(bf16)
         back_ref[:, cols] = jnp.dot(w_back, queries, preferred_element_type=f32).astype(bf16)
-    part_ref[...] = jnp.broadcast_to(lines_ref[...][None], part_ref.shape)
+    part_ref[...] = jnp.broadcast_to(lines_ref[...].astype(bf16)[None], part_ref.shape)
 
 
 def far_kernel(qn_ref, lse_ref, s_far_ref, near_ref, far_ref):
@@ -312,15 +316,23 @@
         out_ref[rows, cols] = grad.astype(bf16)
 
 
-def sum_kernel(in_ref, out_ref):
-    total = jnp.sum(in_ref[...], axis=0)
-    out_ref[...] = jnp.broadcast_to(total[None], out_ref.shape)
+def total_of(in_ref):
+    total = jnp.sum(in_ref[...].astype(f32), axis=0)
+    loss = total[GAIN_ROWS : GAIN_ROWS + 1] + total[GAIN_ROWS + 1 : GAIN_ROWS + 2]
+    return total[:GAIN_ROWS], loss
+
+
+def sum_kernel(in_ref, out_ref, lines):
+    gain, loss = total_of(in_ref)
+    lines[:GAIN_ROWS, :] = gain
+    lines[GAIN_ROWS:, :] = in_two(jnp.broadcast_to(loss, (SUM_ROWS - GAIN_ROWS, LANES)))
+    out_ref[...] = jnp.broadcast_to(lines[...].astype(bf16)[None], out_ref.shape)
 
 
 def end_kernel(denom, in_ref, gain_ref, loss_ref):
-    total = jnp.sum(in_ref[...], axis=0) / denom
-    gain_ref[...] = total[:GAIN_ROWS]
-    loss_ref[...] = total[GAIN_ROWS : GAIN_ROWS + 1, 0:1]
+    gain, loss = total_of(in_ref)
+    gain_ref[...] = gain / denom
+    loss_ref[...] = loss[:, 0:1] / denom
 
 
 def body(query_hidden, doc_hidden, gain, positives, neg_blocks):
@@ -349,9 +361,10 @@
     gain_line = kept(gain_line)
     back = permute(dn, [(back_source[i], i) for i in devices])
     swap = permute(dn, swap_route)
-    qn, s_own, *state, picked, hot = call(
+    qn, s_own, *state, picked, hot, scaled = call(
         own_kernel,
-        [held(block, bf16)] + [held(square, f32)] * 3 + [held(block, f32), held(block, bf16), held(square, f32)],
+        [held(block, bf16)] + [held(square, f32)] * 3 + [held(block, f32), held(block, bf16), held(square, f32)]
+        + [held(block, f32)],
         (kept(dn), gain_line),
         distant=(leave(query_hidden), leave(positives)),
         scratch=[pltpu.VMEM(block, bf16), pltpu.VMEM((1, ROWS), jnp.int32), dma((2,))],
@@ -374,10 +387,8 @@
     s_relay, lse, gq, lines = call(
         functools.partial(last_kernel, -1),
         [held(square, f32)] * 2 + [held(block, f32), held(share, f32)],
-        (relay, back, kept(s_back), qn, *map(kept, state), picked, s_own, hot),
+        (relay, back, kept(s_back), qn, *map(kept, state), picked, s_own, hot, kept(scaled)),
         scalars=(neg_blocks,),
-        distant=(leave(query_hidden),),
-        scratch=[pltpu.VMEM(block, bf16), dma((1,))],
         aliases={7: 2},
     )
     lse = kept(lse)
@@ -386,11 +397,13 @@
         return kept(lax.all_to_all(x, AXES[axis], 0, 0, tiled=True))
 
     def summed(x, axis, after=()):
-        return call(sum_kernel, held((sizes[axis], *share), f32), (x,), after=after)
+        return call(
+            sum_kernel, held((sizes[axis], *share), bf16), (x,), after=after, scratch=[pltpu.VMEM(share, f32)]
+        )
 
     t_near, t_back, part = call(
         near_kernel,
-        [held((2, *block), bf16), held(block, bf16), held((sizes[0], *share), f32)],
+        [held((2, *block), bf16), held(block, bf16), held((sizes[0], *share), bf16)],
         (qn, lse, kept(s_relay), kept(s_swap), kept(s_back), kept(lines)),
     )
     near_term = permute(t_near, swap_route)
@@ -407,21 +420,24 @@
         scratch=[pltpu.VMEM(block, bf16), pltpu.VMEM(block, bf16), pltpu.VMEM((STEP, WIDTH), f32), dma((PARTS + 1,))],
     )
     part = summed(part, 1, after=(t_own,))
-    part = summed(exchange(part, 1), 2)
-    part = exchange(part, 2)
+    ready = summed(exchange(part, 1), 2)
+    part = exchange(ready, 2)
     grad_doc = call(
         grad_doc_kernel,
         distant_array(block, bf16),
         (gain_line, kept(t_own), far_term),
         distant=(leave(doc_hidden),),
+        after=(ready,),
         scratch=[
             pltpu.VMEM(block, bf16), pltpu.VMEM(block, bf16), pltpu.VMEM((STEP, WIDTH), f32), dma((PARTS,)), dma((PARTS,))
         ],
+        flops=3_000_000_000,
     )
     grad_gain, mean_loss = call(
         functools.partial(end_kernel, float(ROWS * count)),
         [jax.ShapeDtypeStruct((GAIN_ROWS, LANES), f32), jax.ShapeDtypeStruct((1, 1), f32)],
         (part,),
+        after=(leave(grad_doc),),
     )
     return mean_loss.reshape(()), grad_gain.reshape(WIDTH), grad_query, grad_doc
 

time: 110 us -> 104 us (0.945)
  the two profiles are of different devices: /device:TPU:1 before, /device:TPU:8 now
where the time goes in v7:
time: 104 us
  starting transfers between devices  37.9 us (36%)
  blocking collectives  33.4 us (32%)
  Pallas kernels  19.8 us (19%)
  waiting for transfers between devices  11.7 us (11%)
    all_to_all x2, blocking collectives, exchange(): return kept(lax.all_to_all(x, AXES[axis], 0, 0, tiled=True))  33.4 us
    ppermute x7, starting transfers between devices, permute(): return lax.ppermute(x, AXES, route)  32.5 us
    pallas_call x13, Pallas kernels, call(): pl.pallas_call(run, in_specs=[in_smem] * len(scalars) + [in_vmem] * len(a...  19.8 us
    ppermute x7, waiting for transfers between devices, permute(): return lax.ppermute(x, AXES, route)  9.97 us
    all_to_all x1, starting transfers between devices, exchange(): return kept(lax.all_to_all(x, AXES[axis], 0, 0, tiled=True))  5.4 us
  transfers between devices with their start and end apart: 8, of which 3 were waited for; matrix products, arithmetic and copies ran while one was open for 0% of the time, Pallas kernels for 15%

profile of v7, /device:TPU:8, one launch (start us, length us, event | category | flops | bytes accessed | tf_op | source)
XLA Modules:
  0.0 103.6 jit_solution(14134869562834835831)
XLA Ops:
  0.6 16.7 %collective-permute-start = (bf16[128,3584]{1,0:T(8,128)(2,1)}, bf16[128,3584]{1,0:T(8,128)(2,1)S(1)}, u32[]{:S(2)}, u32[]{:S(2)}) collective-permute-start(bf16[128,3584]{1,0:T(8,128)(2,1)} %refs_3_.1), channel_id=1, source_target_pairs={{2,0},{767,1},{4,2},{1,3},{6,4},{3,5},{8,6},{5,7},{10,8},{7,9},{12... | collective-permute-start | bytes 2752520 | tf_op jit(solution)/shard_map/ppermute | solution.py:348
  17.3 1.6 %shard_map.84 = (bf16[128,3584]{1,0:T(8,128)(2,1)S(1)}, f32[1,3584]{1,0:T(1,128)S(1)}) custom-call(bf16[128,3584]{1,0:T(8,128)(2,1)} %refs_3_.1, f32[28,128]{1,0:T(8,128)} %bitcast.4), custom_call_target="tpu_custom_call" | custom-call | flops 1000 | bytes 1000 | tf_op jit(solution)/shard_map/pallas_call | solution.py:45
  19.0 1.9 %collective-permute-start.3 = (bf16[128,3584]{1,0:T(8,128)(2,1)S(1)}, bf16[128,3584]{1,0:T(8,128)(2,1)S(1)}, u32[]{:S(2)}, u32[]{:S(2)}) collective-permute-start(bf16[128,3584]{1,0:T(8,128)(2,1)S(1)} %get-tuple-element.30.refs_0_), channel_id=1, source_target_pairs={{0,1},{1,0},{2,3},{3,2},{4,5},{5,4},{6,7},{7,6},{8,9},{9,8},{10,11... | collective-permute-start | bytes 2752520 | tf_op jit(solution)/shard_map/ppermute | solution.py:348
  20.9 1.9 %collective-permute-start.2 = (bf16[128,3584]{1,0:T(8,128)(2,1)S(1)}, bf16[128,3584]{1,0:T(8,128)(2,1)S(1)}, u32[]{:S(2)}, u32[]{:S(2)}) collective-permute-start(bf16[128,3584]{1,0:T(8,128)(2,1)S(1)} %get-tuple-element.30.refs_0_), channel_id=1, source_target_pairs={{766,0},{3,1},{0,2},{5,3},{2,4},{7,5},{4,6},{9,7},{6,8},{11,9},{8,... | collective-permute-start | bytes 2752520 | tf_op jit(solution)/shard_map/ppermute | solution.py:348
  22.8 0.0 copy-start
  22.8 3.1 %shard_map.85 = (bf16[128,3584]{1,0:T(8,128)(2,1)S(1)}, f32[128,128]{1,0:T(8,128)S(1)}, f32[128,128]{1,0:T(8,128)S(1)}, f32[128,128]{1,0:T(8,128)S(1)}, f32[128,...) custom-call(bf16[128,3584]{1,0:T(8,128)(2,1)S(1)} %get-tuple-element.30.refs_, ...), custom_call_target="tpu_custom_call" | custom-call | flops 1000 | bytes 1000 | tf_op jit(solution)/shard_map/pallas_call | solution.py:45
  25.9 6.8 %collective-permute-done.refs_0_ = bf16[128,3584]{1,0:T(8,128)(2,1)S(1)} collective-permute-done((bf16[128,3584]{1,0:T(8,128)(2,1)}, bf16[128,3584]{1,0:T(8,128)(2,1)S(1)}, u32[]{:S(2)}, u32[]{:S(2)}) %collective-permute-start) | collective-permute-done | bytes 917536 | tf_op jit(solution)/shard_map/ppermute | solution.py:348
  32.6 0.4 shard_map.86.refs_2_
  33.1 1.9 %collective-permute-start.1 = (bf16[128,3584]{1,0:T(8,128)(2,1)S(1)}, bf16[128,3584]{1,0:T(8,128)(2,1)S(1)}, u32[]{:S(2)}, u32[]{:S(2)}) collective-permute-start(bf16[128,3584]{1,0:T(8,128)(2,1)S(1)} %shard_map.86.refs_2_), channel_id=1, source_target_pairs={{0,1},{1,0},{2,3},{3,2},{4,5},{5,4},{6,7},{7,6},{8,9},{9,8},{10,11... | collective-permute-start | bytes 2752520 | tf_op jit(solution)/shard_map/ppermute | solution.py:348
  35.0 0.0 collective-permute-done.3.refs_1_
  35.0 0.0 copy-done
  35.0 2.2 %shard_map.87 = (f32[128,128]{1,0:T(8,128)S(1)}, f32[128,128]{1,0:T(8,128)S(1)}, f32[128,128]{1,0:T(8,128)S(1)}, f32[128,128]{1,0:T(8,128)S(1)}, f32[128,3584]{1,0:T(8,128)S(1)}) custom-call(s32[1,4]{1,0:T(1,128)S(1)} %copy-done, bf16[128,3584]{1,0:T(8,128)(2,1)S(1)} %collective-permute-done.3.refs_1_, ...), custom_call_target="tpu_custom_call", output_to_operand_aliasing={{2}: (4, {}), {3}: (5, {}), {4}: (6, {})} | custom-call | flops 1000 | bytes 1000 | tf_op jit(solution)/shard_map/pallas_call | solution.py:45
  37.2 3.2 %collective-permute-done.2.refs_1_.refs_2_ = bf16[128,3584]{1,0:T(8,128)(2,1)S(1)} collective-permute-done((bf16[128,3584]{1,0:T(8,128)(2,1)S(1)}, bf16[128,3584]{1,0:T(8,128)(2,1)S(1)}, u32[]{:S(2)}, u32[]{:S(2)}) %collective-permute-start.2) | collective-permute-done | bytes 917536 | tf_op jit(solution)/shard_map/ppermute | solution.py:348
  40.4 0.9 shard_map.88.refs_3_.refs_4_
  41.3 0.0 collective-permute-done.1.refs_1_
  41.3 2.4 %shard_map.89 = (f32[128,128]{1,0:T(8,128)S(1)}, f32[128,128]{1,0:T(8,128)S(1)}, f32[128,3584]{1,0:T(8,128)S(1)}, f32[32,128]{1,0:T(8,128)S(1)}) custom-call(s32[1,4]{1,0:T(1,128)S(1)} %copy-done, bf16[128,3584]{1,0:T(8,128)(2,1)S(1)} %collective-permute-done.1.refs_1_, ...), custom_call_target="tpu_custom_call", output_to_operand_aliasing={{2}: (7, {})} | custom-call | flops 1000 | bytes 1000 | tf_op jit(solution)/shard_map/pallas_call | solution.py:45
  43.8 0.9 shard_map.90
  44.7 1.9 %collective-permute-start.4 = (bf16[2,128,3584]{2,1,0:T(8,128)(2,1)S(1)}, bf16[2,128,3584]{2,1,0:T(8,128)(2,1)S(1)}, u32[]{:S(2)}, u32[]{:S(2)}) collective-permute-start(bf16[2,128,3584]{2,1,0:T(8,128)(2,1)S(1)} %get-tuple-element.49), channel_id=1, source_target_pairs={{0,1},{1,0},{2,3},{3,2},{4,5},{5,4},{6,7},{7,6},{8,9},{9,8},{10,11... | collective-permute-start | bytes 5505032 | tf_op jit(solution)/shard_map/ppermute | solution.py:348
  46.7 6.3 %collective-permute-start.5 = (bf16[128,3584]{1,0:T(8,128)(2,1)S(1)}, bf16[128,3584]{1,0:T(8,128)(2,1)S(1)}, u32[]{:S(2)}, u32[]{:S(2)}) collective-permute-start(bf16[128,3584]{1,0:T(8,128)(2,1)S(1)} %get-tuple-element.50), channel_id=1, source_target_pairs={{0,766},{1,3},{2,0},{3,5},{4,2},{5,7},{6,4},{7,9},{8,6},{9,11},{10... | collective-permute-start | bytes 2752520 | tf_op jit(solution)/shard_map/ppermute | solution.py:348
  52.9 15.5 %all_to_all.15.refs_4_.refs_0_ = bf16[8,32,128]{2,1,0:T(8,128)(2,1)S(1)} all-to-all(bf16[8,32,128]{2,1,0:T(8,128)(2,1)S(1)} %get-tuple-element.48), channel_id=1, replica_groups=mesh['y'=8,'z'=12,'row'=8] {'y'}, dimensions={0} | all-to-all | bytes 131072 | tf_op jit(solution)/shard_map/all_to_all | solution.py:397
  68.4 0.0 collective-permute-done.4.refs_3_.refs_4_
  68.4 0.5 shard_map.91.refs_9_
  68.9 1.9 %collective-permute-start.6 = (bf16[128,3584]{1,0:T(8,128)(2,1)S(1)}, bf16[128,3584]{1,0:T(8,128)(2,1)}, u32[]{:S(2)}, u32[]{:S(2)}) collective-permute-start(bf16[128,3584]{1,0:T(8,128)(2,1)S(1)} %shard_map.91.refs_9_), channel_id=1, source_target_pairs={{0,2},{1,767},{2,4},{3,1},{4,6},{5,3},{6,8},{7,5},{8,10},{9,7},{10... | collective-permute-start | bytes 2752520 | tf_op jit(solution)/shard_map/ppermute | solution.py:348
  70.8 0.0 collective-permute-done.5.refs_5_
  70.8 2.6 %shard_map.92 = (f32[128,3584]{1,0:T(8,128)S(1)}, bf16[128,3584]{1,0:T(8,128)(2,1)}) custom-call(bf16[128,3584]{1,0:T(8,128)(2,1)S(1)} %get-tuple-element.32.refs_3_.refs_2_.refs_4_.refs_0_, f32[128,128]{1,0:T(8,128)S(1)} %get-tuple-element.44.refs_1_, f32[128,128]{1,0:T(8,128)S(1)} %get-tuple-element.33.refs_2_.refs_9_, ...), custom_call_target="tpu_custom_call" | custom-call | flops 1000 | bytes 1000 | tf_op jit(solution)/shard_map/pallas_call | solution.py:45
  73.4 17.9 %all_to_all.16.refs_0_ = bf16[12,32,128]{2,1,0:T(8,128)(2,1)S(1)} all-to-all(bf16[12,32,128]{2,1,0:T(8,128)(2,1)S(1)} %shard_map.93), channel_id=1, replica_groups=mesh['y'=8,'z'=12,'row'=8] {'z'}, dimensions={0} | all-to-all | bytes 196608 | tf_op jit(solution)/shard_map/all_to_all | solution.py:397
  91.3 0.7 shard_map.94.refs_4_
  92.0 5.4 %all-to-all-start.2 = ((bf16[8,32,128]{2,1,0:T(8,128)(2,1)}), bf16[8,32,128]{2,1,0:T(8,128)(2,1)S(1)}, u32[]{:S(2)}, u32[]{:S(2)}) async-start(bf16[8,32,128]{2,1,0:T(8,128)(2,1)} %shard_map.94.refs_4_), calls=%async_computation.2 | async-start | bytes 131072 | tf_op jit(solution)/shard_map/all_to_all | solution.py:397
  97.4 0.0 collective-permute-done.6.refs_2_
  97.4 3.9 %shard_map.95.refs_1_ = bf16[128,3584]{1,0:T(8,128)(2,1)} custom-call(f32[1,3584]{1,0:T(1,128)S(1)} %get-tuple-element.31.refs_1_.refs_6_.refs_0_, f32[128,3584]{1,0:T(8,128)S(1)} %get-tuple-element.52.refs_1_, bf16[128,3584]{1,0:T(8,128)(2,1)} %collective-permute-done.6.refs_2_, bf16[128,3584]{1,0:T(8,128)(2,1)} %refs_3_.1, ...), custom_call_target="tpu_custom_call" | custom-call | flops 3000000000 | bytes 1000 | tf_op jit(solution)/shard_map/pallas_call | solution.py:45
  101.3 1.7 %all-to-all-done.2.refs_0_ = bf16[8,32,128]{2,1,0:T(8,128)(2,1)S(1)} async-done(((bf16[8,32,128]{2,1,0:T(8,128)(2,1)}), bf16[8,32,128]{2,1,0:T(8,128)(2,1)S(1)}, u32[]{:S(2)}, u32[]{:S(2)}) %all-to-all-start.2) | async-done | bytes 65568 | tf_op jit(solution)/shard_map/all_to_all | solution.py:397
  103.0 0.6 shard_map.96
  (1 shorter events, 0.0 us)
Async XLA Ops:
  0.6 32.0 %collective-permute-start = (bf16[128,3584]{1,0:T(8,128)(2,1)}, bf16[128,3584]{1,0:T(8,128)(2,1)S(1)}, u32[]{:S(2)}, u32[]{:S(2)}) collective-permute-start(bf16[128,3584]{1,0:T(8,128)(2,1)} %refs_3_.1), channel_id=1, source_target_pairs={{2,0},{767,1},{4,2},{1,3},{6,4},{3,5},{8,6},{5,7},{10,8},{7,9},{12... | collective-permute-start | bytes 2752520 | tf_op jit(solution)/shard_map/ppermute | solution.py:348
  19.0 16.0 %collective-permute-start.3 = (bf16[128,3584]{1,0:T(8,128)(2,1)S(1)}, bf16[128,3584]{1,0:T(8,128)(2,1)S(1)}, u32[]{:S(2)}, u32[]{:S(2)}) collective-permute-start(bf16[128,3584]{1,0:T(8,128)(2,1)S(1)} %get-tuple-element.30.refs_0_), channel_id=1, source_target_pairs={{0,1},{1,0},{2,3},{3,2},{4,5},{5,4},{6,7},{7,6},{8,9},{9,8},{10,11... | collective-permute-start | bytes 2752520 | tf_op jit(solution)/shard_map/ppermute | solution.py:348
  20.9 19.5 %collective-permute-start.2 = (bf16[128,3584]{1,0:T(8,128)(2,1)S(1)}, bf16[128,3584]{1,0:T(8,128)(2,1)S(1)}, u32[]{:S(2)}, u32[]{:S(2)}) collective-permute-start(bf16[128,3584]{1,0:T(8,128)(2,1)S(1)} %get-tuple-element.30.refs_0_), channel_id=1, source_target_pairs={{766,0},{3,1},{0,2},{5,3},{2,4},{7,5},{4,6},{9,7},{6,8},{11,9},{8,... | collective-permute-start | bytes 2752520 | tf_op jit(solution)/shard_map/ppermute | solution.py:348
  22.8 12.2 %copy-start = (s32[1,4]{1,0:T(1,128)S(1)}, s32[1,4]{1,0:T(1,128)}, u32[]{:S(2)}) copy-start(s32[1,4]{1,0:T(1,128)} %refs_0_.7) | copy-start | bytes 52
  33.1 8.3 %collective-permute-start.1 = (bf16[128,3584]{1,0:T(8,128)(2,1)S(1)}, bf16[128,3584]{1,0:T(8,128)(2,1)S(1)}, u32[]{:S(2)}, u32[]{:S(2)}) collective-permute-start(bf16[128,3584]{1,0:T(8,128)(2,1)S(1)} %shard_map.86.refs_2_), channel_id=1, source_target_pairs={{0,1},{1,0},{2,3},{3,2},{4,5},{5,4},{6,7},{7,6},{8,9},{9,8},{10,11... | collective-permute-start | bytes 2752520 | tf_op jit(solution)/shard_map/ppermute | solution.py:348
  44.7 23.7 %collective-permute-start.4 = (bf16[2,128,3584]{2,1,0:T(8,128)(2,1)S(1)}, bf16[2,128,3584]{2,1,0:T(8,128)(2,1)S(1)}, u32[]{:S(2)}, u32[]{:S(2)}) collective-permute-start(bf16[2,128,3584]{2,1,0:T(8,128)(2,1)S(1)} %get-tuple-element.49), channel_id=1, source_target_pairs={{0,1},{1,0},{2,3},{3,2},{4,5},{5,4},{6,7},{7,6},{8,9},{9,8},{10,11... | collective-permute-start | bytes 5505032 | tf_op jit(solution)/shard_map/ppermute | solution.py:348
  46.7 24.1 %collective-permute-start.5 = (bf16[128,3584]{1,0:T(8,128)(2,1)S(1)}, bf16[128,3584]{1,0:T(8,128)(2,1)S(1)}, u32[]{:S(2)}, u32[]{:S(2)}) collective-permute-start(bf16[128,3584]{1,0:T(8,128)(2,1)S(1)} %get-tuple-element.50), channel_id=1, source_target_pairs={{0,766},{1,3},{2,0},{3,5},{4,2},{5,7},{6,4},{7,9},{8,6},{9,11},{10... | collective-permute-start | bytes 2752520 | tf_op jit(solution)/shard_map/ppermute | solution.py:348
  68.9 28.5 %collective-permute-start.6 = (bf16[128,3584]{1,0:T(8,128)(2,1)S(1)}, bf16[128,3584]{1,0:T(8,128)(2,1)}, u32[]{:S(2)}, u32[]{:S(2)}) collective-permute-start(bf16[128,3584]{1,0:T(8,128)(2,1)S(1)} %shard_map.91.refs_9_), channel_id=1, source_target_pairs={{0,2},{1,767},{2,4},{3,1},{4,6},{5,3},{6,8},{7,5},{8,10},{9,7},{10... | collective-permute-start | bytes 2752520 | tf_op jit(solution)/shard_map/ppermute | solution.py:348
  92.0 11.0 %all-to-all-start.2 = ((bf16[8,32,128]{2,1,0:T(8,128)(2,1)}), bf16[8,32,128]{2,1,0:T(8,128)(2,1)S(1)}, u32[]{:S(2)}, u32[]{:S(2)}) async-start(bf16[8,32,128]{2,1,0:T(8,128)(2,1)} %shard_map.94.refs_4_), calls=%async_computation.2 | async-start | bytes 131072 | tf_op jit(solution)/shard_map/all_to_all | solution.py:397

commit v8 on v7

--- a/solution.py
+++ b/solution.py
@@ -119,7 +119,7 @@
 
 
 def own_kernel(
-    dn_ref, gain_ref, q_hbm, pos_hbm, qn_ref, s_ref, top_ref, total_ref, acc_ref, picked_ref, hot_ref, scaled_ref, q_ref, pos_ref, sems
+    dn_ref, gain_ref, q_hbm, pos_hbm, qn_ref, s_ref, top_ref, total_ref, acc_ref, picked_ref, hot_ref, scaled_ref, factor_ref, q_ref, pos_ref, sems
 ):
     copies = [pltpu.make_async_copy(q_hbm, q_ref, sems.at[0]), pltpu.make_async_copy(pos_hbm, pos_ref, sems.at[1])]
     for copy in copies:
@@ -129,7 +129,9 @@
     gain = gain_ref[...]
     for i in range(0, ROWS, STEP):
         values = q_ref[i : i + STEP, :].astype(f32)
-        scaled = values * factor_of(values)
+        factor = factor_of(values)
+        scaled = values * factor
+        factor_ref[i : i + STEP, :] = jnp.broadcast_to(factor, (STEP, LANES))
         scaled_ref[i : i + STEP, :] = scaled
         qn_ref[i : i + STEP, :] = (scaled * gain).astype(bf16)
     scores = scores_of(qn_ref[...], dn_ref[...])
@@ -244,24 +246,28 @@
 
 
 def home_kernel(
-    qn_ref, lse_ref, s_own_ref, hot_ref, near_ref, back_ref, gain_ref, gq_ref, q_hbm, own_ref, grad_hbm, q_ref, grad_ref, scaled_ref, sems
+    qn_ref, lse_ref, s_own_ref, hot_ref, near_ref, back_ref, gain_ref, gq_ref, scaled_ref, factor_ref,
+    own_ref, grad_hbm, grad_ref, sems,
 ):
-    incoming = pltpu.make_async_copy(q_hbm, q_ref, sems.at[PARTS])
-    incoming.start()
-    weight = turned(s_own_ref, lse_ref, hot_ref)
-    for c in range(0, WIDTH, CHUNK):
-        cols = slice(c, c + CHUNK)
-        term = jnp.dot(weight, qn_ref[:, cols], preferred_element_type=f32)
-        own_ref[:, cols] = term + near_ref[1, :, cols].astype(f32) + back_ref[:, cols].astype(f32)
-    incoming.wait()
-
-    def values_at(rows, cols):
-        return q_ref[rows, cols].astype(f32)
-
-    def cotangent_at(rows, cols):
-        return gq_ref[rows, cols]
-
-    send_parts(lambda rows: pull(values_at, cotangent_at, gain_ref, scaled_ref, grad_ref, rows), grad_ref, grad_hbm, sems)
+    def work(rows):
+        inner = jnp.zeros((STEP, CHUNK), f32)
+        chunks = [slice(c, c + CHUNK) for c in range(0, WIDTH, CHUNK)]
+        for cols in chunks:
+            inner = inner + scaled_ref[rows, cols] * (gain_ref[:, cols] * gq_ref[rows, cols])
+        inner = jnp.sum(inner, axis=-1, keepdims=True) / WIDTH
+        factor = factor_ref[rows, 0:1]
+        for cols in chunks:
+            grad = gain_ref[:, cols] * gq_ref[rows, cols] - scaled_ref[rows, cols] * inner
+            grad_ref[rows, cols] = (factor * grad).astype(bf16)
+
+    def terms():
+        weight = turned(s_own_ref, lse_ref, hot_ref)
+        for c in range(0, WIDTH, CHUNK):
+            cols = slice(c, c + CHUNK)
+            term = jnp.dot(weight, qn_ref[:, cols], preferred_element_type=f32)
+            own_ref[:, cols] = term + near_ref[1, :, cols].astype(f32) + back_ref[:, cols].astype(f32)
+
+    send_parts(work, grad_ref, grad_hbm, sems, terms)
 
 
 def grad_doc_kernel(gain_ref, own_ref, far_ref, d_hbm, grad_hbm, d_ref, grad_ref, scaled_ref, sems, in_sems):
@@ -286,7 +292,7 @@
     send_parts(work, grad_ref, grad_hbm, sems)
 
 
-def send_parts(work, out_ref, target, sems):
+def send_parts(work, out_ref, target, sems, meanwhile=None):
     outgoing = []
     for part in range(PARTS):
         for i in range(part * PART, (part + 1) * PART, STEP):
@@ -295,6 +301,8 @@
         copy = pltpu.make_async_copy(out_ref.at[rows, :], target.at[rows, :], sems.at[part])
         copy.start()
         outgoing.append(copy)
+    if meanwhile is not None:
+        meanwhile()
     for copy in outgoing:
         copy.wait()
 
@@ -361,10 +369,10 @@
     gain_line = kept(gain_line)
     back = permute(dn, [(back_source[i], i) for i in devices])
     swap = permute(dn, swap_route)
-    qn, s_own, *state, picked, hot, scaled = call(
+    qn, s_own, *state, picked, hot, scaled, factor = call(
         own_kernel,
         [held(block, bf16)] + [held(square, f32)] * 3 + [held(block, f32), held(block, bf16), held(square, f32)]
-        + [held(block, f32)],
+        + [held(block, f32), held(square, f32)],
         (kept(dn), gain_line),
         distant=(leave(query_hidden), leave(positives)),
         scratch=[pltpu.VMEM(block, bf16), pltpu.VMEM((1, ROWS), jnp.int32), dma((2,))],
@@ -414,10 +422,9 @@
     t_own, grad_query = call(
         home_kernel,
         [held(block, f32), distant_array(block, bf16)],
-        (qn, lse, s_own, hot, near_term, back_term, gain_line, kept(gq)),
-        distant=(leave(query_hidden),),
+        (qn, lse, s_own, hot, near_term, back_term, gain_line, kept(gq), kept(scaled), kept(factor)),
         after=(far_sum,),
-        scratch=[pltpu.VMEM(block, bf16), pltpu.VMEM(block, bf16), pltpu.VMEM((STEP, WIDTH), f32), dma((PARTS + 1,))],
+        scratch=[pltpu.VMEM(block, bf16), dma((PARTS,))],
     )
     part = summed(part, 1, after=(t_own,))
     ready = summed(exchange(part, 1), 2)

time: 104 us -> 103 us (level)
  no operation moved by 1% of the time
where the time goes in v8:
time: 103 us
  starting transfers between devices  37.9 us (37%)
  blocking collectives  33.4 us (32%)
  Pallas kernels  19 us (18%)
  waiting for transfers between devices  11.7 us (11%)
    all_to_all x2, blocking collectives, exchange(): return kept(lax.all_to_all(x, AXES[axis], 0, 0, tiled=True))  33.4 us
    ppermute x7, starting transfers between devices, permute(): return lax.ppermute(x, AXES, route)  32.5 us
    pallas_call x13, Pallas kernels, call(): pl.pallas_call(run, in_specs=[in_smem] * len(scalars) + [in_vmem] * len(a...  19 us
    ppermute x7, waiting for transfers between devices, permute(): return lax.ppermute(x, AXES, route)  9.99 us
    all_to_all x1, starting transfers between devices, exchange(): return kept(lax.all_to_all(x, AXES[axis], 0, 0, tiled=True))  5.4 us
  transfers between devices with their start and end apart: 8, of which 3 were waited for; matrix products, arithmetic and copies ran while one was open for 0% of the time, Pallas kernels for 15%

profile of v8, /device:TPU:8, one launch (start us, length us, event | category | flops | bytes accessed | tf_op | source)
XLA Modules:
  0.0 102.9 jit_solution(5481970656787356673)
XLA Ops:
  0.6 16.7 %collective-permute-start = (bf16[128,3584]{1,0:T(8,128)(2,1)}, bf16[128,3584]{1,0:T(8,128)(2,1)S(1)}, u32[]{:S(2)}, u32[]{:S(2)}) collective-permute-start(bf16[128,3584]{1,0:T(8,128)(2,1)} %refs_3_.1), channel_id=1, source_target_pairs={{2,0},{767,1},{4,2},{1,3},{6,4},{3,5},{8,6},{5,7},{10,8},{7,9},{12... | collective-permute-start | bytes 2752520 | tf_op jit(solution)/shard_map/ppermute | solution.py:356
  17.3 1.6 %shard_map.84 = (bf16[128,3584]{1,0:T(8,128)(2,1)S(1)}, f32[1,3584]{1,0:T(1,128)S(1)}) custom-call(bf16[128,3584]{1,0:T(8,128)(2,1)} %refs_3_.1, f32[28,128]{1,0:T(8,128)} %bitcast.4), custom_call_target="tpu_custom_call" | custom-call | flops 1000 | bytes 1000 | tf_op jit(solution)/shard_map/pallas_call | solution.py:45
  19.0 1.9 %collective-permute-start.3 = (bf16[128,3584]{1,0:T(8,128)(2,1)S(1)}, bf16[128,3584]{1,0:T(8,128)(2,1)S(1)}, u32[]{:S(2)}, u32[]{:S(2)}) collective-permute-start(bf16[128,3584]{1,0:T(8,128)(2,1)S(1)} %get-tuple-element.31.refs_0_), channel_id=1, source_target_pairs={{0,1},{1,0},{2,3},{3,2},{4,5},{5,4},{6,7},{7,6},{8,9},{9,8},{10,11... | collective-permute-start | bytes 2752520 | tf_op jit(solution)/shard_map/ppermute | solution.py:356
  20.9 1.9 %collective-permute-start.2 = (bf16[128,3584]{1,0:T(8,128)(2,1)S(1)}, bf16[128,3584]{1,0:T(8,128)(2,1)S(1)}, u32[]{:S(2)}, u32[]{:S(2)}) collective-permute-start(bf16[128,3584]{1,0:T(8,128)(2,1)S(1)} %get-tuple-element.31.refs_0_), channel_id=1, source_target_pairs={{766,0},{3,1},{0,2},{5,3},{2,4},{7,5},{4,6},{9,7},{6,8},{11,9},{8,... | collective-permute-start | bytes 2752520 | tf_op jit(solution)/shard_map/ppermute | solution.py:356
  22.8 0.0 copy-start
  22.8 3.0 %shard_map.85 = (bf16[128,3584]{1,0:T(8,128)(2,1)S(1)}, f32[128,128]{1,0:T(8,128)S(1)}, f32[128,128]{1,0:T(8,128)S(1)}, f32[128,128]{1,0:T(8,128)S(1)}, f32[128,...) custom-call(bf16[128,3584]{1,0:T(8,128)(2,1)S(1)} %get-tuple-element, ...), custom_call_target="tpu_custom_call" | custom-call | flops 1000 | bytes 1000 | tf_op jit(solution)/shard_map/pallas_call | solution.py:45
  25.9 6.8 %collective-permute-done.refs_0_ = bf16[128,3584]{1,0:T(8,128)(2,1)S(1)} collective-permute-done((bf16[128,3584]{1,0:T(8,128)(2,1)}, bf16[128,3584]{1,0:T(8,128)(2,1)S(1)}, u32[]{:S(2)}, u32[]{:S(2)}) %collective-permute-start) | collective-permute-done | bytes 917536 | tf_op jit(solution)/shard_map/ppermute | solution.py:356
  32.6 0.4 shard_map.86.refs_2_
  33.1 1.9 %collective-permute-start.1 = (bf16[128,3584]{1,0:T(8,128)(2,1)S(1)}, bf16[128,3584]{1,0:T(8,128)(2,1)S(1)}, u32[]{:S(2)}, u32[]{:S(2)}) collective-permute-start(bf16[128,3584]{1,0:T(8,128)(2,1)S(1)} %shard_map.86.refs_2_), channel_id=1, source_target_pairs={{0,1},{1,0},{2,3},{3,2},{4,5},{5,4},{6,7},{7,6},{8,9},{9,8},{10,11... | collective-permute-start | bytes 2752520 | tf_op jit(solution)/shard_map/ppermute | solution.py:356
  35.0 0.0 collective-permute-done.3.refs_1_
  35.0 0.0 copy-done
  35.0 2.2 %shard_map.87 = (f32[128,128]{1,0:T(8,128)S(1)}, f32[128,128]{1,0:T(8,128)S(1)}, f32[128,128]{1,0:T(8,128)S(1)}, f32[128,128]{1,0:T(8,128)S(1)}, f32[128,3584]{1,0:T(8,128)S(1)}) custom-call(s32[1,4]{1,0:T(1,128)S(1)} %copy-done, bf16[128,3584]{1,0:T(8,128)(2,1)S(1)} %collective-permute-done.3.refs_1_, ...), custom_call_target="tpu_custom_call", output_to_operand_aliasing={{2}: (4, {}), {3}: (5, {}), {4}: (6, {})} | custom-call | flops 1000 | bytes 1000 | tf_op jit(solution)/shard_map/pallas_call | solution.py:45
  37.2 3.2 %collective-permute-done.2.refs_1_.refs_2_ = bf16[128,3584]{1,0:T(8,128)(2,1)S(1)} collective-permute-done((bf16[128,3584]{1,0:T(8,128)(2,1)S(1)}, bf16[128,3584]{1,0:T(8,128)(2,1)S(1)}, u32[]{:S(2)}, u32[]{:S(2)}) %collective-permute-start.2) | collective-permute-done | bytes 917536 | tf_op jit(solution)/shard_map/ppermute | solution.py:356
  40.4 0.9 shard_map.88.refs_3_.refs_4_
  41.3 0.0 collective-permute-done.1.refs_1_
  41.3 2.5 %shard_map.89 = (f32[128,128]{1,0:T(8,128)S(1)}, f32[128,128]{1,0:T(8,128)S(1)}, f32[128,3584]{1,0:T(8,128)S(1)}, f32[32,128]{1,0:T(8,128)S(1)}) custom-call(s32[1,4]{1,0:T(1,128)S(1)} %copy-done, bf16[128,3584]{1,0:T(8,128)(2,1)S(1)} %collective-permute-done.1.refs_1_, ...), custom_call_target="tpu_custom_call", output_to_operand_aliasing={{2}: (7, {})} | custom-call | flops 1000 | bytes 1000 | tf_op jit(solution)/shard_map/pallas_call | solution.py:45
  43.8 0.9 shard_map.90
  44.8 1.9 %collective-permute-start.4 = (bf16[2,128,3584]{2,1,0:T(8,128)(2,1)S(1)}, bf16[2,128,3584]{2,1,0:T(8,128)(2,1)S(1)}, u32[]{:S(2)}, u32[]{:S(2)}) collective-permute-start(bf16[2,128,3584]{2,1,0:T(8,128)(2,1)S(1)} %get-tuple-element.50), channel_id=1, source_target_pairs={{0,1},{1,0},{2,3},{3,2},{4,5},{5,4},{6,7},{7,6},{8,9},{9,8},{10,11... | collective-permute-start | bytes 5505032 | tf_op jit(solution)/shard_map/ppermute | solution.py:356
  46.7 6.3 %collective-permute-start.5 = (bf16[128,3584]{1,0:T(8,128)(2,1)S(1)}, bf16[128,3584]{1,0:T(8,128)(2,1)S(1)}, u32[]{:S(2)}, u32[]{:S(2)}) collective-permute-start(bf16[128,3584]{1,0:T(8,128)(2,1)S(1)} %get-tuple-element.51), channel_id=1, source_target_pairs={{0,766},{1,3},{2,0},{3,5},{4,2},{5,7},{6,4},{7,9},{8,6},{9,11},{10... | collective-permute-start | bytes 2752520 | tf_op jit(solution)/shard_map/ppermute | solution.py:356
  53.0 15.5 %all_to_all.15.refs_4_.refs_0_ = bf16[8,32,128]{2,1,0:T(8,128)(2,1)S(1)} all-to-all(bf16[8,32,128]{2,1,0:T(8,128)(2,1)S(1)} %get-tuple-element.49), channel_id=1, replica_groups=mesh['y'=8,'z'=12,'row'=8] {'y'}, dimensions={0} | all-to-all | bytes 131072 | tf_op jit(solution)/shard_map/all_to_all | solution.py:405
  68.4 0.0 collective-permute-done.4.refs_3_.refs_4_
  68.4 0.5 shard_map.91.refs_10_
  68.9 1.9 %collective-permute-start.6 = (bf16[128,3584]{1,0:T(8,128)(2,1)S(1)}, bf16[128,3584]{1,0:T(8,128)(2,1)}, u32[]{:S(2)}, u32[]{:S(2)}) collective-permute-start(bf16[128,3584]{1,0:T(8,128)(2,1)S(1)} %shard_map.91.refs_10_), channel_id=1, source_target_pairs={{0,2},{1,767},{2,4},{3,1},{4,6},{5,3},{6,8},{7,5},{8,10},{9,7},{10... | collective-permute-start | bytes 2752520 | tf_op jit(solution)/shard_map/ppermute | solution.py:356
  70.8 0.0 collective-permute-done.5.refs_5_
  70.8 1.8 %shard_map.92 = (f32[128,3584]{1,0:T(8,128)S(1)}, bf16[128,3584]{1,0:T(8,128)(2,1)}) custom-call(bf16[128,3584]{1,0:T(8,128)(2,1)S(1)} %get-tuple-element.33.refs_3_.refs_2_.refs_4_.refs_0_, f32[128,128]{1,0:T(8,128)S(1)} %get-tuple-element.45.refs_1_, f32[128,128]{1,0:T(8,128)S(1)} %get-tuple-element.34.refs_2_.refs_9_, ...), custom_call_target="tpu_custom_call" | custom-call | flops 1000 | bytes 1000 | tf_op jit(solution)/shard_map/pallas_call | solution.py:45
  72.7 17.9 %all_to_all.16.refs_0_ = bf16[12,32,128]{2,1,0:T(8,128)(2,1)S(1)} all-to-all(bf16[12,32,128]{2,1,0:T(8,128)(2,1)S(1)} %shard_map.93), channel_id=1, replica_groups=mesh['y'=8,'z'=12,'row'=8] {'z'}, dimensions={0} | all-to-all | bytes 196608 | tf_op jit(solution)/shard_map/all_to_all | solution.py:405
  90.6 0.7 shard_map.94.refs_4_
  91.2 5.4 %all-to-all-start.2 = ((bf16[8,32,128]{2,1,0:T(8,128)(2,1)}), bf16[8,32,128]{2,1,0:T(8,128)(2,1)S(1)}, u32[]{:S(2)}, u32[]{:S(2)}) async-start(bf16[8,32,128]{2,1,0:T(8,128)(2,1)} %shard_map.94.refs_4_), calls=%async_computation.2 | async-start | bytes 131072 | tf_op jit(solution)/shard_map/all_to_all | solution.py:405
  96.6 0.0 collective-permute-done.6.refs_2_
  96.7 3.9 %shard_map.95.refs_1_ = bf16[128,3584]{1,0:T(8,128)(2,1)} custom-call(f32[1,3584]{1,0:T(1,128)S(1)} %get-tuple-element.32.refs_1_.refs_6_.refs_0_, f32[128,3584]{1,0:T(8,128)S(1)} %get-tuple-element.54.refs_1_, bf16[128,3584]{1,0:T(8,128)(2,1)} %collective-permute-done.6.refs_2_, bf16[128,3584]{1,0:T(8,128)(2,1)} %refs_3_.1, ...), custom_call_target="tpu_custom_call" | custom-call | flops 3000000000 | bytes 1000 | tf_op jit(solution)/shard_map/pallas_call | solution.py:45
  100.6 1.7 %all-to-all-done.2.refs_0_ = bf16[8,32,128]{2,1,0:T(8,128)(2,1)S(1)} async-done(((bf16[8,32,128]{2,1,0:T(8,128)(2,1)}), bf16[8,32,128]{2,1,0:T(8,128)(2,1)S(1)}, u32[]{:S(2)}, u32[]{:S(2)}) %all-to-all-start.2) | async-done | bytes 65568 | tf_op jit(solution)/shard_map/all_to_all | solution.py:405
  102.3 0.6 shard_map.96
  (1 shorter events, 0.0 us)
Async XLA Ops:
  0.6 32.0 %collective-permute-start = (bf16[128,3584]{1,0:T(8,128)(2,1)}, bf16[128,3584]{1,0:T(8,128)(2,1)S(1)}, u32[]{:S(2)}, u32[]{:S(2)}) collective-permute-start(bf16[128,3584]{1,0:T(8,128)(2,1)} %refs_3_.1), channel_id=1, source_target_pairs={{2,0},{767,1},{4,2},{1,3},{6,4},{3,5},{8,6},{5,7},{10,8},{7,9},{12... | collective-permute-start | bytes 2752520 | tf_op jit(solution)/shard_map/ppermute | solution.py:356
  19.0 16.0 %collective-permute-start.3 = (bf16[128,3584]{1,0:T(8,128)(2,1)S(1)}, bf16[128,3584]{1,0:T(8,128)(2,1)S(1)}, u32[]{:S(2)}, u32[]{:S(2)}) collective-permute-start(bf16[128,3584]{1,0:T(8,128)(2,1)S(1)} %get-tuple-element.31.refs_0_), channel_id=1, source_target_pairs={{0,1},{1,0},{2,3},{3,2},{4,5},{5,4},{6,7},{7,6},{8,9},{9,8},{10,11... | collective-permute-start | bytes 2752520 | tf_op jit(solution)/shard_map/ppermute | solution.py:356
  20.9 19.5 %collective-permute-start.2 = (bf16[128,3584]{1,0:T(8,128)(2,1)S(1)}, bf16[128,3584]{1,0:T(8,128)(2,1)S(1)}, u32[]{:S(2)}, u32[]{:S(2)}) collective-permute-start(bf16[128,3584]{1,0:T(8,128)(2,1)S(1)} %get-tuple-element.31.refs_0_), channel_id=1, source_target_pairs={{766,0},{3,1},{0,2},{5,3},{2,4},{7,5},{4,6},{9,7},{6,8},{11,9},{8,... | collective-permute-start | bytes 2752520 | tf_op jit(solution)/shard_map/ppermute | solution.py:356
  22.8 12.2 %copy-start = (s32[1,4]{1,0:T(1,128)S(1)}, s32[1,4]{1,0:T(1,128)}, u32[]{:S(2)}) copy-start(s32[1,4]{1,0:T(1,128)} %refs_0_.7) | copy-start | bytes 52
  33.1 8.3 %collective-permute-start.1 = (bf16[128,3584]{1,0:T(8,128)(2,1)S(1)}, bf16[128,3584]{1,0:T(8,128)(2,1)S(1)}, u32[]{:S(2)}, u32[]{:S(2)}) collective-permute-start(bf16[128,3584]{1,0:T(8,128)(2,1)S(1)} %shard_map.86.refs_2_), channel_id=1, source_target_pairs={{0,1},{1,0},{2,3},{3,2},{4,5},{5,4},{6,7},{7,6},{8,9},{9,8},{10,11... | collective-permute-start | bytes 2752520 | tf_op jit(solution)/shard_map/ppermute | solution.py:356
  44.8 23.7 %collective-permute-start.4 = (bf16[2,128,3584]{2,1,0:T(8,128)(2,1)S(1)}, bf16[2,128,3584]{2,1,0:T(8,128)(2,1)S(1)}, u32[]{:S(2)}, u32[]{:S(2)}) collective-permute-start(bf16[2,128,3584]{2,1,0:T(8,128)(2,1)S(1)} %get-tuple-element.50), channel_id=1, source_target_pairs={{0,1},{1,0},{2,3},{3,2},{4,5},{5,4},{6,7},{7,6},{8,9},{9,8},{10,11... | collective-permute-start | bytes 5505032 | tf_op jit(solution)/shard_map/ppermute | solution.py:356
  46.7 24.1 %collective-permute-start.5 = (bf16[128,3584]{1,0:T(8,128)(2,1)S(1)}, bf16[128,3584]{1,0:T(8,128)(2,1)S(1)}, u32[]{:S(2)}, u32[]{:S(2)}) collective-permute-start(bf16[128,3584]{1,0:T(8,128)(2,1)S(1)} %get-tuple-element.51), channel_id=1, source_target_pairs={{0,766},{1,3},{2,0},{3,5},{4,2},{5,7},{6,4},{7,9},{8,6},{9,11},{10... | collective-permute-start | bytes 2752520 | tf_op jit(solution)/shard_map/ppermute | solution.py:356
  68.9 27.8 %collective-permute-start.6 = (bf16[128,3584]{1,0:T(8,128)(2,1)S(1)}, bf16[128,3584]{1,0:T(8,128)(2,1)}, u32[]{:S(2)}, u32[]{:S(2)}) collective-permute-start(bf16[128,3584]{1,0:T(8,128)(2,1)S(1)} %shard_map.91.refs_10_), channel_id=1, source_target_pairs={{0,2},{1,767},{2,4},{3,1},{4,6},{5,3},{6,8},{7,5},{8,10},{9,7},{10... | collective-permute-start | bytes 2752520 | tf_op jit(solution)/shard_map/ppermute | solution.py:356
  91.2 11.0 %all-to-all-start.2 = ((bf16[8,32,128]{2,1,0:T(8,128)(2,1)}), bf16[8,32,128]{2,1,0:T(8,128)(2,1)S(1)}, u32[]{:S(2)}, u32[]{:S(2)}) async-start(bf16[8,32,128]{2,1,0:T(8,128)(2,1)} %shard_map.94.refs_4_), calls=%async_computation.2 | async-start | bytes 131072 | tf_op jit(solution)/shard_map/all_to_all | solution.py:405

commit v9 on v8

--- a/solution.py
+++ b/solution.py
@@ -270,13 +270,14 @@
     send_parts(work, grad_ref, grad_hbm, sems, terms)
 
 
-def grad_doc_kernel(gain_ref, own_ref, far_ref, d_hbm, grad_hbm, d_ref, grad_ref, scaled_ref, sems, in_sems):
+def grad_doc_kernel(gain_ref, own_ref, far_hbm, d_hbm, grad_hbm, d_ref, far_ref, grad_ref, scaled_ref, sems, in_sems):
     incoming = []
     for part in range(PARTS):
         rows = pl.ds(part * PART, PART)
-        copy = pltpu.make_async_copy(d_hbm.at[rows, :], d_ref.at[rows, :], in_sems.at[part])
-        copy.start()
-        incoming.append(copy)
+        for k, (source, target) in enumerate(((d_hbm, d_ref), (far_hbm, far_ref))):
+            copy = pltpu.make_async_copy(source.at[rows, :], target.at[rows, :], in_sems.at[k, part])
+            copy.start()
+            incoming.append(copy)
 
     def values_at(rows, cols):
         return d_ref[rows, cols].astype(f32)
@@ -286,7 +287,8 @@
 
     def work(rows):
         if rows.start % PART == 0:
-            incoming[rows.start // PART].wait()
+            incoming[2 * (rows.start // PART)].wait()
+            incoming[2 * (rows.start // PART) + 1].wait()
         pull(values_at, cotangent_at, gain_ref, scaled_ref, grad_ref, rows)
 
     send_parts(work, grad_ref, grad_hbm, sems)
@@ -432,11 +434,12 @@
     grad_doc = call(
         grad_doc_kernel,
         distant_array(block, bf16),
-        (gain_line, kept(t_own), far_term),
-        distant=(leave(doc_hidden),),
+        (gain_line, kept(t_own)),
+        distant=(far_term, leave(doc_hidden)),
         after=(ready,),
         scratch=[
-            pltpu.VMEM(block, bf16), pltpu.VMEM(block, bf16), pltpu.VMEM((STEP, WIDTH), f32), dma((PARTS,)), dma((PARTS,))
+            pltpu.VMEM(block, bf16), pltpu.VMEM(block, bf16), pltpu.VMEM(block, bf16), pltpu.VMEM((STEP, WIDTH), f32),
+            dma((PARTS,)), dma((2, PARTS)),
         ],
         flops=3_000_000_000,
     )

time: 103 us -> 103 us (level)
  transfers between devices with their start and end apart: 8 -> 8, of which waited for: 3 -> 3; matrix products, arithmetic and copies ran while one was open for 0% -> 0% of each run, Pallas kernels for 15% -> 14%
where the time goes in v9:
time: 103 us
  starting transfers between devices  37.9 us (37%)
  blocking collectives  33.4 us (32%)
  Pallas kernels  18 us (17%)
  waiting for transfers between devices  12.7 us (12%)
    all_to_all x2, blocking collectives, exchange(): return kept(lax.all_to_all(x, AXES[axis], 0, 0, tiled=True))  33.4 us
    ppermute x7, starting transfers between devices, permute(): return lax.ppermute(x, AXES, route)  32.5 us
    pallas_call x13, Pallas kernels, call(): pl.pallas_call(run, in_specs=[in_smem] * len(scalars) + [in_vmem] * len(a...  18 us
    ppermute x7, waiting for transfers between devices, permute(): return lax.ppermute(x, AXES, route)  9.99 us
    all_to_all x1, starting transfers between devices, exchange(): return kept(lax.all_to_all(x, AXES[axis], 0, 0, tiled=True))  5.4 us
    all_to_all x1, waiting for transfers between devices, exchange(): return kept(lax.all_to_all(x, AXES[axis], 0, 0, tiled=True))  2.74 us
  transfers between devices with their start and end apart: 8, of which 3 were waited for; matrix products, arithmetic and copies ran while one was open for 0% of the time, Pallas kernels for 14%

profile of v9, /device:TPU:8, one launch (start us, length us, event | category | flops | bytes accessed | tf_op | source)
XLA Modules:
  0.0 102.9 jit_solution(11619905629008491046)
XLA Ops:
  0.6 16.7 %collective-permute-start = (bf16[128,3584]{1,0:T(8,128)(2,1)}, bf16[128,3584]{1,0:T(8,128)(2,1)S(1)}, u32[]{:S(2)}, u32[]{:S(2)}) collective-permute-start(bf16[128,3584]{1,0:T(8,128)(2,1)} %refs_3_.1), channel_id=1, source_target_pairs={{2,0},{767,1},{4,2},{1,3},{6,4},{3,5},{8,6},{5,7},{10,8},{7,9},{12... | collective-permute-start | bytes 2752520 | tf_op jit(solution)/shard_map/ppermute | solution.py:358
  17.3 1.6 %shard_map.84 = (bf16[128,3584]{1,0:T(8,128)(2,1)S(1)}, f32[1,3584]{1,0:T(1,128)S(1)}) custom-call(bf16[128,3584]{1,0:T(8,128)(2,1)} %refs_3_.1, f32[28,128]{1,0:T(8,128)} %bitcast.4), custom_call_target="tpu_custom_call" | custom-call | flops 1000 | bytes 1000 | tf_op jit(solution)/shard_map/pallas_call | solution.py:45
  19.0 1.9 %collective-permute-start.3 = (bf16[128,3584]{1,0:T(8,128)(2,1)S(1)}, bf16[128,3584]{1,0:T(8,128)(2,1)S(1)}, u32[]{:S(2)}, u32[]{:S(2)}) collective-permute-start(bf16[128,3584]{1,0:T(8,128)(2,1)S(1)} %get-tuple-element.31.refs_0_), channel_id=1, source_target_pairs={{0,1},{1,0},{2,3},{3,2},{4,5},{5,4},{6,7},{7,6},{8,9},{9,8},{10,11... | collective-permute-start | bytes 2752520 | tf_op jit(solution)/shard_map/ppermute | solution.py:358
  20.9 1.9 %collective-permute-start.2 = (bf16[128,3584]{1,0:T(8,128)(2,1)S(1)}, bf16[128,3584]{1,0:T(8,128)(2,1)S(1)}, u32[]{:S(2)}, u32[]{:S(2)}) collective-permute-start(bf16[128,3584]{1,0:T(8,128)(2,1)S(1)} %get-tuple-element.31.refs_0_), channel_id=1, source_target_pairs={{766,0},{3,1},{0,2},{5,3},{2,4},{7,5},{4,6},{9,7},{6,8},{11,9},{8,... | collective-permute-start | bytes 2752520 | tf_op jit(solution)/shard_map/ppermute | solution.py:358
  22.8 0.0 copy-start
  22.8 3.0 %shard_map.85 = (bf16[128,3584]{1,0:T(8,128)(2,1)S(1)}, f32[128,128]{1,0:T(8,128)S(1)}, f32[128,128]{1,0:T(8,128)S(1)}, f32[128,128]{1,0:T(8,128)S(1)}, f32[128,...) custom-call(bf16[128,3584]{1,0:T(8,128)(2,1)S(1)} %get-tuple-element, ...), custom_call_target="tpu_custom_call" | custom-call | flops 1000 | bytes 1000 | tf_op jit(solution)/shard_map/pallas_call | solution.py:45
  25.9 6.8 %collective-permute-done.refs_0_ = bf16[128,3584]{1,0:T(8,128)(2,1)S(1)} collective-permute-done((bf16[128,3584]{1,0:T(8,128)(2,1)}, bf16[128,3584]{1,0:T(8,128)(2,1)S(1)}, u32[]{:S(2)}, u32[]{:S(2)}) %collective-permute-start) | collective-permute-done | bytes 917536 | tf_op jit(solution)/shard_map/ppermute | solution.py:358
  32.6 0.4 shard_map.86.refs_2_
  33.1 1.9 %collective-permute-start.1 = (bf16[128,3584]{1,0:T(8,128)(2,1)S(1)}, bf16[128,3584]{1,0:T(8,128)(2,1)S(1)}, u32[]{:S(2)}, u32[]{:S(2)}) collective-permute-start(bf16[128,3584]{1,0:T(8,128)(2,1)S(1)} %shard_map.86.refs_2_), channel_id=1, source_target_pairs={{0,1},{1,0},{2,3},{3,2},{4,5},{5,4},{6,7},{7,6},{8,9},{9,8},{10,11... | collective-permute-start | bytes 2752520 | tf_op jit(solution)/shard_map/ppermute | solution.py:358
  35.0 0.0 collective-permute-done.3.refs_1_
  35.0 0.0 copy-done
  35.0 2.2 %shard_map.87 = (f32[128,128]{1,0:T(8,128)S(1)}, f32[128,128]{1,0:T(8,128)S(1)}, f32[128,128]{1,0:T(8,128)S(1)}, f32[128,128]{1,0:T(8,128)S(1)}, f32[128,3584]{1,0:T(8,128)S(1)}) custom-call(s32[1,4]{1,0:T(1,128)S(1)} %copy-done, bf16[128,3584]{1,0:T(8,128)(2,1)S(1)} %collective-permute-done.3.refs_1_, ...), custom_call_target="tpu_custom_call", output_to_operand_aliasing={{2}: (4, {}), {3}: (5, {}), {4}: (6, {})} | custom-call | flops 1000 | bytes 1000 | tf_op jit(solution)/shard_map/pallas_call | solution.py:45
  37.2 3.2 %collective-permute-done.2.refs_1_.refs_2_ = bf16[128,3584]{1,0:T(8,128)(2,1)S(1)} collective-permute-done((bf16[128,3584]{1,0:T(8,128)(2,1)S(1)}, bf16[128,3584]{1,0:T(8,128)(2,1)S(1)}, u32[]{:S(2)}, u32[]{:S(2)}) %collective-permute-start.2) | collective-permute-done | bytes 917536 | tf_op jit(solution)/shard_map/ppermute | solution.py:358
  40.4 0.9 shard_map.88.refs_3_.refs_4_
  41.3 0.0 collective-permute-done.1.refs_1_
  41.3 2.5 %shard_map.89 = (f32[128,128]{1,0:T(8,128)S(1)}, f32[128,128]{1,0:T(8,128)S(1)}, f32[128,3584]{1,0:T(8,128)S(1)}, f32[32,128]{1,0:T(8,128)S(1)}) custom-call(s32[1,4]{1,0:T(1,128)S(1)} %copy-done, bf16[128,3584]{1,0:T(8,128)(2,1)S(1)} %collective-permute-done.1.refs_1_, ...), custom_call_target="tpu_custom_call", output_to_operand_aliasing={{2}: (7, {})} | custom-call | flops 1000 | bytes 1000 | tf_op jit(solution)/shard_map/pallas_call | solution.py:45
  43.8 0.9 shard_map.90
  44.8 1.9 %collective-permute-start.4 = (bf16[2,128,3584]{2,1,0:T(8,128)(2,1)S(1)}, bf16[2,128,3584]{2,1,0:T(8,128)(2,1)S(1)}, u32[]{:S(2)}, u32[]{:S(2)}) collective-permute-start(bf16[2,128,3584]{2,1,0:T(8,128)(2,1)S(1)} %get-tuple-element.50), channel_id=1, source_target_pairs={{0,1},{1,0},{2,3},{3,2},{4,5},{5,4},{6,7},{7,6},{8,9},{9,8},{10,11... | collective-permute-start | bytes 5505032 | tf_op jit(solution)/shard_map/ppermute | solution.py:358
  46.7 6.3 %collective-permute-start.5 = (bf16[128,3584]{1,0:T(8,128)(2,1)S(1)}, bf16[128,3584]{1,0:T(8,128)(2,1)S(1)}, u32[]{:S(2)}, u32[]{:S(2)}) collective-permute-start(bf16[128,3584]{1,0:T(8,128)(2,1)S(1)} %get-tuple-element.51), channel_id=1, source_target_pairs={{0,766},{1,3},{2,0},{3,5},{4,2},{5,7},{6,4},{7,9},{8,6},{9,11},{10... | collective-permute-start | bytes 2752520 | tf_op jit(solution)/shard_map/ppermute | solution.py:358
  53.0 15.5 %all_to_all.15.refs_4_.refs_0_ = bf16[8,32,128]{2,1,0:T(8,128)(2,1)S(1)} all-to-all(bf16[8,32,128]{2,1,0:T(8,128)(2,1)S(1)} %get-tuple-element.49), channel_id=1, replica_groups=mesh['y'=8,'z'=12,'row'=8] {'y'}, dimensions={0} | all-to-all | bytes 131072 | tf_op jit(solution)/shard_map/all_to_all | solution.py:407
  68.4 0.0 collective-permute-done.4.refs_3_.refs_4_
  68.4 0.5 shard_map.91.refs_10_
  68.9 1.9 %collective-permute-start.6 = (bf16[128,3584]{1,0:T(8,128)(2,1)S(1)}, bf16[128,3584]{1,0:T(8,128)(2,1)}, u32[]{:S(2)}, u32[]{:S(2)}) collective-permute-start(bf16[128,3584]{1,0:T(8,128)(2,1)S(1)} %shard_map.91.refs_10_), channel_id=1, source_target_pairs={{0,2},{1,767},{2,4},{3,1},{4,6},{5,3},{6,8},{7,5},{8,10},{9,7},{10... | collective-permute-start | bytes 2752520 | tf_op jit(solution)/shard_map/ppermute | solution.py:358
  70.8 0.0 collective-permute-done.5.refs_5_
  70.8 1.8 %shard_map.92 = (f32[128,3584]{1,0:T(8,128)S(1)}, bf16[128,3584]{1,0:T(8,128)(2,1)}) custom-call(bf16[128,3584]{1,0:T(8,128)(2,1)S(1)} %get-tuple-element.33.refs_3_.refs_2_.refs_4_.refs_0_, f32[128,128]{1,0:T(8,128)S(1)} %get-tuple-element.45.refs_1_, f32[128,128]{1,0:T(8,128)S(1)} %get-tuple-element.34.refs_2_.refs_9_, ...), custom_call_target="tpu_custom_call" | custom-call | flops 1000 | bytes 1000 | tf_op jit(solution)/shard_map/pallas_call | solution.py:45
  72.7 17.9 %all_to_all.16.refs_0_ = bf16[12,32,128]{2,1,0:T(8,128)(2,1)S(1)} all-to-all(bf16[12,32,128]{2,1,0:T(8,128)(2,1)S(1)} %shard_map.93), channel_id=1, replica_groups=mesh['y'=8,'z'=12,'row'=8] {'z'}, dimensions={0} | all-to-all | bytes 196608 | tf_op jit(solution)/shard_map/all_to_all | solution.py:407
  90.6 0.7 shard_map.94.refs_4_
  91.2 5.4 %all-to-all-start.2 = ((bf16[8,32,128]{2,1,0:T(8,128)(2,1)}), bf16[8,32,128]{2,1,0:T(8,128)(2,1)S(1)}, u32[]{:S(2)}, u32[]{:S(2)}) async-start(bf16[8,32,128]{2,1,0:T(8,128)(2,1)} %shard_map.94.refs_4_), calls=%async_computation.2 | async-start | bytes 131072 | tf_op jit(solution)/shard_map/all_to_all | solution.py:407
  96.6 0.0 collective-permute-done.6.refs_2_
  96.7 2.9 %shard_map.95.refs_1_ = bf16[128,3584]{1,0:T(8,128)(2,1)} custom-call(f32[1,3584]{1,0:T(1,128)S(1)} %get-tuple-element.32.refs_1_.refs_6_.refs_0_, f32[128,3584]{1,0:T(8,128)S(1)} %get-tuple-element.54.refs_1_, bf16[128,3584]{1,0:T(8,128)(2,1)} %collective-permute-done.6.refs_2_, bf16[128,3584]{1,0:T(8,128)(2,1)} %refs_3_.1, ...), custom_call_target="tpu_custom_call" | custom-call | flops 3000000000 | bytes 1000 | tf_op jit(solution)/shard_map/pallas_call | solution.py:45
  99.5 2.7 %all-to-all-done.2.refs_0_ = bf16[8,32,128]{2,1,0:T(8,128)(2,1)S(1)} async-done(((bf16[8,32,128]{2,1,0:T(8,128)(2,1)}), bf16[8,32,128]{2,1,0:T(8,128)(2,1)S(1)}, u32[]{:S(2)}, u32[]{:S(2)}) %all-to-all-start.2) | async-done | bytes 65568 | tf_op jit(solution)/shard_map/all_to_all | solution.py:407
  102.3 0.6 shard_map.96
  (1 shorter events, 0.0 us)
Async XLA Ops:
  0.6 32.0 %collective-permute-start = (bf16[128,3584]{1,0:T(8,128)(2,1)}, bf16[128,3584]{1,0:T(8,128)(2,1)S(1)}, u32[]{:S(2)}, u32[]{:S(2)}) collective-permute-start(bf16[128,3584]{1,0:T(8,128)(2,1)} %refs_3_.1), channel_id=1, source_target_pairs={{2,0},{767,1},{4,2},{1,3},{6,4},{3,5},{8,6},{5,7},{10,8},{7,9},{12... | collective-permute-start | bytes 2752520 | tf_op jit(solution)/shard_map/ppermute | solution.py:358
  19.0 16.0 %collective-permute-start.3 = (bf16[128,3584]{1,0:T(8,128)(2,1)S(1)}, bf16[128,3584]{1,0:T(8,128)(2,1)S(1)}, u32[]{:S(2)}, u32[]{:S(2)}) collective-permute-start(bf16[128,3584]{1,0:T(8,128)(2,1)S(1)} %get-tuple-element.31.refs_0_), channel_id=1, source_target_pairs={{0,1},{1,0},{2,3},{3,2},{4,5},{5,4},{6,7},{7,6},{8,9},{9,8},{10,11... | collective-permute-start | bytes 2752520 | tf_op jit(solution)/shard_map/ppermute | solution.py:358
  20.9 19.5 %collective-permute-start.2 = (bf16[128,3584]{1,0:T(8,128)(2,1)S(1)}, bf16[128,3584]{1,0:T(8,128)(2,1)S(1)}, u32[]{:S(2)}, u32[]{:S(2)}) collective-permute-start(bf16[128,3584]{1,0:T(8,128)(2,1)S(1)} %get-tuple-element.31.refs_0_), channel_id=1, source_target_pairs={{766,0},{3,1},{0,2},{5,3},{2,4},{7,5},{4,6},{9,7},{6,8},{11,9},{8,... | collective-permute-start | bytes 2752520 | tf_op jit(solution)/shard_map/ppermute | solution.py:358
  22.8 12.2 %copy-start = (s32[1,4]{1,0:T(1,128)S(1)}, s32[1,4]{1,0:T(1,128)}, u32[]{:S(2)}) copy-start(s32[1,4]{1,0:T(1,128)} %refs_0_.7) | copy-start | bytes 52
  33.1 8.3 %collective-permute-start.1 = (bf16[128,3584]{1,0:T(8,128)(2,1)S(1)}, bf16[128,3584]{1,0:T(8,128)(2,1)S(1)}, u32[]{:S(2)}, u32[]{:S(2)}) collective-permute-start(bf16[128,3584]{1,0:T(8,128)(2,1)S(1)} %shard_map.86.refs_2_), channel_id=1, source_target_pairs={{0,1},{1,0},{2,3},{3,2},{4,5},{5,4},{6,7},{7,6},{8,9},{9,8},{10,11... | collective-permute-start | bytes 2752520 | tf_op jit(solution)/shard_map/ppermute | solution.py:358
  44.8 23.7 %collective-permute-start.4 = (bf16[2,128,3584]{2,1,0:T(8,128)(2,1)S(1)}, bf16[2,128,3584]{2,1,0:T(8,128)(2,1)S(1)}, u32[]{:S(2)}, u32[]{:S(2)}) collective-permute-start(bf16[2,128,3584]{2,1,0:T(8,128)(2,1)S(1)} %get-tuple-element.50), channel_id=1, source_target_pairs={{0,1},{1,0},{2,3},{3,2},{4,5},{5,4},{6,7},{7,6},{8,9},{9,8},{10,11... | collective-permute-start | bytes 5505032 | tf_op jit(solution)/shard_map/ppermute | solution.py:358
  46.7 24.1 %collective-permute-start.5 = (bf16[128,3584]{1,0:T(8,128)(2,1)S(1)}, bf16[128,3584]{1,0:T(8,128)(2,1)S(1)}, u32[]{:S(2)}, u32[]{:S(2)}) collective-permute-start(bf16[128,3584]{1,0:T(8,128)(2,1)S(1)} %get-tuple-element.51), channel_id=1, source_target_pairs={{0,766},{1,3},{2,0},{3,5},{4,2},{5,7},{6,4},{7,9},{8,6},{9,11},{10... | collective-permute-start | bytes 2752520 | tf_op jit(solution)/shard_map/ppermute | solution.py:358
  68.9 27.8 %collective-permute-start.6 = (bf16[128,3584]{1,0:T(8,128)(2,1)S(1)}, bf16[128,3584]{1,0:T(8,128)(2,1)}, u32[]{:S(2)}, u32[]{:S(2)}) collective-permute-start(bf16[128,3584]{1,0:T(8,128)(2,1)S(1)} %shard_map.91.refs_10_), channel_id=1, source_target_pairs={{0,2},{1,767},{2,4},{3,1},{4,6},{5,3},{6,8},{7,5},{8,10},{9,7},{10... | collective-permute-start | bytes 2752520 | tf_op jit(solution)/shard_map/ppermute | solution.py:358
  91.2 11.0 %all-to-all-start.2 = ((bf16[8,32,128]{2,1,0:T(8,128)(2,1)}), bf16[8,32,128]{2,1,0:T(8,128)(2,1)S(1)}, u32[]{:S(2)}, u32[]{:S(2)}) async-start(bf16[8,32,128]{2,1,0:T(8,128)(2,1)} %shard_map.94.refs_4_), calls=%async_computation.2 | async-start | bytes 131072 | tf_op jit(solution)/shard_map/all_to_all | solution.py:407
